TPU v7x, 768 devices: a whole 4x8x12 slice. The times are simulated.
768 devices in a mesh: dp: 24 (over z, core), ctx: 32 (over y, x).
Axes of the slice: x: 4, y: 8, z: 12, core: 2. Of those that a mesh axis runs over, the one named last changes fastest.
Arguments:
- queries: bfloat16 [122880, 2048], P(('dp', 'ctx')), may hold values from -10 to 10
- key_value: bfloat16 [12288, 2, 2048], P(('dp', 'ctx')), may hold values from -10 to 10
- out_grad: bfloat16 [122880, 2048], P(('dp', 'ctx')), may hold values from -6 to 6
- packing: int32 [12288], P(('dp', 'ctx')), may hold values from 0 to 383, as said below
- memory_docs: int32 [24, 512], P('dp'), may hold values from 0 to 15, never falling along the last dimension, each value on 1 to 170 neighbouring positions
- decoder_docs: int32 [24, 5120], P('dp', 'ctx'), may hold values from 0 to 15, never falling along the last dimension, each value on 1 to 1706 neighbouring positions
Outputs:
- attended: bfloat16 [122880, 2048], P(('dp', 'ctx'))
- query_grad: bfloat16 [122880, 2048], P(('dp', 'ctx'))
- key_value_grad: bfloat16 [12288, 2, 2048], P(('dp', 'ctx'))
Inputs may be any that keep to these rules, and one draw needn't show every extreme that they name: For each ctx index c, packing maps the 384 encoder tokens of ctx index c one to one onto 0 .. 383; packing // 16 is the token's group. No device sends more than 2 tokens to one group, and every device sends exactly 2 tokens to at least one group. `memory_docs`: within a group, document ids never fall along the memory rows, every id 0 .. 15 occurs, a document has at most 170 memory rows, and one has exactly that many. `decoder_docs`: within a group, document ids never fall along the decoder rows, every id 0 .. 15 occurs, a document has at most 1706 decoder rows, and one has exactly that many.
All inputs are finite; a program needn't handle non-finite values.
Results may differ from a plain program's by a relative error of at most 0.014.
The roundings to bfloat16 on the way count: a program that leaves them out, or rounds other values in their place, can miss the bound.
Values may be sent and summed in bfloat16 or wider, within the bound.
No kernel may reach another device: no remote copies, remote signals or barrier semaphores. Data moves between devices by JAX's collectives and lax.ppermute only.
A program may use at most 64 MiB of HBM per device.

v0:
```python
import math

import jax
import jax.numpy as jnp
from jax import lax
from jax.sharding import PartitionSpec as P

DH = 64


MASKED = -1e30


def split_heads(matrix, head_block):
    row_count, width_all = matrix.shape
    return matrix.reshape(row_count, width_all // (head_block * DH), head_block, DH).transpose(
        1, 0, 2, 3
    )


def join_heads(blocks):
    block_count, row_count, head_block, depth = blocks.shape
    return blocks.transpose(1, 0, 2, 3).reshape(row_count, block_count * head_block * depth)


def block_forward(query_block, key_block, value_block, grad_block, allowed, score_scale):
    scores = (
        jnp.einsum("qhd,khd->hqk", query_block, key_block, preferred_element_type=jnp.float32)
        * score_scale
    )
    scores = jnp.where(allowed[None], scores, MASKED)
    row_max = jnp.max(scores, axis=-1, keepdims=True)
    weights = jnp.where(allowed[None], jnp.exp(scores - row_max), 0.0)
    row_total = jnp.sum(weights, axis=-1, keepdims=True)
    normed = weights / row_total
    rounded = normed.astype(jnp.bfloat16)
    attended = jnp.einsum("hqk,khd->qhd", rounded, value_block, preferred_element_type=jnp.float32)
    grad_normed = jnp.einsum(
        "qhd,khd->hqk", grad_block, value_block, preferred_element_type=jnp.float32
    )
    row_delta = jnp.sum(normed * grad_normed, axis=-1, keepdims=True)
    grad_scores = (normed * (grad_normed - row_delta)).astype(jnp.bfloat16)
    query_grad = (
        jnp.einsum("hqk,khd->qhd", grad_scores, key_block, preferred_element_type=jnp.float32)
        * score_scale
    )
    return (attended, query_grad, rounded, grad_scores, row_max, row_total, row_delta)


def shards(queries, key_value, out_grad, packing, memory_docs, decoder_docs):
    group_count = lax.axis_size("dp")
    enc_rows = key_value.shape[0]
    head_width = key_value.shape[2]
    slot_cap = max(2, 2 * enc_rows // group_count)
    slot_count = group_count * slot_cap
    score_scale = 1.0 / math.sqrt(DH)
    target_group = packing // enc_rows
    token_index = jnp.arange(enc_rows, dtype=jnp.int32)
    earlier = (target_group[:, None] == target_group[None, :]) & (
        token_index[None, :] < token_index[:, None]
    )
    send_slot = target_group * slot_cap + jnp.sum(earlier, axis=1)
    placing = jnp.arange(slot_count, dtype=jnp.int32)[:, None] == send_slot[None, :]
    placing_half = placing.astype(jnp.bfloat16)
    flat_pairs = key_value.reshape(enc_rows, 2 * head_width)
    send_pairs = jnp.dot(placing_half, flat_pairs, preferred_element_type=jnp.float32).astype(
        jnp.bfloat16
    )
    send_label = jnp.sum(jnp.where(placing, (packing % enc_rows + 1)[None, :], 0), axis=1).astype(
        jnp.bfloat16
    )
    recv_pairs, recv_label = (
        lax.all_to_all(send_pairs, "dp", split_axis=0, concat_axis=0, tiled=True),
        lax.all_to_all(send_label, "dp", split_axis=0, concat_axis=0, tiled=True),
    )
    filling = recv_label.astype(jnp.int32)[:, None] - 1 == token_index[None, :]
    filling_half = filling.astype(jnp.bfloat16)
    memory = jnp.dot(filling_half.T, recv_pairs, preferred_element_type=jnp.float32).astype(
        jnp.bfloat16
    )
    group_pairs = lax.all_gather(memory, "ctx", axis=0, tiled=True)
    memory_row_docs = memory_docs[0]
    decoder_row_docs = decoder_docs[0]
    allowed = decoder_row_docs[:, None] == memory_row_docs[None, :]
    head_block = math.gcd(8, head_width // DH)
    query_parts = split_heads(queries, head_block)
    grad_parts = split_heads(out_grad, head_block)
    key_parts = split_heads(group_pairs[:, :head_width], head_block)
    value_parts = split_heads(group_pairs[:, head_width:], head_block)

    def per_heads(inputs):
        query_block, key_block, value_block, grad_block = inputs
        attended, query_grad, rounded, grad_scores, row_max, row_total, row_delta = block_forward(
            query_block, key_block, value_block, grad_block, allowed, score_scale
        )
        key_grad = (
            jnp.einsum("hqk,qhd->khd", grad_scores, query_block, preferred_element_type=jnp.float32)
            * score_scale
        )
        value_grad = jnp.einsum(
            "hqk,qhd->khd", rounded, grad_block, preferred_element_type=jnp.float32
        )
        return (attended, query_grad, key_grad, value_grad)

    attended, query_grad, key_grad, value_grad = lax.map(
        per_heads, (query_parts, key_parts, value_parts, grad_parts)
    )
    key_term = jnp.concatenate([join_heads(key_grad), join_heads(value_grad)], axis=1)
    memory_grad = lax.psum_scatter(
        key_term.astype(jnp.bfloat16), "ctx", scatter_dimension=0, tiled=True
    )
    back_pairs = jnp.dot(filling_half, memory_grad, preferred_element_type=jnp.float32).astype(
        jnp.bfloat16
    )
    returned = lax.all_to_all(back_pairs, "dp", split_axis=0, concat_axis=0, tiled=True)
    enc_grads = jnp.dot(placing_half.T, returned, preferred_element_type=jnp.float32).astype(
        jnp.bfloat16
    )
    return (
        join_heads(attended).astype(jnp.bfloat16),
        join_heads(query_grad).astype(jnp.bfloat16),
        enc_grads.reshape(enc_rows, 2, head_width),
    )


def solution(mesh):
    return jax.shard_map(
        shards,
        mesh=mesh,
        in_specs=(
            P(("dp", "ctx"), None),
            P(("dp", "ctx"), None, None),
            P(("dp", "ctx"), None),
            P(("dp", "ctx")),
            P("dp", None),
            P("dp", "ctx"),
        ),
        out_specs=(P(("dp", "ctx"), None), P(("dp", "ctx"), None), P(("dp", "ctx"), None, None)),
        check_vma=False,
    )
```

profile of v0, /device:TPU:1, one launch (start us, length us, event | category | flops | bytes accessed | tf_op | source)
XLA Modules:
  0.0 497.6 jit_solution(8345255560708762331)
XLA Ops:
  8.9 16.7 %all-to-all-start = ((bf16[24,2,1]{1,2,0:T(2,128)(2,1)}), bf16[24,2,1]{1,2,0:T(2,128)(2,1)S(1)}, u32[]{:S(2)}, u32[]{:S(2)}) async-start(bf16[24,2,1]{1,2,0:T(2,128)(2,1)} %convert_element_type.79), calls=%async_computation | async-start | bytes 24576 | tf_op jit(solution)/shard_map/all_to_all | solution.py:74
  28.0 7.0 %all-to-all-done = bf16[24,2,1]{1,2,0:T(2,128)(2,1)S(1)} async-done(((bf16[24,2,1]{1,2,0:T(2,128)(2,1)}), bf16[24,2,1]{1,2,0:T(2,128)(2,1)S(1)}, u32[]{:S(2)}, u32[]{:S(2)}) %all-to-all-start) | async-done | bytes 128 | tf_op jit(solution)/shard_map/all_to_all | solution.py:74
  35.0 4.2 all-to-all-start.1
  39.4 18.0 %all-to-all-done.1 = bf16[24,2,4096]{2,1,0:T(2,128)(2,1)S(1)} async-done(((bf16[24,2,4096]{2,1,0:T(2,128)(2,1)}), bf16[24,2,4096]{2,1,0:T(2,128)(2,1)S(1)}, u32[]{:S(2)}, u32[]{:S(2)}) %all-to-all-start.1) | async-done | bytes 393248 | tf_op jit(solution)/shard_map/all_to_all | solution.py:73
  61.2 84.2 %all-gather.2.cloned.1.call-done = bf16[512,4096]{1,0:T(8,128)(2,1)} async-done(((bf16[16,4096]{1,0:T(8,128)(2,1)}), bf16[512,4096]{1,0:T(8,128)(2,1)}) %all-gather.2.cloned.1.call-update) | async-done | bytes 4194320 | tf_op jit(solution)/shard_map/all_gather | solution.py:81
  145.4 4.0 fusion.66
  149.4 3.9 copy.29
  153.4 2.5 copy.31
  155.8 59.3 %while.17 = (s32[]{:T(128)}, bf16[4,160,8,64]{1,3,2,0:T(8,128)(2,1)}, bf16[4,160,8,64]{1,3,2,0:T(8,128)(2,1)}, bf16[4,512,8,64]{1,3,2,0:T(8,128)(2,1)}, bf16[4,5...) while((s32[]{:T(128)}, ...), condition=%wide.region_6.7_spmd.clone, body=%wide.region_2.6_spmd.clone.sunk | while | flops 514227456 | bytes 67664792 | solution.py:105
  155.9 2.5 fusion.98
  168.3 2.4 fusion.99
  170.8 2.5 fusion.98
  183.1 2.4 fusion.99
  185.6 2.5 fusion.98
  192.9 2.0 fusion.100
  197.9 2.4 fusion.99
  200.5 2.5 fusion.98
  212.8 2.4 fusion.99
  215.2 4.4 pad_maximum_fusion
  219.6 6.5 %copy.37 = bf16[512,4096]{1,0:T(8,128)(2,1)} copy(bf16[512,4096]{0,1:T(8,128)(2,1)} %pad_maximum_fusion) | data formatting | bytes 8388608
  226.1 228.2 %reduce-scatter.4.cloned.1.call-done = bf16[16,4096]{1,0:T(8,128)(2,1)} async-done(((bf16[512,4096]{1,0:T(8,128)(2,1)}), bf16[16,4096]{1,0:T(8,128)(2,1)}) %reduce-scatter.4.cloned.1.call-update) | async-done | bytes 131088
  456.5 14.9 %all-to-all-start.2 = ((bf16[24,2,4096]{2,1,0:T(2,128)(2,1)}), bf16[24,2,4096]{2,1,0:T(2,128)(2,1)S(1)}, u32[]{:S(2)}, u32[]{:S(2)}) async-start(bf16[24,2,4096]{2,1,0:T(2,128)(2,1)} %all_to_all.24), calls=%async_computation.2 | async-start | bytes 786432 | tf_op jit(solution)/shard_map/all_to_all | solution.py:115
  471.4 2.1 copy.35
  474.7 14.9 %all-to-all-done.2 = bf16[24,2,4096]{2,1,0:T(2,128)(2,1)S(1)} async-done(((bf16[24,2,4096]{2,1,0:T(2,128)(2,1)}), bf16[24,2,4096]{2,1,0:T(2,128)(2,1)S(1)}, u32[]{:S(2)}, u32[]{:S(2)}) %all-to-all-start.2) | async-done | bytes 393248 | tf_op jit(solution)/shard_map/all_to_all | solution.py:115
  (110 shorter events, 49.8 us)
Async XLA Ops:
  7.2 51.5 %copy-start.7 = (bf16[160,2048]{1,0:T(8,128)(2,1)S(1)}, bf16[160,2048]{1,0:T(8,128)(2,1)}, u32[]{:S(2)}) copy-start(bf16[160,2048]{1,0:T(8,128)(2,1)} %param.8) | copy-start | bytes 1966084
  8.9 26.0 %all-to-all-start = ((bf16[24,2,1]{1,2,0:T(2,128)(2,1)}), bf16[24,2,1]{1,2,0:T(2,128)(2,1)S(1)}, u32[]{:S(2)}, u32[]{:S(2)}) async-start(bf16[24,2,1]{1,2,0:T(2,128)(2,1)} %convert_element_type.79), calls=%async_computation | async-start | bytes 24576 | tf_op jit(solution)/shard_map/all_to_all | solution.py:74
  26.6 33.4 %copy-start.8 = (bf16[160,2048]{1,0:T(8,128)(2,1)S(1)}, bf16[160,2048]{1,0:T(8,128)(2,1)}, u32[]{:S(2)}) copy-start(bf16[160,2048]{1,0:T(8,128)(2,1)} %param.10) | copy-start | bytes 1966084
  35.0 22.4 %all-to-all-start.1 = ((bf16[24,2,4096]{2,1,0:T(2,128)(2,1)}), bf16[24,2,4096]{2,1,0:T(2,128)(2,1)S(1)}, u32[]{:S(2)}, u32[]{:S(2)}) async-start(bf16[24,2,4096]{2,1,0:T(2,128)(2,1)} %all_to_all.21), calls=%async_computation.1 | async-start | bytes 786432 | tf_op jit(solution)/shard_map/all_to_all | solution.py:73
  39.2 106.2 %all-gather.2.cloned.1.call-start = ((), (), s32[]{:S(2)}) async-start(), calls=%async_computation.4 | async-start | bytes 4325376 | tf_op jit(solution)/shard_map/all_gather | solution.py:81
  58.5 395.7 %reduce-scatter.4.cloned.1.call-start = ((), (), s32[]{:S(2)}) async-start(), calls=%async_computation.5 | async-start | bytes 4325376
  153.3 2.5 copy-start.9
  153.3 2.5 copy-start.10
  160.4 2.9 copy-start.4
  160.8 4.4 copy-start.2
  163.2 3.6 copy-start.1
  165.2 1.6 copy-start.5
  175.2 2.9 copy-start.4
  175.6 4.4 copy-start.2
  178.1 3.6 copy-start.1
  190.1 2.9 copy-start.4
  190.5 4.4 copy-start.2
  192.9 3.6 copy-start.1
  194.9 1.6 copy-start.5
  204.9 2.9 copy-start.4
  205.3 4.4 copy-start.2
  207.8 3.6 copy-start.1
  226.1 247.4 %copy-start.6 = (bf16[4,160,8,64]{1,3,2,0:T(8,128)(2,1)S(1)}, bf16[4,160,8,64]{1,3,2,0:T(8,128)(2,1)}, u32[]{:S(2)}) copy-start(bf16[4,160,8,64]{1,3,2,0:T(8,128)(2,1)} %get-tuple-element.59) | copy-start | bytes 1966084
  456.5 33.1 %all-to-all-start.2 = ((bf16[24,2,4096]{2,1,0:T(2,128)(2,1)}), bf16[24,2,4096]{2,1,0:T(2,128)(2,1)S(1)}, u32[]{:S(2)}, u32[]{:S(2)}) async-start(bf16[24,2,4096]{2,1,0:T(2,128)(2,1)} %all_to_all.24), calls=%async_computation.2 | async-start | bytes 786432 | tf_op jit(solution)/shard_map/all_to_all | solution.py:115
  (10 other events, 15.1 us)
Sparse Core Ops, SparseCore 0:
  58.7 86.6 all-gather.1
  226.2 228.0 reduce-scatter.3
where the time goes:
time: 500 us; the launch traced here: 498 us
  waiting for transfers between devices  352 us (70%)
  matrix products  49.5 us (10%)
  local copies, waits for them, and re-layouts  37.7 us (8%)
  starting transfers between devices  35.9 us (7%)
  between operations  14.2 us (3%)
  other arithmetic  7.62 us (2%)
    unnamed x3, waiting for transfers between devices  228 us
    all_gather x1, waiting for transfers between devices, shards(): group_pairs = lax.all_gather(memory, 'ctx', axis=0, tiled=True)  84.2 us
    all_to_all x1, waiting for transfers between devices, shards(): lax.all_to_all(send_pairs, 'dp', split_axis=0, concat_axis=0, tiled=True)  18 us
    all_to_all x1, starting transfers between devices, shards(): lax.all_to_all(send_label, 'dp', split_axis=0, concat_axis=0, tiled=True)  16.7 us
    all_to_all x1, waiting for transfers between devices, shards(): lax.all_to_all(back_pairs, 'dp', split_axis=0, concat_axis=0, tiled=True)  14.9 us
    all_to_all x1, starting transfers between devices, shards(): lax.all_to_all(back_pairs, 'dp', split_axis=0, concat_axis=0, tiled=True)  14.9 us
    while x48, local copies, waits for them, and re-layouts  10 us
    unnamed x14, local copies, waits for them, and re-layouts  10 us
  transfers between devices with their start and end apart: 5, of which 5 were waited for; matrix products, arithmetic and copies ran while one was open for 1% of the time, Pallas kernels for 0%

commit v1 on v0

v1 whole, which is shorter than its diff:
```python
import functools
import math

import jax
import jax.numpy as jnp
from jax import lax
from jax.experimental import pallas as pl
from jax.experimental.pallas import tpu as pltpu
from jax.sharding import PartitionSpec as P

DH = 64
LANES = 128
FAR = -1e30
BLOCK = 4
VMEM_BYTES = 48 * 1024 * 1024
ANY = pl.BlockSpec(memory_space=pl.ANY)
SMEM = pl.BlockSpec(memory_space=pltpu.SMEM)


def run_copies(copies):
    for copy in copies:
        copy.start()
    for copy in copies:
        copy.wait()


def pack_kernel(member_ref, queries_ref, grads_ref, docs_ref, *rest):
    pieces, sems = rest[:-1], rest[-1]
    half = queries_ref.shape[1] // len(pieces)
    copies = []
    for d, piece in enumerate(pieces):
        columns = pl.ds(pl.multiple_of((member_ref[0] ^ d) * half, half), half)
        copies += [
            pltpu.make_async_copy(
                queries_ref.at[:, columns], piece.at[:, pl.ds(0, half)], sems.at[d, 0]
            ),
            pltpu.make_async_copy(
                grads_ref.at[:, columns], piece.at[:, pl.ds(half, half)], sems.at[d, 1]
            ),
            pltpu.make_async_copy(docs_ref, piece.at[:, pl.ds(2 * half, LANES)], sems.at[d, 2]),
        ]
    run_copies(copies)


def pack(member, queries, grads, docs):
    rows, width = queries.shape
    piece = jax.ShapeDtypeStruct((rows, 2 * width // BLOCK + LANES), queries.dtype)
    return pl.pallas_call(
        pack_kernel,
        out_shape=[piece] * BLOCK,
        in_specs=[SMEM, ANY, ANY, ANY],
        out_specs=[ANY] * BLOCK,
        scratch_shapes=[pltpu.SemaphoreType.DMA((BLOCK, 3))],
        cost_estimate=pl.CostEstimate(
            flops=0, bytes_accessed=4 * 2 * rows * width, transcendentals=0
        ),
        name="pack",
    )(member, queries, grads, docs)


def unpack_kernel(member_ref, *rest):
    pieces, (attended_ref, query_grad_ref, sems) = rest[:-3], rest[-3:]
    half = attended_ref.shape[1] // len(pieces)
    copies = []
    for d, piece in enumerate(pieces):
        columns = pl.ds(pl.multiple_of((member_ref[0] ^ d) * half, half), half)
        for which, out_ref in enumerate((attended_ref, query_grad_ref)):
            copies.append(
                pltpu.make_async_copy(
                    piece.at[:, pl.ds(which * half, half)],
                    out_ref.at[:, columns],
                    sems.at[d, which],
                )
            )
    run_copies(copies)


def unpack(member, pieces, width):
    rows = pieces[0].shape[0]
    out = jax.ShapeDtypeStruct((rows, width), pieces[0].dtype)
    return pl.pallas_call(
        unpack_kernel,
        out_shape=[out, out],
        in_specs=[SMEM] + [ANY] * BLOCK,
        out_specs=[ANY, ANY],
        scratch_shapes=[pltpu.SemaphoreType.DMA((BLOCK, 2))],
        cost_estimate=pl.CostEstimate(
            flops=0, bytes_accessed=4 * 2 * rows * width, transcendentals=0
        ),
        name="unpack",
    )(member, *pieces)


def nt_dot(left, right):
    return lax.dot_general(
        left, right, (((1,), (1,)), ((), ())), preferred_element_type=jnp.float32
    )


def tn_dot(left, right):
    return lax.dot_general(
        left, right, (((0,), (0,)), ((), ())), preferred_element_type=jnp.float32
    )


def nn_dot(left, right):
    return jnp.dot(left, right, preferred_element_type=jnp.float32)


def attend_kernel(far_ref, kv_ref, *rest):
    pieces, rest = rest[:BLOCK], rest[BLOCK:]
    grad_ref, outs, rest = rest[0], rest[1 : 1 + BLOCK], rest[1 + BLOCK :]
    held, keys, values, rounded, grad_scores, result, sems = rest
    rows = pieces[0].shape[0]
    mem_rows, width = kv_ref.shape
    half = width // 2
    scale = 1.0 / math.sqrt(DH)
    loads = [
        pltpu.make_async_copy(piece, held.at[pl.ds(d * rows, rows)], sems.at[d])
        for d, piece in enumerate(pieces)
    ]
    run_copies(loads)
    low = lax.broadcasted_iota(jnp.int32, (mem_rows, LANES), 1) < DH
    zero = jnp.zeros((mem_rows, LANES), jnp.bfloat16)
    keys[pl.ds(0, mem_rows), pl.ds(LANES, LANES)] = far_ref[...]
    keys[pl.ds(mem_rows, mem_rows), pl.ds(LANES, LANES)] = far_ref[...]
    for pair in range(half // LANES):
        key_columns = pl.ds(pair * LANES, LANES)
        value_columns = pl.ds(half + pair * LANES, LANES)
        key_pair = kv_ref[:, key_columns] * jnp.bfloat16(scale)
        value_pair = kv_ref[:, value_columns]
        keys[pl.ds(0, mem_rows), pl.ds(0, LANES)] = jnp.where(low, key_pair, zero)
        keys[pl.ds(mem_rows, mem_rows), pl.ds(0, LANES)] = jnp.where(low, zero, key_pair)
        values[pl.ds(0, mem_rows)] = jnp.where(low, value_pair, zero)
        values[pl.ds(mem_rows, mem_rows)] = jnp.where(low, zero, value_pair)

        def step(index, carry):
            here = pl.ds(pl.multiple_of(index * rows, rows), rows)
            query = jnp.concatenate([held[here, key_columns], held[here, pl.ds(width, LANES)]], 1)
            scores = nt_dot(query, keys[...])
            grad_normed = nt_dot(held[here, value_columns], values[...])
            for head in range(2):
                mine = slice(head * mem_rows, (head + 1) * mem_rows)
                part = scores[:, mine]
                weights = jnp.exp(part - jnp.max(part, axis=1, keepdims=True))
                normed = weights * (1.0 / jnp.sum(weights, axis=1, keepdims=True))
                part_grad = grad_normed[:, mine]
                delta = jnp.sum(normed * part_grad, axis=1, keepdims=True)
                rounded[here, mine] = normed.astype(jnp.bfloat16)
                grad_scores[here, mine] = (normed * (part_grad - delta)).astype(jnp.bfloat16)
            result[here, key_columns] = nn_dot(rounded[here, :], values[...]).astype(jnp.bfloat16)
            result[here, value_columns] = nn_dot(
                grad_scores[here, :], keys[:, pl.ds(0, LANES)]
            ).astype(jnp.bfloat16)
            return carry

        lax.fori_loop(0, BLOCK, step, 0)
        key_grad = tn_dot(grad_scores[...], held[:, key_columns]) * scale
        value_grad = tn_dot(rounded[...], held[:, value_columns])
        grad_ref[:, key_columns] = jnp.where(
            low, key_grad[:mem_rows], key_grad[mem_rows:]
        ).astype(jnp.bfloat16)
        grad_ref[:, value_columns] = jnp.where(
            low, value_grad[:mem_rows], value_grad[mem_rows:]
        ).astype(jnp.bfloat16)
    run_copies(
        [
            pltpu.make_async_copy(result.at[pl.ds(d * rows, rows)], out, sems.at[d])
            for d, out in enumerate(outs)
        ]
    )


def attend(far, memory, pieces):
    rows = pieces[0].shape[0]
    mem_rows, width = memory.shape
    all_rows = BLOCK * rows
    half = jnp.bfloat16
    return pl.pallas_call(
        attend_kernel,
        out_shape=[jax.ShapeDtypeStruct((mem_rows, width), half)]
        + [jax.ShapeDtypeStruct((rows, width), half)] * BLOCK,
        in_specs=[pl.BlockSpec(memory_space=pltpu.VMEM)] * 2 + [ANY] * BLOCK,
        out_specs=[pl.BlockSpec(memory_space=pltpu.VMEM)] + [ANY] * BLOCK,
        scratch_shapes=[
            pltpu.VMEM((all_rows, width + LANES), half),
            pltpu.VMEM((2 * mem_rows, 2 * LANES), half),
            pltpu.VMEM((2 * mem_rows, LANES), half),
            pltpu.VMEM((all_rows, 2 * mem_rows), half),
            pltpu.VMEM((all_rows, 2 * mem_rows), half),
            pltpu.VMEM((all_rows, width), half),
            pltpu.SemaphoreType.DMA((BLOCK,)),
        ],
        compiler_params=pltpu.CompilerParams(vmem_limit_bytes=VMEM_BYTES),
        cost_estimate=pl.CostEstimate(
            flops=6 * 2 * all_rows * mem_rows * width // 2,
            bytes_accessed=8 * all_rows * width,
            transcendentals=all_rows * mem_rows * width // (2 * DH),
        ),
        name="attend",
    )(far, memory, *pieces)


def shards(queries, key_value, out_grad, packing, memory_docs, decoder_docs):
    group_count = lax.axis_size("dp")
    column_count = lax.axis_size("ctx")
    enc_rows, _, head_width = key_value.shape
    part_width = 2 * head_width // BLOCK
    slot_cap = 2
    slot_count = group_count * slot_cap
    half = jnp.bfloat16

    target_group = packing // enc_rows
    token_index = jnp.arange(enc_rows, dtype=jnp.int32)
    earlier = (target_group[:, None] == target_group[None, :]) & (
        token_index[None, :] < token_index[:, None]
    )
    send_slot = target_group * slot_cap + jnp.sum(earlier, axis=1)
    placing = jnp.arange(slot_count, dtype=jnp.int32)[:, None] == send_slot[None, :]
    placing_half = placing.astype(half)
    labels = jnp.broadcast_to(
        (packing % enc_rows + 1).astype(half)[:, None], (enc_rows, LANES)
    )
    flat_pairs = jnp.concatenate([key_value.reshape(enc_rows, 2 * head_width), labels], axis=1)
    send_pairs = jnp.dot(placing_half, flat_pairs, preferred_element_type=jnp.float32).astype(half)
    received = lax.all_to_all(send_pairs, "dp", split_axis=0, concat_axis=0, tiled=True)

    member = lax.axis_index("ctx") % BLOCK
    member_ref = member.reshape(1).astype(jnp.int32)
    doc_lanes = jnp.arange(LANES, dtype=jnp.int32)
    row_docs = (decoder_docs[0][:, None] == doc_lanes[None, :]).astype(half)
    far = jnp.where(memory_docs[0][:, None] == doc_lanes[None, :], 0.0, FAR).astype(half)
    pieces = pack(member_ref, queries, out_grad, row_docs)
    exchange = [
        [(c, c ^ d) for c in range(column_count)] for d in range(BLOCK)
    ]
    pieces = [pieces[0]] + [
        lax.ppermute(pieces[d], "ctx", exchange[d]) for d in range(1, BLOCK)
    ]

    recv_label = received[:, 2 * head_width].astype(jnp.int32)
    filling = recv_label[:, None] - 1 == token_index[None, :]
    filling_half = filling.astype(half)
    memory = jnp.dot(
        filling_half.T, received[:, : 2 * head_width], preferred_element_type=jnp.float32
    ).astype(half)
    by_member = memory.reshape(enc_rows, 2, BLOCK, part_width // 2).transpose(2, 0, 1, 3)
    by_member = by_member.reshape(1, BLOCK, enc_rows, part_width)
    by_column = jnp.broadcast_to(
        by_member, (column_count // BLOCK, BLOCK, enc_rows, part_width)
    ).reshape(column_count, enc_rows, part_width)
    group_part = lax.all_to_all(by_column, "ctx", split_axis=0, concat_axis=0, tiled=True)
    group_part = group_part.reshape(column_count * enc_rows, part_width)

    part_grad, *results = attend(far, group_part, pieces)

    part_grad = part_grad.reshape(column_count, enc_rows, part_width)
    partials = lax.all_to_all(part_grad, "ctx", split_axis=0, concat_axis=0, tiled=True)
    partials = partials.reshape(column_count // BLOCK, BLOCK, enc_rows, 2, part_width // 2)
    memory_grad = jnp.sum(partials.astype(jnp.float32), axis=0).astype(half)
    memory_grad = memory_grad.transpose(1, 2, 0, 3).reshape(enc_rows, 2 * head_width)
    back_pairs = jnp.dot(filling_half, memory_grad, preferred_element_type=jnp.float32).astype(half)
    returned = lax.all_to_all(back_pairs, "dp", split_axis=0, concat_axis=0, tiled=True)
    enc_grads = jnp.dot(placing_half.T, returned, preferred_element_type=jnp.float32).astype(half)

    results = [results[0]] + [
        lax.ppermute(results[d], "ctx", exchange[d]) for d in range(1, BLOCK)
    ]
    attended, query_grad = unpack(member_ref, results, head_width)
    return attended, query_grad, enc_grads.reshape(enc_rows, 2, head_width)


def solution(mesh):
    return jax.shard_map(
        shards,
        mesh=mesh,
        in_specs=(
            P(("dp", "ctx"), None),
            P(("dp", "ctx"), None, None),
            P(("dp", "ctx"), None),
            P(("dp", "ctx")),
            P("dp", None),
            P("dp", "ctx"),
        ),
        out_specs=(P(("dp", "ctx"), None), P(("dp", "ctx"), None), P(("dp", "ctx"), None, None)),
        check_vma=False,
    )
```

time: 500 us -> 260 us (0.52)
  waiting for transfers between devices: 352 us -> 33.3 us
  Pallas kernels: 0 us -> 105 us
  blocking collectives: 0 us -> 66.2 us
  matrix products: 49.5 us -> 1.1 us
  local copies, waits for them, and re-layouts: 37.7 us -> 8.65 us
  between operations: 14.2 us -> 0.9 us
  starting transfers between devices: 35.9 us -> 41 us
    unnamed x3 -> x0, waiting for transfers between devices: 228 us -> none
    pallas_call x0 -> x3, Pallas kernels: none -> 105 us  [the longest x1 45.9 us: pack(): pl.pallas_call(pack_kernel, out_shape=[piece] * BLOCK, in_specs=[SMEM, AN...]
    all_gather x1 -> x0, waiting for transfers between devices: 84.2 us -> none  [shards(): group_pairs = lax.all_gather(memory, 'ctx', axis=0, tiled=True)]
    all_to_all x0 -> x2, blocking collectives: none -> 66.2 us  [the longest x1 35.1 us: shards(): lax.all_to_all(send_pairs, 'dp', split_axis=0, concat_axis=0, tiled=True)]
    dot_general x21 -> x1, matrix products: 37.7 us -> 0.31 us  [shards(): jnp.dot(filling_half.T, received[:, :2 * head_width], preferred_element_t...]
    ppermute x0 -> x6, waiting for transfers between devices: none -> 33.3 us  [the longest x3 17.2 us: shards(): lax.ppermute(results[d], 'ctx', exchange[d])]
    all_to_all x2 -> x1, waiting for transfers between devices: 25 us -> 0.01 us  [shards(): lax.all_to_all(by_column, 'ctx', split_axis=0, concat_axis=0, tiled=True)]
    ppermute x0 -> x6, starting transfers between devices: none -> 19.2 us  [the longest x3 9.67 us: shards(): lax.ppermute(results[d], 'ctx', exchange[d])]
  transfers between devices with their start and end apart: 5 -> 8, of which waited for: 5 -> 5; matrix products, arithmetic and copies ran while one was open for 1% -> 0% of each run, Pallas kernels for 0% -> 33%
where the time goes in v1:
time: 260 us; the launch traced here: 259 us
  Pallas kernels  105 us (40%)
  blocking collectives  66.2 us (25%)
  starting transfers between devices  41 us (16%)
  waiting for transfers between devices  33.3 us (13%)
  local copies, waits for them, and re-layouts  8.65 us (3%)
  other arithmetic  3.03 us (1%)
    pallas_call x1, Pallas kernels, pack(): pl.pallas_call(pack_kernel, out_shape=[piece] * BLOCK, in_specs=[SMEM, AN...  45.9 us
    pallas_call x1, Pallas kernels, unpack(): pl.pallas_call(unpack_kernel, out_shape=[out, out], in_specs=[SMEM] + [AN...  40.9 us
    all_to_all x1, blocking collectives, shards(): lax.all_to_all(send_pairs, 'dp', split_axis=0, concat_axis=0, tiled=True)  35.1 us
    all_to_all x1, blocking collectives, shards(): lax.all_to_all(part_grad, 'ctx', split_axis=0, concat_axis=0, tiled=True)  31.2 us
    pallas_call x1, Pallas kernels, attend(): pl.pallas_call(attend_kernel, out_shape=[jax.ShapeDtypeStruct((mem_rows,...  18.3 us
    ppermute x3, waiting for transfers between devices, shards(): lax.ppermute(results[d], 'ctx', exchange[d])  17.2 us
    ppermute x3, waiting for transfers between devices, shards(): lax.ppermute(pieces[d], 'ctx', exchange[d])  16.1 us
    all_to_all x1, starting transfers between devices, shards(): lax.all_to_all(back_pairs, 'dp', split_axis=0, concat_axis=0, tiled=True)  12.1 us
  transfers between devices with their start and end apart: 8, of which 5 were waited for; matrix products, arithmetic and copies ran while one was open for 0% of the time, Pallas kernels for 33%

profile of v1, /device:TPU:1, one launch (start us, length us, event | category | flops | bytes accessed | tf_op | source)
XLA Modules:
  0.0 259.3 jit_solution(4517473541992566477)
XLA Ops:
  1.5 0.9 copy.16
  2.9 35.1 %all_to_all.34 = bf16[24,2,4224]{2,1,0:T(2,128)(2,1)S(1)} all-to-all(bf16[24,2,4224]{2,1,0:T(2,128)(2,1)S(1)} %all_to_all.22), channel_id=1, replica_groups=mesh['dp'=24,'ctx'=32] {'dp'}, dimensions={0} | all-to-all | bytes 811008 | tf_op jit(solution)/shard_map/all_to_all | solution.py:226
  38.9 1.1 broadcast_in_dim.18
  40.0 9.7 %all-to-all-start.1 = ((bf16[32,16,1024]{2,1,0:T(8,128)(2,1)}), bf16[32,16,1024]{2,1,0:T(8,128)(2,1)S(1)}, u32[]{:S(2)}, u32[]{:S(2)}) async-start(bf16[32,16,1024]{2,1,0:T(8,128)(2,1)} %bitcast.3), calls=%async_computation.1 | async-start | bytes 2097152 | tf_op jit(solution)/shard_map/all_to_all | solution.py:252
  51.1 45.9 %pack.1 = (bf16[160,1152]{1,0:T(8,128)(2,1)}, bf16[160,1152]{1,0:T(8,128)(2,1)}, bf16[160,1152]{1,0:T(8,128)(2,1)}, bf16[160,1152]{1,0:T(8,128)(2,1)}) custom-call(s32[1]{0:T(128)} %bitcast.member_ref, bf16[160,2048]{1,0:T(8,128)(2,1)} %queries_ref.1, bf16[160,2048]{1,0:T(8,128)(2,1)} %grads_ref.1, bf16[160,128]{1,0:T(8,128)(2,1)} %fusion.4.docs_ref), custom_call_target="tpu_custom_call" | custom-call | bytes 2621440 | tf_op jit(solution)/shard_map/pack/pallas_call | solution.py:48
  96.9 3.1 %collective-permute-start = (bf16[160,1152]{1,0:T(8,128)(2,1)}, bf16[160,1152]{1,0:T(8,128)(2,1)S(1)}, u32[]{:S(2)}, u32[]{:S(2)}) collective-permute-start(bf16[160,1152]{1,0:T(8,128)(2,1)} %get-tuple-element.15), channel_id=1, source_target_pairs={{0,1},{1,0},{2,3},{3,2},{4,5},{5,4},{6,7},{7,6},{8,9},{9,8},{10,11... | collective-permute-start | bytes 1105928 | tf_op jit(solution)/shard_map/ppermute | solution.py:238
  100.1 4.3 %collective-permute-start.1 = (bf16[160,1152]{1,0:T(8,128)(2,1)}, bf16[160,1152]{1,0:T(8,128)(2,1)S(1)}, u32[]{:S(2)}, u32[]{:S(2)}) collective-permute-start(bf16[160,1152]{1,0:T(8,128)(2,1)} %get-tuple-element.16), channel_id=1, source_target_pairs={{0,2},{1,3},{2,0},{3,1},{4,6},{5,7},{6,4},{7,5},{8,10},{9,11},{10,... | collective-permute-start | bytes 1105928 | tf_op jit(solution)/shard_map/ppermute | solution.py:238
  104.4 2.1 collective-permute-start.2
  106.7 9.2 %collective-permute-done.1.rest_2_ = bf16[160,1152]{1,0:T(8,128)(2,1)S(1)} collective-permute-done((bf16[160,1152]{1,0:T(8,128)(2,1)}, bf16[160,1152]{1,0:T(8,128)(2,1)S(1)}, u32[]{:S(2)}, u32[]{:S(2)}) %collective-permute-start.1) | collective-permute-done | bytes 368672 | tf_op jit(solution)/shard_map/ppermute | solution.py:238
  115.9 6.9 %collective-permute-done.2.rest_3_ = bf16[160,1152]{1,0:T(8,128)(2,1)S(1)} collective-permute-done((bf16[160,1152]{1,0:T(8,128)(2,1)}, bf16[160,1152]{1,0:T(8,128)(2,1)S(1)}, u32[]{:S(2)}, u32[]{:S(2)}) %collective-permute-start.2) | collective-permute-done | bytes 368672 | tf_op jit(solution)/shard_map/ppermute | solution.py:238
  122.8 1.0 copy-done.1
  123.8 18.3 %attend.1 = (bf16[512,1024]{1,0:T(8,128)(2,1)S(1)}, bf16[160,1024]{1,0:T(8,128)(2,1)S(1)}, bf16[160,1024]{1,0:T(8,128)(2,1)S(1)}, bf16[160,1024]{1,0:T(8,128)(2,1)S(1)}, bf16[160,1024]{1,0:T(8,128)(2,1)S(1)}) custom-call(bf16[512,128]{1,0:T(8,128)(2,1)S(1)} %select_convert_fusion.far_ref, bf16[512,1024]{1,0:T(8,128)(2,1)S(1)} %bitcast.14, ...), custom_call_target="tpu_custom_call" | custom-call | flops 2013265920 | bytes 5242880 | tf_op jit(solution)/shard_map/attend/pallas_call | solution.py:179
  142.8 31.2 %all_to_all.35 = bf16[32,16,1024]{2,1,0:T(8,128)(2,1)S(1)} all-to-all(bf16[32,16,1024]{2,1,0:T(8,128)(2,1)S(1)} %bitcast.15), channel_id=1, replica_groups=mesh['dp'=24,'ctx'=32] {'ctx'}, dimensions={0} | all-to-all | bytes 2097152 | tf_op jit(solution)/shard_map/all_to_all | solution.py:258
  174.0 0.8 reshape.52
  174.8 1.2 reduce_sum.22
  176.5 1.0 all_to_all.27
  177.5 12.1 %all-to-all-start.3 = ((bf16[24,2,4096]{2,1,0:T(2,128)(2,1)}), bf16[24,2,4096]{2,1,0:T(2,128)(2,1)S(1)}, u32[]{:S(2)}, u32[]{:S(2)}) async-start(bf16[24,2,4096]{2,1,0:T(2,128)(2,1)} %all_to_all.27), calls=%async_computation.3 | async-start | bytes 786432 | tf_op jit(solution)/shard_map/all_to_all | solution.py:263
  189.6 3.4 %collective-permute-start.3 = (bf16[160,1024]{1,0:T(8,128)(2,1)S(1)}, bf16[160,1024]{1,0:T(8,128)(2,1)S(1)}, u32[]{:S(2)}, u32[]{:S(2)}) collective-permute-start(bf16[160,1024]{1,0:T(8,128)(2,1)S(1)} %get-tuple-element.19), channel_id=1, source_target_pairs={{0,1},{1,0},{2,3},{3,2},{4,5},{5,4},{6,7},{7,6},{8,9},{9,8},{10,11... | collective-permute-start | bytes 983048 | tf_op jit(solution)/shard_map/ppermute | solution.py:267
  193.1 4.3 %collective-permute-start.4 = (bf16[160,1024]{1,0:T(8,128)(2,1)S(1)}, bf16[160,1024]{1,0:T(8,128)(2,1)S(1)}, u32[]{:S(2)}, u32[]{:S(2)}) collective-permute-start(bf16[160,1024]{1,0:T(8,128)(2,1)S(1)} %get-tuple-element.20), channel_id=1, source_target_pairs={{0,2},{1,3},{2,0},{3,1},{4,6},{5,7},{6,4},{7,5},{8,10},{9,11},{10,... | collective-permute-start | bytes 983048 | tf_op jit(solution)/shard_map/ppermute | solution.py:267
  197.4 1.9 collective-permute-start.5
  199.3 1.5 collective-permute-done.3.rest_1_
  200.9 9.4 %collective-permute-done.4.rest_2_ = bf16[160,1024]{1,0:T(8,128)(2,1)S(1)} collective-permute-done((bf16[160,1024]{1,0:T(8,128)(2,1)S(1)}, bf16[160,1024]{1,0:T(8,128)(2,1)S(1)}, u32[]{:S(2)}, u32[]{:S(2)}) %collective-permute-start.4) | collective-permute-done | bytes 327712 | tf_op jit(solution)/shard_map/ppermute | solution.py:267
  210.2 6.3 %collective-permute-done.5.rest_3_ = bf16[160,1024]{1,0:T(8,128)(2,1)S(1)} collective-permute-done((bf16[160,1024]{1,0:T(8,128)(2,1)S(1)}, bf16[160,1024]{1,0:T(8,128)(2,1)S(1)}, u32[]{:S(2)}, u32[]{:S(2)}) %collective-permute-start.5) | collective-permute-done | bytes 327712 | tf_op jit(solution)/shard_map/ppermute | solution.py:267
  217.3 40.9 %unpack.1 = (bf16[160,2048]{1,0:T(8,128)(2,1)}, bf16[160,2048]{1,0:T(8,128)(2,1)}) custom-call(s32[1]{0:T(128)} %bitcast.member_ref, bf16[160,1024]{1,0:T(8,128)(2,1)} %copy-done, bf16[160,1024]{1,0:T(8,128)(2,1)} %copy-done.2, bf16[160,1024]{1,0:T(8,128)(2,1)} %copy-done.3, bf16[160,1024]{1,0:T(8,128)(2,1)} %copy-done.4), custom_call_target="tpu_custom_call" | custom-call | bytes 2621440 | tf_op jit(solution)/shard_map/unpack/pallas_call | solution.py:81
  (36 shorter events, 6.7 us)
Async XLA Ops:
  40.0 82.8 %all-to-all-start.1 = ((bf16[32,16,1024]{2,1,0:T(8,128)(2,1)}), bf16[32,16,1024]{2,1,0:T(8,128)(2,1)S(1)}, u32[]{:S(2)}, u32[]{:S(2)}) async-start(bf16[32,16,1024]{2,1,0:T(8,128)(2,1)} %bitcast.3), calls=%async_computation.1 | async-start | bytes 2097152 | tf_op jit(solution)/shard_map/all_to_all | solution.py:252
  49.7 0.7 copy-start.6
  96.9 9.8 %collective-permute-start = (bf16[160,1152]{1,0:T(8,128)(2,1)}, bf16[160,1152]{1,0:T(8,128)(2,1)S(1)}, u32[]{:S(2)}, u32[]{:S(2)}) collective-permute-start(bf16[160,1152]{1,0:T(8,128)(2,1)} %get-tuple-element.15), channel_id=1, source_target_pairs={{0,1},{1,0},{2,3},{3,2},{4,5},{5,4},{6,7},{7,6},{8,9},{9,8},{10,11... | collective-permute-start | bytes 1105928 | tf_op jit(solution)/shard_map/ppermute | solution.py:238
  100.1 6.5 %copy-start.5 = (s32[1,512]{1,0:T(1,128)S(1)}, s32[1,512]{1,0:T(1,128)}, u32[]{:S(2)}) copy-start(s32[1,512]{1,0:T(1,128)} %param.10) | copy-start | bytes 6148
  100.1 15.8 %collective-permute-start.1 = (bf16[160,1152]{1,0:T(8,128)(2,1)}, bf16[160,1152]{1,0:T(8,128)(2,1)S(1)}, u32[]{:S(2)}, u32[]{:S(2)}) collective-permute-start(bf16[160,1152]{1,0:T(8,128)(2,1)} %get-tuple-element.16), channel_id=1, source_target_pairs={{0,2},{1,3},{2,0},{3,1},{4,6},{5,7},{6,4},{7,5},{8,10},{9,11},{10,... | collective-permute-start | bytes 1105928 | tf_op jit(solution)/shard_map/ppermute | solution.py:238
  104.4 18.4 %collective-permute-start.2 = (bf16[160,1152]{1,0:T(8,128)(2,1)}, bf16[160,1152]{1,0:T(8,128)(2,1)S(1)}, u32[]{:S(2)}, u32[]{:S(2)}) collective-permute-start(bf16[160,1152]{1,0:T(8,128)(2,1)} %get-tuple-element.17), channel_id=1, source_target_pairs={{0,3},{1,2},{2,1},{3,0},{4,7},{5,6},{6,5},{7,4},{8,11},{9,10},{10,... | collective-permute-start | bytes 1105928 | tf_op jit(solution)/shard_map/ppermute | solution.py:238
  122.8 1.0 copy-start.1
  142.1 0.7 copy-start
  177.5 80.6 %all-to-all-start.3 = ((bf16[24,2,4096]{2,1,0:T(2,128)(2,1)}), bf16[24,2,4096]{2,1,0:T(2,128)(2,1)S(1)}, u32[]{:S(2)}, u32[]{:S(2)}) async-start(bf16[24,2,4096]{2,1,0:T(2,128)(2,1)} %all_to_all.27), calls=%async_computation.3 | async-start | bytes 786432 | tf_op jit(solution)/shard_map/all_to_all | solution.py:263
  189.6 11.2 %collective-permute-start.3 = (bf16[160,1024]{1,0:T(8,128)(2,1)S(1)}, bf16[160,1024]{1,0:T(8,128)(2,1)S(1)}, u32[]{:S(2)}, u32[]{:S(2)}) collective-permute-start(bf16[160,1024]{1,0:T(8,128)(2,1)S(1)} %get-tuple-element.19), channel_id=1, source_target_pairs={{0,1},{1,0},{2,3},{3,2},{4,5},{5,4},{6,7},{7,6},{8,9},{9,8},{10,11... | collective-permute-start | bytes 983048 | tf_op jit(solution)/shard_map/ppermute | solution.py:267
  193.1 17.1 %collective-permute-start.4 = (bf16[160,1024]{1,0:T(8,128)(2,1)S(1)}, bf16[160,1024]{1,0:T(8,128)(2,1)S(1)}, u32[]{:S(2)}, u32[]{:S(2)}) collective-permute-start(bf16[160,1024]{1,0:T(8,128)(2,1)S(1)} %get-tuple-element.20), channel_id=1, source_target_pairs={{0,2},{1,3},{2,0},{3,1},{4,6},{5,7},{6,4},{7,5},{8,10},{9,11},{10,... | collective-permute-start | bytes 983048 | tf_op jit(solution)/shard_map/ppermute | solution.py:267
  197.4 19.1 %collective-permute-start.5 = (bf16[160,1024]{1,0:T(8,128)(2,1)S(1)}, bf16[160,1024]{1,0:T(8,128)(2,1)S(1)}, u32[]{:S(2)}, u32[]{:S(2)}) collective-permute-start(bf16[160,1024]{1,0:T(8,128)(2,1)S(1)} %get-tuple-element.21), channel_id=1, source_target_pairs={{0,3},{1,2},{2,1},{3,0},{4,7},{5,6},{6,5},{7,4},{8,11},{9,10},{10,... | collective-permute-start | bytes 983048 | tf_op jit(solution)/shard_map/ppermute | solution.py:267
  200.8 15.7 %copy-start.2 = (bf16[160,1024]{1,0:T(8,128)(2,1)}, bf16[160,1024]{1,0:T(8,128)(2,1)S(1)}, u32[]{:S(2)}) copy-start(bf16[160,1024]{1,0:T(8,128)(2,1)S(1)} %collective-permute-done.3.rest_1_) | copy-start | bytes 983044
  210.2 6.3 %copy-start.3 = (bf16[160,1024]{1,0:T(8,128)(2,1)}, bf16[160,1024]{1,0:T(8,128)(2,1)S(1)}, u32[]{:S(2)}) copy-start(bf16[160,1024]{1,0:T(8,128)(2,1)S(1)} %collective-permute-done.4.rest_2_) | copy-start | bytes 983044
  216.6 0.7 copy-start.4

commit v2 on v1

v2 whole, which is shorter than its diff:
```python
import math

import jax
import jax.numpy as jnp
from jax import lax
from jax.experimental import pallas as pl
from jax.experimental.pallas import tpu as pltpu
from jax.sharding import PartitionSpec as P

DH = 64
LANES = 128
FAR = -1e30
BLOCK = 8
CHUNK = 256
SPANS = (128, 256, 512)
VMEM_BYTES = 48 * 1024 * 1024
COPY_BYTES = 16 * 1024 * 1024
EARLY = 4
RETURNED = 4
VMEM = pl.BlockSpec(memory_space=pltpu.VMEM)
ANY = pl.BlockSpec(memory_space=pl.ANY)
SMEM = pl.BlockSpec(memory_space=pltpu.SMEM)


def run_copies(copies):
    for copy in copies:
        copy.start()
    for copy in copies:
        copy.wait()


def pack_kernel(member_ref, queries_ref, grads_ref, docs_ref, *pieces):
    half = queries_ref.shape[1] // len(pieces)
    for d, piece in enumerate(pieces):
        columns = pl.ds(pl.multiple_of((member_ref[0] ^ d) * half, half), half)
        piece[:, pl.ds(0, half)] = queries_ref[:, columns]
        piece[:, pl.ds(half, half)] = grads_ref[:, columns]
        piece[:, pl.ds(2 * half, LANES)] = docs_ref[...]


def pack(member, queries, grads, docs):
    rows, width = queries.shape
    piece = jax.ShapeDtypeStruct((rows, 2 * width // BLOCK + LANES), queries.dtype)
    return pl.pallas_call(
        pack_kernel,
        out_shape=[piece] * BLOCK,
        in_specs=[SMEM, VMEM, VMEM, VMEM],
        out_specs=[VMEM] * BLOCK,
        compiler_params=pltpu.CompilerParams(vmem_limit_bytes=COPY_BYTES),
        cost_estimate=pl.CostEstimate(
            flops=0, bytes_accessed=4 * 2 * rows * width, transcendentals=0
        ),
        name="pack",
    )(member, queries, grads, docs)


def unpack_kernel(member_ref, *rest):
    pieces, (attended_ref, query_grad_ref) = rest[:-2], rest[-2:]
    half = attended_ref.shape[1] // len(pieces)
    for d, piece in enumerate(pieces):
        columns = pl.ds(pl.multiple_of((member_ref[0] ^ d) * half, half), half)
        attended_ref[:, columns] = piece[:, pl.ds(0, half)]
        query_grad_ref[:, columns] = piece[:, pl.ds(half, half)]


def unpack(member, pieces, width):
    rows = pieces[0].shape[0]
    out = jax.ShapeDtypeStruct((rows, width), pieces[0].dtype)
    return pl.pallas_call(
        unpack_kernel,
        out_shape=[out, out],
        in_specs=[SMEM] + [VMEM] * BLOCK,
        out_specs=[VMEM, VMEM],
        compiler_params=pltpu.CompilerParams(vmem_limit_bytes=COPY_BYTES),
        cost_estimate=pl.CostEstimate(
            flops=0, bytes_accessed=4 * 2 * rows * width, transcendentals=0
        ),
        name="unpack",
    )(member, *pieces)


def nt_dot(left, right):
    return lax.dot_general(
        left, right, (((1,), (1,)), ((), ())), preferred_element_type=jnp.float32
    )


def tn_dot(left, right):
    return lax.dot_general(
        left, right, (((0,), (0,)), ((), ())), preferred_element_type=jnp.float32
    )


def nn_dot(left, right):
    return jnp.dot(left, right, preferred_element_type=jnp.float32)


def attend_kernel(member_ref, far_ref, spans_ref, kv_ref, *rest):
    pieces, rest = rest[:BLOCK], rest[BLOCK:]
    grad_ref, outs, rest = rest[0], rest[1 : 1 + BLOCK], rest[1 + BLOCK :]
    held, keys, key_aug, values, key_acc, value_acc, result, window, sems = rest
    rows = pieces[0].shape[0]
    mem_rows, width = kv_ref.shape
    half = width // 2
    pairs = half // LANES
    chunks = BLOCK * rows // CHUNK
    scale = 1.0 / math.sqrt(DH)

    def place(d):
        return pl.ds(pl.multiple_of((member_ref[0] ^ d) * rows, rows), rows)

    loads = [
        pltpu.make_async_copy(piece, held.at[place(d)], sems.at[d])
        for d, piece in enumerate(pieces)
    ]
    for load in loads:
        load.start()
    for load in loads:
        load.wait()
    for chunk in range(chunks):
        docs = held[pl.ds(chunk * CHUNK, CHUNK), pl.ds(width, LANES)].astype(jnp.float32)
        present = jnp.max(docs, axis=0, keepdims=True) > 0.0
        window[chunk, 0] = jnp.min(jnp.where(present, spans_ref[0:1], float(mem_rows))).astype(
            jnp.int32
        )
        window[chunk, 1] = jnp.max(jnp.where(present, spans_ref[1:2], 0.0)).astype(jnp.int32)
    low = lax.broadcasted_iota(jnp.int32, (mem_rows, LANES), 1) < DH
    zero = jnp.zeros((mem_rows, LANES), jnp.bfloat16)
    for pair in range(pairs):
        key_pair = kv_ref[:, pl.ds(pair * LANES, LANES)] * jnp.bfloat16(scale)
        value_pair = kv_ref[:, pl.ds(half + pair * LANES, LANES)]
        keys[pair] = key_pair
        for head in range(2):
            mine = low if head == 0 else ~low
            key_aug[pair, head, :, pl.ds(0, LANES)] = jnp.where(mine, key_pair, zero)
            key_aug[pair, head, :, pl.ds(LANES, LANES)] = far_ref[...]
            values[pair, head] = jnp.where(mine, value_pair, zero)
    key_acc[...] = jnp.zeros_like(key_acc)
    value_acc[...] = jnp.zeros_like(value_acc)

    def on_window(here, start, span):
        mine = pl.ds(start, span)
        docs = held[here, pl.ds(width, LANES)]
        half_lanes = lax.broadcasted_iota(jnp.int32, (span, LANES), 1) < DH
        key_columns = [pl.ds(pair * LANES, LANES) for pair in range(pairs)]
        value_columns = [pl.ds(half + pair * LANES, LANES) for pair in range(pairs)]
        query = [held[here, columns] for columns in key_columns]
        grad = [held[here, columns] for columns in value_columns]
        scores = [
            nt_dot(
                key_aug[pair, :, mine, :].reshape(2 * span, 2 * LANES),
                jnp.concatenate([query[pair], docs], axis=1),
            ).reshape(2, span, CHUNK)
            for pair in range(pairs)
        ]
        grad_normed = [
            nt_dot(values[pair, :, mine, :].reshape(2 * span, LANES), grad[pair]).reshape(
                2, span, CHUNK
            )
            for pair in range(pairs)
        ]
        rounded, grad_scores = [], []
        for pair in range(pairs):
            top = jnp.max(scores[pair], axis=1, keepdims=True)
            weights = jnp.exp(scores[pair] - top)
            normed = weights * (1.0 / jnp.sum(weights, axis=1, keepdims=True))
            delta = jnp.sum(normed * grad_normed[pair], axis=1, keepdims=True)
            rounded.append(normed.astype(jnp.bfloat16))
            grad_scores.append((normed * (grad_normed[pair] - delta)).astype(jnp.bfloat16))
        for pair in range(pairs):
            key_grad = nn_dot(grad_scores[pair].reshape(2 * span, CHUNK), query[pair])
            value_grad = nn_dot(rounded[pair].reshape(2 * span, CHUNK), grad[pair])
            key_acc[pair, mine, :] += jnp.where(half_lanes, key_grad[:span], key_grad[span:])
            value_acc[pair, mine, :] += jnp.where(half_lanes, value_grad[:span], value_grad[span:])
            key_turned = keys[pair, mine, :].T
            value_turned = kv_ref[mine, value_columns[pair]].T
            for columns, turned, terms in (
                (key_columns[pair], value_turned, rounded[pair]),
                (value_columns[pair], key_turned, grad_scores[pair]),
            ):
                both = [
                    nn_dot(turned[head * DH : (head + 1) * DH], terms[head]) for head in range(2)
                ]
                result[here, columns] = jnp.concatenate(both, axis=0).astype(jnp.bfloat16).T

    def step(chunk, carry):
        here = pl.ds(pl.multiple_of(chunk * CHUNK, CHUNK), CHUNK)
        first, last = window[chunk, 0], window[chunk, 1]
        taken = jnp.bool_(False)
        for span in SPANS:
            start = jnp.minimum((first // 16) * 16, mem_rows - span)
            fits = last <= start + span

            @pl.when(fits & ~taken)
            def _(start=start, span=span):
                on_window(here, pl.multiple_of(start, 16), span)

            taken = taken | fits
        return carry

    lax.fori_loop(0, chunks, step, 0)
    for pair in range(pairs):
        grad_ref[:, pl.ds(pair * LANES, LANES)] = (key_acc[pair] * scale).astype(jnp.bfloat16)
        grad_ref[:, pl.ds(half + pair * LANES, LANES)] = value_acc[pair].astype(jnp.bfloat16)
    run_copies(
        [
            pltpu.make_async_copy(result.at[place(d)], out, sems.at[d])
            for d, out in enumerate(outs)
        ]
    )


def attend(member, far, spans, memory, pieces):
    rows = pieces[0].shape[0]
    mem_rows, width = memory.shape
    all_rows = BLOCK * rows
    heads = width // (2 * DH)
    half = jnp.bfloat16
    return pl.pallas_call(
        attend_kernel,
        out_shape=[jax.ShapeDtypeStruct((mem_rows, width), half)]
        + [jax.ShapeDtypeStruct((rows, width), half)] * BLOCK,
        in_specs=[SMEM] + [VMEM] * 3 + [ANY] * BLOCK,
        out_specs=[VMEM] + [ANY] * BLOCK,
        scratch_shapes=[
            pltpu.VMEM((all_rows, width + LANES), half),
            pltpu.VMEM((heads // 2, mem_rows, LANES), half),
            pltpu.VMEM((heads // 2, 2, mem_rows, 2 * LANES), half),
            pltpu.VMEM((heads // 2, 2, mem_rows, LANES), half),
            pltpu.VMEM((heads // 2, mem_rows, LANES), jnp.float32),
            pltpu.VMEM((heads // 2, mem_rows, LANES), jnp.float32),
            pltpu.VMEM((all_rows, width), half),
            pltpu.SMEM((8, 2), jnp.int32),
            pltpu.SemaphoreType.DMA((BLOCK,)),
        ],
        compiler_params=pltpu.CompilerParams(vmem_limit_bytes=VMEM_BYTES),
        cost_estimate=pl.CostEstimate(
            flops=6 * 2 * all_rows * mem_rows * width // 2,
            bytes_accessed=8 * all_rows * width,
            transcendentals=all_rows * mem_rows * width // (2 * DH),
        ),
        name="attend",
    )(member, far, spans, memory, *pieces)


def shards(queries, key_value, out_grad, packing, memory_docs, decoder_docs):
    group_count = lax.axis_size("dp")
    column_count = lax.axis_size("ctx")
    enc_rows, _, head_width = key_value.shape
    part_width = 2 * head_width // BLOCK
    slot_cap = 2
    slot_count = group_count * slot_cap
    half = jnp.bfloat16

    target_group = packing // enc_rows
    token_index = jnp.arange(enc_rows, dtype=jnp.int32)
    earlier = (target_group[:, None] == target_group[None, :]) & (
        token_index[None, :] < token_index[:, None]
    )
    send_slot = target_group * slot_cap + jnp.sum(earlier, axis=1)
    placing = jnp.arange(slot_count, dtype=jnp.int32)[:, None] == send_slot[None, :]
    placing_half = placing.astype(half)
    labels = jnp.broadcast_to(
        (packing % enc_rows + 1).astype(half)[:, None], (enc_rows, LANES)
    )
    flat_pairs = jnp.concatenate([key_value.reshape(enc_rows, 2 * head_width), labels], axis=1)
    send_pairs = jnp.dot(placing_half, flat_pairs, preferred_element_type=jnp.float32).astype(half)
    received = lax.all_to_all(send_pairs, "dp", split_axis=0, concat_axis=0, tiled=True)

    member = lax.axis_index("ctx") % BLOCK
    member_ref = member.reshape(1).astype(jnp.int32)
    doc_lanes = jnp.arange(LANES, dtype=jnp.int32)
    row_docs = (decoder_docs[0][:, None] == doc_lanes[None, :]).astype(half)
    far = jnp.where(memory_docs[0][:, None] == doc_lanes[None, :], 0.0, FAR).astype(half)
    starts = jnp.sum(memory_docs[0][:, None] < doc_lanes[None, :], axis=0)
    ends = jnp.sum(memory_docs[0][:, None] <= doc_lanes[None, :], axis=0)
    spans = jnp.stack([starts, ends] + [starts] * 6).astype(jnp.float32)
    pieces = pack(member_ref, queries, out_grad, row_docs)
    exchange = [
        [(c, c ^ d) for c in range(column_count)] for d in range(BLOCK)
    ]
    pieces = [pieces[0]] + [
        lax.ppermute(pieces[d], "ctx", exchange[d]) for d in range(1, BLOCK)
    ]

    recv_label = received[:, 2 * head_width].astype(jnp.int32)
    filling = recv_label[:, None] - 1 == token_index[None, :]
    filling_half = filling.astype(half)
    memory = jnp.dot(
        filling_half.T, received[:, : 2 * head_width], preferred_element_type=jnp.float32
    ).astype(half)
    by_member = memory.reshape(enc_rows, 2, BLOCK, part_width // 2).transpose(2, 0, 1, 3)
    by_member = by_member.reshape(1, BLOCK, enc_rows, part_width)
    by_column = jnp.broadcast_to(
        by_member, (column_count // BLOCK, BLOCK, enc_rows, part_width)
    ).reshape(column_count, enc_rows, part_width)
    by_column, pieces[1 : 1 + EARLY] = lax.optimization_barrier(
        (by_column, pieces[1 : 1 + EARLY])
    )
    group_part = lax.all_to_all(by_column, "ctx", split_axis=0, concat_axis=0, tiled=True)
    group_part = group_part.reshape(column_count * enc_rows, part_width)

    part_grad, *results = attend(member_ref, far, spans, group_part, pieces)

    results = [results[0]] + [
        lax.ppermute(results[d], "ctx", exchange[d]) for d in range(1, BLOCK)
    ]
    part_grad = part_grad.reshape(column_count, enc_rows, part_width)
    partials = lax.all_to_all(part_grad, "ctx", split_axis=0, concat_axis=0, tiled=True)
    partials, results[1 : 1 + RETURNED] = lax.optimization_barrier(
        (partials, results[1 : 1 + RETURNED])
    )
    partials = partials.reshape(column_count // BLOCK, BLOCK, enc_rows, 2, part_width // 2)
    memory_grad = jnp.sum(partials.astype(jnp.float32), axis=0).astype(half)
    memory_grad = memory_grad.transpose(1, 2, 0, 3).reshape(enc_rows, 2 * head_width)
    back_pairs = jnp.dot(filling_half, memory_grad, preferred_element_type=jnp.float32).astype(half)
    returned = lax.all_to_all(back_pairs, "dp", split_axis=0, concat_axis=0, tiled=True)
    enc_grads = jnp.dot(placing_half.T, returned, preferred_element_type=jnp.float32).astype(half)

    attended, query_grad = unpack(member_ref, results, head_width)
    return attended, query_grad, enc_grads.reshape(enc_rows, 2, head_width)


def solution(mesh):
    return jax.shard_map(
        shards,
        mesh=mesh,
        in_specs=(
            P(("dp", "ctx"), None),
            P(("dp", "ctx"), None, None),
            P(("dp", "ctx"), None),
            P(("dp", "ctx")),
            P("dp", None),
            P("dp", "ctx"),
        ),
        out_specs=(P(("dp", "ctx"), None), P(("dp", "ctx"), None), P(("dp", "ctx"), None, None)),
        check_vma=False,
    )
```

time: 260 us -> 150 us (0.58)
  Pallas kernels: 105 us -> 11.6 us
  blocking collectives: 66.2 us -> 0 us
  starting transfers between devices: 41 us -> 90.4 us
    pallas_call x2, Pallas kernels: 86.8 us -> 1.41 us  [the longest x1 1.22 us: unpack(): pl.pallas_call(unpack_kernel, out_shape=[out, out], in_specs=[SMEM] + [VM...]
    all_to_all x2 -> x0, blocking collectives: 66.2 us -> none  [the longest x1 35.1 us: shards(): lax.all_to_all(send_pairs, 'dp', split_axis=0, concat_axis=0, tiled=True)]
    all_to_all x0 -> x2, starting transfers between devices: none -> 23 us  [the longest x1 16.7 us: shards(): lax.all_to_all(send_pairs, 'dp', split_axis=0, concat_axis=0, tiled=True)]
    ppermute x3 -> x7, starting transfers between devices: 9.58 us -> 24.2 us  [shards(): lax.ppermute(pieces[d], 'ctx', exchange[d])]
    ppermute x3 -> x7, starting transfers between devices: 9.67 us -> 23.9 us  [shards(): lax.ppermute(results[d], 'ctx', exchange[d])]
    pallas_call x1, Pallas kernels: 18.3 us -> 10.2 us  [attend(): pl.pallas_call(attend_kernel, out_shape=[jax.ShapeDtypeStruct((mem_rows,...]
    all_to_all x0 -> x2, waiting for transfers between devices: none -> 4.85 us  [the longest x1 4.85 us: shards(): lax.all_to_all(send_pairs, 'dp', split_axis=0, concat_axis=0, tiled=True)]
    ppermute x3 -> x7, waiting for transfers between devices: 17.2 us -> 12.8 us  [shards(): lax.ppermute(results[d], 'ctx', exchange[d])]
  transfers between devices with their start and end apart: 8 -> 18, of which waited for: 5 -> 10; matrix products, arithmetic and copies ran while one was open for 0% -> 1% of each run, Pallas kernels for 33% -> 1%
where the time goes in v2:
time: 150 us; the launch traced here: 148 us
  starting transfers between devices  90.4 us (60%)
  waiting for transfers between devices  34 us (23%)
  Pallas kernels  11.6 us (8%)
  local copies, waits for them, and re-layouts  8.34 us (6%)
  other arithmetic  2.04 us (1%)
    ppermute x7, starting transfers between devices, shards(): lax.ppermute(pieces[d], 'ctx', exchange[d])  24.2 us
    ppermute x7, starting transfers between devices, shards(): lax.ppermute(results[d], 'ctx', exchange[d])  23.9 us
    all_to_all x1, starting transfers between devices, shards(): lax.all_to_all(send_pairs, 'dp', split_axis=0, concat_axis=0, tiled=True)  16.7 us
    ppermute x7, waiting for transfers between devices, shards(): lax.ppermute(pieces[d], 'ctx', exchange[d])  16 us
    ppermute x7, waiting for transfers between devices, shards(): lax.ppermute(results[d], 'ctx', exchange[d])  12.8 us
    pallas_call x1, Pallas kernels, attend(): pl.pallas_call(attend_kernel, out_shape=[jax.ShapeDtypeStruct((mem_rows,...  10.2 us
    all_to_all x1, starting transfers between devices, shards(): lax.all_to_all(back_pairs, 'dp', split_axis=0, concat_axis=0, tiled=True)  10 us
    all_to_all x1, starting transfers between devices, shards(): lax.all_to_all(by_column, 'ctx', split_axis=0, concat_axis=0, tiled=True)  9.23 us
  transfers between devices with their start and end apart: 18, of which 10 were waited for; matrix products, arithmetic and copies ran while one was open for 1% of the time, Pallas kernels for 1%

profile of v2, /device:TPU:1, one launch (start us, length us, event | category | flops | bytes accessed | tf_op | source)
XLA Modules:
  0.0 148.5 jit_solution(12427553429598926980)
XLA Ops:
  3.7 16.7 %all-to-all-start = ((bf16[24,2,4224]{2,1,0:T(2,128)(2,1)}), bf16[24,2,4224]{2,1,0:T(2,128)(2,1)}, u32[]{:S(2)}, u32[]{:S(2)}) async-start(bf16[24,2,4224]{2,1,0:T(2,128)(2,1)} %all_to_all.22), calls=%async_computation | async-start | bytes 811008 | tf_op jit(solution)/shard_map/all_to_all | solution.py:268
  21.4 3.1 %collective-permute-start = (bf16[160,640]{1,0:T(8,128)(2,1)S(1)}, bf16[160,640]{1,0:T(8,128)(2,1)S(1)}, u32[]{:S(2)}, u32[]{:S(2)}) collective-permute-start(bf16[160,640]{1,0:T(8,128)(2,1)S(1)} %get-tuple-element.32), channel_id=1, source_target_pairs={{0,1},{1,0},{2,3},{3,2},{4,5},{5,4},{6,7},{7,6},{8,9},{9,8},{10,11... | collective-permute-start | bytes 614408 | tf_op jit(solution)/shard_map/ppermute | solution.py:283
  24.5 4.4 %collective-permute-start.1 = (bf16[160,640]{1,0:T(8,128)(2,1)S(1)}, bf16[160,640]{1,0:T(8,128)(2,1)S(1)}, u32[]{:S(2)}, u32[]{:S(2)}) collective-permute-start(bf16[160,640]{1,0:T(8,128)(2,1)S(1)} %get-tuple-element.33), channel_id=1, source_target_pairs={{0,2},{1,3},{2,0},{3,1},{4,6},{5,7},{6,4},{7,5},{8,10},{9,11},{10,... | collective-permute-start | bytes 614408 | tf_op jit(solution)/shard_map/ppermute | solution.py:283
  31.0 3.2 %collective-permute-start.3 = (bf16[160,640]{1,0:T(8,128)(2,1)S(1)}, bf16[160,640]{1,0:T(8,128)(2,1)S(1)}, u32[]{:S(2)}, u32[]{:S(2)}) collective-permute-start(bf16[160,640]{1,0:T(8,128)(2,1)S(1)} %get-tuple-element.35), channel_id=1, source_target_pairs={{0,4},{1,5},{2,6},{3,7},{4,0},{5,1},{6,2},{7,3},{8,12},{9,13},{10,... | collective-permute-start | bytes 614408 | tf_op jit(solution)/shard_map/ppermute | solution.py:283
  34.2 4.9 %all-to-all-done = bf16[24,2,4224]{2,1,0:T(2,128)(2,1)} async-done(((bf16[24,2,4224]{2,1,0:T(2,128)(2,1)}), bf16[24,2,4224]{2,1,0:T(2,128)(2,1)}, u32[]{:S(2)}, u32[]{:S(2)}) %all-to-all-start) | async-done | bytes 405536 | tf_op jit(solution)/shard_map/all_to_all | solution.py:268
  42.3 9.2 %all-to-all-start.1 = ((bf16[32,16,512]{2,1,0:T(8,128)(2,1)}), bf16[32,16,512]{2,1,0:T(8,128)(2,1)S(1)}, u32[]{:S(2)}, u32[]{:S(2)}) async-start(bf16[32,16,512]{2,1,0:T(8,128)(2,1)} %bitcast.5), calls=%async_computation.1 | async-start | bytes 1048576 | tf_op jit(solution)/shard_map/all_to_all | solution.py:300
  51.5 4.0 %collective-permute-start.4 = (bf16[160,640]{1,0:T(8,128)(2,1)S(1)}, bf16[160,640]{1,0:T(8,128)(2,1)S(1)}, u32[]{:S(2)}, u32[]{:S(2)}) collective-permute-start(bf16[160,640]{1,0:T(8,128)(2,1)S(1)} %get-tuple-element.42), channel_id=1, source_target_pairs={{0,5},{1,4},{2,7},{3,6},{4,1},{5,0},{6,3},{7,2},{8,13},{9,12},{10,... | collective-permute-start | bytes 614408 | tf_op jit(solution)/shard_map/ppermute | solution.py:283
  55.6 4.3 %collective-permute-start.5 = (bf16[160,640]{1,0:T(8,128)(2,1)S(1)}, bf16[160,640]{1,0:T(8,128)(2,1)S(1)}, u32[]{:S(2)}, u32[]{:S(2)}) collective-permute-start(bf16[160,640]{1,0:T(8,128)(2,1)S(1)} %get-tuple-element.43), channel_id=1, source_target_pairs={{0,6},{1,7},{2,4},{3,5},{4,2},{5,3},{6,0},{7,1},{8,14},{9,15},{10,... | collective-permute-start | bytes 614408 | tf_op jit(solution)/shard_map/ppermute | solution.py:283
  59.9 3.1 %collective-permute-start.6 = (bf16[160,640]{1,0:T(8,128)(2,1)S(1)}, bf16[160,640]{1,0:T(8,128)(2,1)S(1)}, u32[]{:S(2)}, u32[]{:S(2)}) collective-permute-start(bf16[160,640]{1,0:T(8,128)(2,1)S(1)} %get-tuple-element.44), channel_id=1, source_target_pairs={{0,7},{1,6},{2,5},{3,4},{4,3},{5,2},{6,1},{7,0},{8,15},{9,14},{10,... | collective-permute-start | bytes 614408 | tf_op jit(solution)/shard_map/ppermute | solution.py:283
  63.3 4.8 %collective-permute-done.4.rest_5_ = bf16[160,640]{1,0:T(8,128)(2,1)S(1)} collective-permute-done((bf16[160,640]{1,0:T(8,128)(2,1)S(1)}, bf16[160,640]{1,0:T(8,128)(2,1)S(1)}, u32[]{:S(2)}, u32[]{:S(2)}) %collective-permute-start.4) | collective-permute-done | bytes 204832 | tf_op jit(solution)/shard_map/ppermute | solution.py:283
  68.1 6.4 %collective-permute-done.5.rest_6_ = bf16[160,640]{1,0:T(8,128)(2,1)S(1)} collective-permute-done((bf16[160,640]{1,0:T(8,128)(2,1)S(1)}, bf16[160,640]{1,0:T(8,128)(2,1)S(1)}, u32[]{:S(2)}, u32[]{:S(2)}) %collective-permute-start.5) | collective-permute-done | bytes 204832 | tf_op jit(solution)/shard_map/ppermute | solution.py:283
  74.5 4.3 %collective-permute-done.6.rest_7_ = bf16[160,640]{1,0:T(8,128)(2,1)S(1)} collective-permute-done((bf16[160,640]{1,0:T(8,128)(2,1)S(1)}, bf16[160,640]{1,0:T(8,128)(2,1)S(1)}, u32[]{:S(2)}, u32[]{:S(2)}) %collective-permute-start.6) | collective-permute-done | bytes 204832 | tf_op jit(solution)/shard_map/ppermute | solution.py:283
  78.8 10.2 %attend.1 = (bf16[512,512]{1,0:T(8,128)(2,1)}, bf16[160,512]{1,0:T(8,128)(2,1)S(1)}, bf16[160,512]{1,0:T(8,128)(2,1)S(1)}, bf16[160,512]{1,0:T(8,128)(2,1)S(1)},...) custom-call(s32[1]{0:T(128)} %bitcast.member_ref, ...), custom_call_target="tpu_custom_call" | custom-call | flops 2013265920 | bytes 5242880 | tf_op jit(solution)/shard_map/attend/pallas_call | solution.py:219
  90.4 6.3 %all-to-all-start.2 = ((bf16[32,16,512]{2,1,0:T(8,128)(2,1)}), bf16[32,16,512]{2,1,0:T(8,128)(2,1)S(1)}, u32[]{:S(2)}, u32[]{:S(2)}) async-start(bf16[32,16,512]{2,1,0:T(8,128)(2,1)} %bitcast.8), calls=%async_computation.2 | async-start | bytes 1048576 | tf_op jit(solution)/shard_map/all_to_all | solution.py:309
  96.7 3.1 %collective-permute-start.7 = (bf16[160,512]{1,0:T(8,128)(2,1)S(1)}, bf16[160,512]{1,0:T(8,128)(2,1)S(1)}, u32[]{:S(2)}, u32[]{:S(2)}) collective-permute-start(bf16[160,512]{1,0:T(8,128)(2,1)S(1)} %copy-done.5), channel_id=1, source_target_pairs={{0,1},{1,0},{2,3},{3,2},{4,5},{5,4},{6,7},{7,6},{8,9},{9,8},{10,11... | collective-permute-start | bytes 491528 | tf_op jit(solution)/shard_map/ppermute | solution.py:306
  99.8 4.3 %collective-permute-start.8 = (bf16[160,512]{1,0:T(8,128)(2,1)S(1)}, bf16[160,512]{1,0:T(8,128)(2,1)S(1)}, u32[]{:S(2)}, u32[]{:S(2)}) collective-permute-start(bf16[160,512]{1,0:T(8,128)(2,1)S(1)} %copy-done.3), channel_id=1, source_target_pairs={{0,2},{1,3},{2,0},{3,1},{4,6},{5,7},{6,4},{7,5},{8,10},{9,11},{10,... | collective-permute-start | bytes 491528 | tf_op jit(solution)/shard_map/ppermute | solution.py:306
  106.3 3.1 %collective-permute-start.10 = (bf16[160,512]{1,0:T(8,128)(2,1)S(1)}, bf16[160,512]{1,0:T(8,128)(2,1)S(1)}, u32[]{:S(2)}, u32[]{:S(2)}) collective-permute-start(bf16[160,512]{1,0:T(8,128)(2,1)S(1)} %get-tuple-element.50), channel_id=1, source_target_pairs={{0,4},{1,5},{2,6},{3,7},{4,0},{5,1},{6,2},{7,3},{8,12},{9,13},{10,... | collective-permute-start | bytes 491528 | tf_op jit(solution)/shard_map/ppermute | solution.py:306
  109.4 4.2 %collective-permute-done.8.rest_2_ = bf16[160,512]{1,0:T(8,128)(2,1)S(1)} collective-permute-done((bf16[160,512]{1,0:T(8,128)(2,1)S(1)}, bf16[160,512]{1,0:T(8,128)(2,1)S(1)}, u32[]{:S(2)}, u32[]{:S(2)}) %collective-permute-start.8) | collective-permute-done | bytes 163872 | tf_op jit(solution)/shard_map/ppermute | solution.py:306
  113.6 3.2 %collective-permute-done.9.rest_3_ = bf16[160,512]{1,0:T(8,128)(2,1)S(1)} collective-permute-done((bf16[160,512]{1,0:T(8,128)(2,1)S(1)}, bf16[160,512]{1,0:T(8,128)(2,1)S(1)}, u32[]{:S(2)}, u32[]{:S(2)}) %collective-permute-start.9) | collective-permute-done | bytes 163872 | tf_op jit(solution)/shard_map/ppermute | solution.py:306
  119.1 10.0 %all-to-all-start.3 = ((bf16[24,2,4096]{2,1,0:T(2,128)(2,1)}), bf16[24,2,4096]{2,1,0:T(2,128)(2,1)S(1)}, u32[]{:S(2)}, u32[]{:S(2)}) async-start(bf16[24,2,4096]{2,1,0:T(2,128)(2,1)} %all_to_all.27), calls=%async_computation.3 | async-start | bytes 786432 | tf_op jit(solution)/shard_map/all_to_all | solution.py:317
  129.1 2.4 %collective-permute-start.11 = (bf16[160,512]{1,0:T(8,128)(2,1)S(1)}, bf16[160,512]{1,0:T(8,128)(2,1)S(1)}, u32[]{:S(2)}, u32[]{:S(2)}) collective-permute-start(bf16[160,512]{1,0:T(8,128)(2,1)S(1)} %get-tuple-element.55), channel_id=1, source_target_pairs={{0,5},{1,4},{2,7},{3,6},{4,1},{5,0},{6,3},{7,2},{8,13},{9,12},{10,... | collective-permute-start | bytes 491528 | tf_op jit(solution)/shard_map/ppermute | solution.py:306
  131.5 3.8 %collective-permute-start.12 = (bf16[160,512]{1,0:T(8,128)(2,1)S(1)}, bf16[160,512]{1,0:T(8,128)(2,1)S(1)}, u32[]{:S(2)}, u32[]{:S(2)}) collective-permute-start(bf16[160,512]{1,0:T(8,128)(2,1)S(1)} %get-tuple-element.56), channel_id=1, source_target_pairs={{0,6},{1,7},{2,4},{3,5},{4,2},{5,3},{6,0},{7,1},{8,14},{9,15},{10,... | collective-permute-start | bytes 491528 | tf_op jit(solution)/shard_map/ppermute | solution.py:306
  135.4 5.0 %collective-permute-start.13 = (bf16[160,512]{1,0:T(8,128)(2,1)S(1)}, bf16[160,512]{1,0:T(8,128)(2,1)S(1)}, u32[]{:S(2)}, u32[]{:S(2)}) collective-permute-start(bf16[160,512]{1,0:T(8,128)(2,1)S(1)} %get-tuple-element.57), channel_id=1, source_target_pairs={{0,7},{1,6},{2,5},{3,4},{4,3},{5,2},{6,1},{7,0},{8,15},{9,14},{10,... | collective-permute-start | bytes 491528 | tf_op jit(solution)/shard_map/ppermute | solution.py:306
  141.1 4.6 %collective-permute-done.13.rest_7_ = bf16[160,512]{1,0:T(8,128)(2,1)S(1)} collective-permute-done((bf16[160,512]{1,0:T(8,128)(2,1)S(1)}, bf16[160,512]{1,0:T(8,128)(2,1)S(1)}, u32[]{:S(2)}, u32[]{:S(2)}) %collective-permute-start.13) | collective-permute-done | bytes 163872 | tf_op jit(solution)/shard_map/ppermute | solution.py:306
  (59 shorter events, 18.7 us)
Async XLA Ops:
  2.8 18.4 %copy-start = (bf16[160,2048]{1,0:T(8,128)(2,1)S(1)}, bf16[160,2048]{1,0:T(8,128)(2,1)}, u32[]{:S(2)}) copy-start(bf16[160,2048]{1,0:T(8,128)(2,1)} %queries_ref.1) | copy-start | bytes 1966084
  2.8 18.4 %copy-start.1 = (bf16[160,2048]{1,0:T(8,128)(2,1)S(1)}, bf16[160,2048]{1,0:T(8,128)(2,1)}, u32[]{:S(2)}) copy-start(bf16[160,2048]{1,0:T(8,128)(2,1)} %grads_ref.1) | copy-start | bytes 1966084
  3.7 35.4 %all-to-all-start = ((bf16[24,2,4224]{2,1,0:T(2,128)(2,1)}), bf16[24,2,4224]{2,1,0:T(2,128)(2,1)}, u32[]{:S(2)}, u32[]{:S(2)}) async-start(bf16[24,2,4224]{2,1,0:T(2,128)(2,1)} %all_to_all.22), calls=%async_computation | async-start | bytes 811008 | tf_op jit(solution)/shard_map/all_to_all | solution.py:268
  20.4 0.7 copy-start.7
  21.4 19.5 %collective-permute-start = (bf16[160,640]{1,0:T(8,128)(2,1)S(1)}, bf16[160,640]{1,0:T(8,128)(2,1)S(1)}, u32[]{:S(2)}, u32[]{:S(2)}) collective-permute-start(bf16[160,640]{1,0:T(8,128)(2,1)S(1)} %get-tuple-element.32), channel_id=1, source_target_pairs={{0,1},{1,0},{2,3},{3,2},{4,5},{5,4},{6,7},{7,6},{8,9},{9,8},{10,11... | collective-permute-start | bytes 614408 | tf_op jit(solution)/shard_map/ppermute | solution.py:283
  24.5 16.4 %collective-permute-start.1 = (bf16[160,640]{1,0:T(8,128)(2,1)S(1)}, bf16[160,640]{1,0:T(8,128)(2,1)S(1)}, u32[]{:S(2)}, u32[]{:S(2)}) collective-permute-start(bf16[160,640]{1,0:T(8,128)(2,1)S(1)} %get-tuple-element.33), channel_id=1, source_target_pairs={{0,2},{1,3},{2,0},{3,1},{4,6},{5,7},{6,4},{7,5},{8,10},{9,11},{10,... | collective-permute-start | bytes 614408 | tf_op jit(solution)/shard_map/ppermute | solution.py:283
  28.9 12.5 %collective-permute-start.2 = (bf16[160,640]{1,0:T(8,128)(2,1)S(1)}, bf16[160,640]{1,0:T(8,128)(2,1)S(1)}, u32[]{:S(2)}, u32[]{:S(2)}) collective-permute-start(bf16[160,640]{1,0:T(8,128)(2,1)S(1)} %get-tuple-element.34), channel_id=1, source_target_pairs={{0,3},{1,2},{2,1},{3,0},{4,7},{5,6},{6,5},{7,4},{8,11},{9,10},{10,... | collective-permute-start | bytes 614408 | tf_op jit(solution)/shard_map/ppermute | solution.py:283
  31.0 10.4 %collective-permute-start.3 = (bf16[160,640]{1,0:T(8,128)(2,1)S(1)}, bf16[160,640]{1,0:T(8,128)(2,1)S(1)}, u32[]{:S(2)}, u32[]{:S(2)}) collective-permute-start(bf16[160,640]{1,0:T(8,128)(2,1)S(1)} %get-tuple-element.35), channel_id=1, source_target_pairs={{0,4},{1,5},{2,6},{3,7},{4,0},{5,1},{6,2},{7,3},{8,12},{9,13},{10,... | collective-permute-start | bytes 614408 | tf_op jit(solution)/shard_map/ppermute | solution.py:283
  42.3 36.6 %all-to-all-start.1 = ((bf16[32,16,512]{2,1,0:T(8,128)(2,1)}), bf16[32,16,512]{2,1,0:T(8,128)(2,1)S(1)}, u32[]{:S(2)}, u32[]{:S(2)}) async-start(bf16[32,16,512]{2,1,0:T(8,128)(2,1)} %bitcast.5), calls=%async_computation.1 | async-start | bytes 1048576 | tf_op jit(solution)/shard_map/all_to_all | solution.py:300
  51.5 16.7 %collective-permute-start.4 = (bf16[160,640]{1,0:T(8,128)(2,1)S(1)}, bf16[160,640]{1,0:T(8,128)(2,1)S(1)}, u32[]{:S(2)}, u32[]{:S(2)}) collective-permute-start(bf16[160,640]{1,0:T(8,128)(2,1)S(1)} %get-tuple-element.42), channel_id=1, source_target_pairs={{0,5},{1,4},{2,7},{3,6},{4,1},{5,0},{6,3},{7,2},{8,13},{9,12},{10,... | collective-permute-start | bytes 614408 | tf_op jit(solution)/shard_map/ppermute | solution.py:283
  55.5 7.4 %copy-start.6 = (s32[1,512]{1,0:T(1,128)S(1)}, s32[1,512]{1,0:T(1,128)}, u32[]{:S(2)}) copy-start(s32[1,512]{1,0:T(1,128)} %param.10) | copy-start | bytes 6148
  55.6 19.0 %collective-permute-start.5 = (bf16[160,640]{1,0:T(8,128)(2,1)S(1)}, bf16[160,640]{1,0:T(8,128)(2,1)S(1)}, u32[]{:S(2)}, u32[]{:S(2)}) collective-permute-start(bf16[160,640]{1,0:T(8,128)(2,1)S(1)} %get-tuple-element.43), channel_id=1, source_target_pairs={{0,6},{1,7},{2,4},{3,5},{4,2},{5,3},{6,0},{7,1},{8,14},{9,15},{10,... | collective-permute-start | bytes 614408 | tf_op jit(solution)/shard_map/ppermute | solution.py:283
  59.9 19.0 %collective-permute-start.6 = (bf16[160,640]{1,0:T(8,128)(2,1)S(1)}, bf16[160,640]{1,0:T(8,128)(2,1)S(1)}, u32[]{:S(2)}, u32[]{:S(2)}) collective-permute-start(bf16[160,640]{1,0:T(8,128)(2,1)S(1)} %get-tuple-element.44), channel_id=1, source_target_pairs={{0,7},{1,6},{2,5},{3,4},{4,3},{5,2},{6,1},{7,0},{8,15},{9,14},{10,... | collective-permute-start | bytes 614408 | tf_op jit(solution)/shard_map/ppermute | solution.py:283
  90.4 6.3 %copy-start.5 = (bf16[160,512]{1,0:T(8,128)(2,1)S(1)}, bf16[160,512]{1,0:T(8,128)(2,1)}, u32[]{:S(2)}) copy-start(bf16[160,512]{1,0:T(8,128)(2,1)} %copy-done.4) | copy-start | bytes 491524
  90.4 9.4 %copy-start.3 = (bf16[160,512]{1,0:T(8,128)(2,1)S(1)}, bf16[160,512]{1,0:T(8,128)(2,1)}, u32[]{:S(2)}) copy-start(bf16[160,512]{1,0:T(8,128)(2,1)} %copy-done.2) | copy-start | bytes 491524
  90.4 26.5 %all-to-all-start.2 = ((bf16[32,16,512]{2,1,0:T(8,128)(2,1)}), bf16[32,16,512]{2,1,0:T(8,128)(2,1)S(1)}, u32[]{:S(2)}, u32[]{:S(2)}) async-start(bf16[32,16,512]{2,1,0:T(8,128)(2,1)} %bitcast.8), calls=%async_computation.2 | async-start | bytes 1048576 | tf_op jit(solution)/shard_map/all_to_all | solution.py:309
  96.7 12.8 %collective-permute-start.7 = (bf16[160,512]{1,0:T(8,128)(2,1)S(1)}, bf16[160,512]{1,0:T(8,128)(2,1)S(1)}, u32[]{:S(2)}, u32[]{:S(2)}) collective-permute-start(bf16[160,512]{1,0:T(8,128)(2,1)S(1)} %copy-done.5), channel_id=1, source_target_pairs={{0,1},{1,0},{2,3},{3,2},{4,5},{5,4},{6,7},{7,6},{8,9},{9,8},{10,11... | collective-permute-start | bytes 491528 | tf_op jit(solution)/shard_map/ppermute | solution.py:306
  99.8 13.8 %collective-permute-start.8 = (bf16[160,512]{1,0:T(8,128)(2,1)S(1)}, bf16[160,512]{1,0:T(8,128)(2,1)S(1)}, u32[]{:S(2)}, u32[]{:S(2)}) collective-permute-start(bf16[160,512]{1,0:T(8,128)(2,1)S(1)} %copy-done.3), channel_id=1, source_target_pairs={{0,2},{1,3},{2,0},{3,1},{4,6},{5,7},{6,4},{7,5},{8,10},{9,11},{10,... | collective-permute-start | bytes 491528 | tf_op jit(solution)/shard_map/ppermute | solution.py:306
  104.1 12.7 %collective-permute-start.9 = (bf16[160,512]{1,0:T(8,128)(2,1)S(1)}, bf16[160,512]{1,0:T(8,128)(2,1)S(1)}, u32[]{:S(2)}, u32[]{:S(2)}) collective-permute-start(bf16[160,512]{1,0:T(8,128)(2,1)S(1)} %get-tuple-element.49), channel_id=1, source_target_pairs={{0,3},{1,2},{2,1},{3,0},{4,7},{5,6},{6,5},{7,4},{8,11},{9,10},{10,... | collective-permute-start | bytes 491528 | tf_op jit(solution)/shard_map/ppermute | solution.py:306
  106.3 10.6 %collective-permute-start.10 = (bf16[160,512]{1,0:T(8,128)(2,1)S(1)}, bf16[160,512]{1,0:T(8,128)(2,1)S(1)}, u32[]{:S(2)}, u32[]{:S(2)}) collective-permute-start(bf16[160,512]{1,0:T(8,128)(2,1)S(1)} %get-tuple-element.50), channel_id=1, source_target_pairs={{0,4},{1,5},{2,6},{3,7},{4,0},{5,1},{6,2},{7,3},{8,12},{9,13},{10,... | collective-permute-start | bytes 491528 | tf_op jit(solution)/shard_map/ppermute | solution.py:306
  119.1 28.2 %all-to-all-start.3 = ((bf16[24,2,4096]{2,1,0:T(2,128)(2,1)}), bf16[24,2,4096]{2,1,0:T(2,128)(2,1)S(1)}, u32[]{:S(2)}, u32[]{:S(2)}) async-start(bf16[24,2,4096]{2,1,0:T(2,128)(2,1)} %all_to_all.27), calls=%async_computation.3 | async-start | bytes 786432 | tf_op jit(solution)/shard_map/all_to_all | solution.py:317
  129.1 11.2 %collective-permute-start.11 = (bf16[160,512]{1,0:T(8,128)(2,1)S(1)}, bf16[160,512]{1,0:T(8,128)(2,1)S(1)}, u32[]{:S(2)}, u32[]{:S(2)}) collective-permute-start(bf16[160,512]{1,0:T(8,128)(2,1)S(1)} %get-tuple-element.55), channel_id=1, source_target_pairs={{0,5},{1,4},{2,7},{3,6},{4,1},{5,0},{6,3},{7,2},{8,13},{9,12},{10,... | collective-permute-start | bytes 491528 | tf_op jit(solution)/shard_map/ppermute | solution.py:306
  131.5 9.6 %collective-permute-start.12 = (bf16[160,512]{1,0:T(8,128)(2,1)S(1)}, bf16[160,512]{1,0:T(8,128)(2,1)S(1)}, u32[]{:S(2)}, u32[]{:S(2)}) collective-permute-start(bf16[160,512]{1,0:T(8,128)(2,1)S(1)} %get-tuple-element.56), channel_id=1, source_target_pairs={{0,6},{1,7},{2,4},{3,5},{4,2},{5,3},{6,0},{7,1},{8,14},{9,15},{10,... | collective-permute-start | bytes 491528 | tf_op jit(solution)/shard_map/ppermute | solution.py:306
  135.4 10.4 %collective-permute-start.13 = (bf16[160,512]{1,0:T(8,128)(2,1)S(1)}, bf16[160,512]{1,0:T(8,128)(2,1)S(1)}, u32[]{:S(2)}, u32[]{:S(2)}) collective-permute-start(bf16[160,512]{1,0:T(8,128)(2,1)S(1)} %get-tuple-element.57), channel_id=1, source_target_pairs={{0,7},{1,6},{2,5},{3,4},{4,3},{5,2},{6,1},{7,0},{8,15},{9,14},{10,... | collective-permute-start | bytes 491528 | tf_op jit(solution)/shard_map/ppermute | solution.py:306
  (2 other events, 1.3 us)

commit v3 on v2

--- a/solution.py
+++ b/solution.py
@@ -9,14 +9,15 @@
 
 DH = 64
 LANES = 128
+TILE = 16
 FAR = -1e30
 BLOCK = 8
 CHUNK = 256
-SPANS = (128, 256, 512)
+SPANS = (64, 128, 256, 384, 512)
 VMEM_BYTES = 48 * 1024 * 1024
 COPY_BYTES = 16 * 1024 * 1024
-EARLY = 4
-RETURNED = 4
+EARLY, LATE = (2, 6, 5, 4), (7, 3, 1)
+RETURNED, LAST = (2, 1, 3), (6, 7, 5, 4)
 VMEM = pl.BlockSpec(memory_space=pltpu.VMEM)
 ANY = pl.BlockSpec(memory_space=pl.ANY)
 SMEM = pl.BlockSpec(memory_space=pltpu.SMEM)
@@ -29,18 +30,19 @@
         copy.wait()
 
 
-def pack_kernel(member_ref, queries_ref, grads_ref, docs_ref, *pieces):
+def pack_kernel(member_ref, queries_ref, grads_ref, bounds_ref, *pieces):
     half = queries_ref.shape[1] // len(pieces)
+    rows = queries_ref.shape[0]
     for d, piece in enumerate(pieces):
         columns = pl.ds(pl.multiple_of((member_ref[0] ^ d) * half, half), half)
-        piece[:, pl.ds(0, half)] = queries_ref[:, columns]
-        piece[:, pl.ds(half, half)] = grads_ref[:, columns]
-        piece[:, pl.ds(2 * half, LANES)] = docs_ref[...]
-
-
-def pack(member, queries, grads, docs):
+        piece[pl.ds(0, rows), pl.ds(0, half)] = queries_ref[:, columns]
+        piece[pl.ds(0, rows), pl.ds(half, half)] = grads_ref[:, columns]
+        piece[pl.ds(rows, TILE), :] = bounds_ref[...]
+
+
+def pack(member, queries, grads, bounds):
     rows, width = queries.shape
-    piece = jax.ShapeDtypeStruct((rows, 2 * width // BLOCK + LANES), queries.dtype)
+    piece = jax.ShapeDtypeStruct((rows + TILE, 2 * width // BLOCK), queries.dtype)
     return pl.pallas_call(
         pack_kernel,
         out_shape=[piece] * BLOCK,
@@ -51,7 +53,7 @@
             flops=0, bytes_accessed=4 * 2 * rows * width, transcendentals=0
         ),
         name="pack",
-    )(member, queries, grads, docs)
+    )(member, queries, grads, bounds)
 
 
 def unpack_kernel(member_ref, *rest):
@@ -98,8 +100,8 @@
 def attend_kernel(member_ref, far_ref, spans_ref, kv_ref, *rest):
     pieces, rest = rest[:BLOCK], rest[BLOCK:]
     grad_ref, outs, rest = rest[0], rest[1 : 1 + BLOCK], rest[1 + BLOCK :]
-    held, keys, key_aug, values, key_acc, value_acc, result, window, sems = rest
-    rows = pieces[0].shape[0]
+    held, edges, spread, docs, keys, key_aug, values, key_acc, value_acc, result, window, sems = rest
+    rows = pieces[0].shape[0] - TILE
     mem_rows, width = kv_ref.shape
     half = width // 2
     pairs = half // LANES
@@ -109,21 +111,18 @@
     def place(d):
         return pl.ds(pl.multiple_of((member_ref[0] ^ d) * rows, rows), rows)
 
-    loads = [
-        pltpu.make_async_copy(piece, held.at[place(d)], sems.at[d])
-        for d, piece in enumerate(pieces)
-    ]
+    loads = []
+    for d, piece in enumerate(pieces):
+        loads += [
+            pltpu.make_async_copy(piece.at[pl.ds(0, rows)], held.at[place(d)], sems.at[0, d]),
+            pltpu.make_async_copy(
+                piece.at[pl.ds(rows, TILE), pl.ds(0, LANES)],
+                edges.at[member_ref[0] ^ d],
+                sems.at[1, d],
+            ),
+        ]
     for load in loads:
         load.start()
-    for load in loads:
-        load.wait()
-    for chunk in range(chunks):
-        docs = held[pl.ds(chunk * CHUNK, CHUNK), pl.ds(width, LANES)].astype(jnp.float32)
-        present = jnp.max(docs, axis=0, keepdims=True) > 0.0
-        window[chunk, 0] = jnp.min(jnp.where(present, spans_ref[0:1], float(mem_rows))).astype(
-            jnp.int32
-        )
-        window[chunk, 1] = jnp.max(jnp.where(present, spans_ref[1:2], 0.0)).astype(jnp.int32)
     low = lax.broadcasted_iota(jnp.int32, (mem_rows, LANES), 1) < DH
     zero = jnp.zeros((mem_rows, LANES), jnp.bfloat16)
     for pair in range(pairs):
@@ -138,9 +137,27 @@
     key_acc[...] = jnp.zeros_like(key_acc)
     value_acc[...] = jnp.zeros_like(value_acc)
 
+    for load in loads:
+        load.wait()
+    row = lax.broadcasted_iota(jnp.int32, (rows, LANES), 0).astype(jnp.float32)
+    for source in range(BLOCK):
+        edge = edges[source].astype(jnp.float32)
+        first, last = edge[0:1], edge[1:2]
+        inside = (row >= first) & (row < last)
+        docs[pl.ds(source * rows, rows), :] = jnp.where(inside, 1.0, 0.0).astype(jnp.bfloat16)
+        spread[0, pl.ds(source, 1), :] = first + source * rows
+        spread[1, pl.ds(source, 1), :] = last + source * rows
+    for chunk in range(chunks):
+        opens = jnp.maximum(spread[0], float(chunk * CHUNK))
+        present = opens < jnp.minimum(spread[1], float((chunk + 1) * CHUNK))
+        window[chunk, 0] = jnp.min(jnp.where(present, spans_ref[0:1], float(mem_rows))).astype(
+            jnp.int32
+        )
+        window[chunk, 1] = jnp.max(jnp.where(present, spans_ref[1:2], 0.0)).astype(jnp.int32)
+
     def on_window(here, start, span):
         mine = pl.ds(start, span)
-        docs = held[here, pl.ds(width, LANES)]
+        chunk_docs = docs[here, :]
         half_lanes = lax.broadcasted_iota(jnp.int32, (span, LANES), 1) < DH
         key_columns = [pl.ds(pair * LANES, LANES) for pair in range(pairs)]
         value_columns = [pl.ds(half + pair * LANES, LANES) for pair in range(pairs)]
@@ -149,7 +166,7 @@
         scores = [
             nt_dot(
                 key_aug[pair, :, mine, :].reshape(2 * span, 2 * LANES),
-                jnp.concatenate([query[pair], docs], axis=1),
+                jnp.concatenate([query[pair], chunk_docs], axis=1),
             ).reshape(2, span, CHUNK)
             for pair in range(pairs)
         ]
@@ -204,14 +221,14 @@
         grad_ref[:, pl.ds(half + pair * LANES, LANES)] = value_acc[pair].astype(jnp.bfloat16)
     run_copies(
         [
-            pltpu.make_async_copy(result.at[place(d)], out, sems.at[d])
+            pltpu.make_async_copy(result.at[place(d)], out, sems.at[0, d])
             for d, out in enumerate(outs)
         ]
     )
 
 
 def attend(member, far, spans, memory, pieces):
-    rows = pieces[0].shape[0]
+    rows = pieces[0].shape[0] - TILE
     mem_rows, width = memory.shape
     all_rows = BLOCK * rows
     heads = width // (2 * DH)
@@ -223,7 +240,10 @@
         in_specs=[SMEM] + [VMEM] * 3 + [ANY] * BLOCK,
         out_specs=[VMEM] + [ANY] * BLOCK,
         scratch_shapes=[
-            pltpu.VMEM((all_rows, width + LANES), half),
+            pltpu.VMEM((all_rows, width), half),
+            pltpu.VMEM((BLOCK, TILE, LANES), half),
+            pltpu.VMEM((2, BLOCK, LANES), jnp.float32),
+            pltpu.VMEM((all_rows, LANES), half),
             pltpu.VMEM((heads // 2, mem_rows, LANES), half),
             pltpu.VMEM((heads // 2, 2, mem_rows, 2 * LANES), half),
             pltpu.VMEM((heads // 2, 2, mem_rows, LANES), half),
@@ -231,7 +251,7 @@
             pltpu.VMEM((heads // 2, mem_rows, LANES), jnp.float32),
             pltpu.VMEM((all_rows, width), half),
             pltpu.SMEM((8, 2), jnp.int32),
-            pltpu.SemaphoreType.DMA((BLOCK,)),
+            pltpu.SemaphoreType.DMA((2, BLOCK)),
         ],
         compiler_params=pltpu.CompilerParams(vmem_limit_bytes=VMEM_BYTES),
         cost_estimate=pl.CostEstimate(
@@ -270,18 +290,23 @@
     member = lax.axis_index("ctx") % BLOCK
     member_ref = member.reshape(1).astype(jnp.int32)
     doc_lanes = jnp.arange(LANES, dtype=jnp.int32)
-    row_docs = (decoder_docs[0][:, None] == doc_lanes[None, :]).astype(half)
+    bounds = jnp.stack(
+        [
+            jnp.sum(decoder_docs[0][:, None] < doc_lanes[None, :], axis=0),
+            jnp.sum(decoder_docs[0][:, None] <= doc_lanes[None, :], axis=0),
+        ]
+    ).astype(half)
+    bounds = jnp.pad(bounds, ((0, TILE - 2), (0, part_width - LANES)))
     far = jnp.where(memory_docs[0][:, None] == doc_lanes[None, :], 0.0, FAR).astype(half)
     starts = jnp.sum(memory_docs[0][:, None] < doc_lanes[None, :], axis=0)
     ends = jnp.sum(memory_docs[0][:, None] <= doc_lanes[None, :], axis=0)
     spans = jnp.stack([starts, ends] + [starts] * 6).astype(jnp.float32)
-    pieces = pack(member_ref, queries, out_grad, row_docs)
+    pieces = list(pack(member_ref, queries, out_grad, bounds))
     exchange = [
         [(c, c ^ d) for c in range(column_count)] for d in range(BLOCK)
     ]
-    pieces = [pieces[0]] + [
-        lax.ppermute(pieces[d], "ctx", exchange[d]) for d in range(1, BLOCK)
-    ]
+    for d in EARLY + LATE:
+        pieces[d] = lax.ppermute(pieces[d], "ctx", exchange[d])
 
     recv_label = received[:, 2 * head_width].astype(jnp.int32)
     filling = recv_label[:, None] - 1 == token_index[None, :]
@@ -294,22 +319,19 @@
     by_column = jnp.broadcast_to(
         by_member, (column_count // BLOCK, BLOCK, enc_rows, part_width)
     ).reshape(column_count, enc_rows, part_width)
-    by_column, pieces[1 : 1 + EARLY] = lax.optimization_barrier(
-        (by_column, pieces[1 : 1 + EARLY])
-    )
+    for d in EARLY:
+        by_column, pieces[d] = lax.optimization_barrier((by_column, pieces[d]))
     group_part = lax.all_to_all(by_column, "ctx", split_axis=0, concat_axis=0, tiled=True)
     group_part = group_part.reshape(column_count * enc_rows, part_width)
 
     part_grad, *results = attend(member_ref, far, spans, group_part, pieces)
 
-    results = [results[0]] + [
-        lax.ppermute(results[d], "ctx", exchange[d]) for d in range(1, BLOCK)
-    ]
+    for d in RETURNED + LAST:
+        results[d] = lax.ppermute(results[d], "ctx", exchange[d])
     part_grad = part_grad.reshape(column_count, enc_rows, part_width)
     partials = lax.all_to_all(part_grad, "ctx", split_axis=0, concat_axis=0, tiled=True)
-    partials, results[1 : 1 + RETURNED] = lax.optimization_barrier(
-        (partials, results[1 : 1 + RETURNED])
-    )
+    for d in RETURNED:
+        partials, results[d] = lax.optimization_barrier((partials, results[d]))
     partials = partials.reshape(column_count // BLOCK, BLOCK, enc_rows, 2, part_width // 2)
     memory_grad = jnp.sum(partials.astype(jnp.float32), axis=0).astype(half)
     memory_grad = memory_grad.transpose(1, 2, 0, 3).reshape(enc_rows, 2 * head_width)

time: 150 us -> 140 us (0.933)
  waiting for transfers between devices: 34 us -> 24.8 us
  starting transfers between devices: 90.4 us -> 92.3 us
  local copies, waits for them, and re-layouts: 8.34 us -> 6.67 us
    ppermute x14, waiting for transfers between devices: 28.8 us -> 17.6 us  [the longest x7 9.59 us: shards(): results[d] = lax.ppermute(results[d], 'ctx', exchange[d])]
    all_to_all x1, waiting for transfers between devices: 0.01 us -> 3.62 us  [shards(): lax.all_to_all(part_grad, 'ctx', split_axis=0, concat_axis=0, tiled=True)]
    all_to_all x1, starting transfers between devices: 10 us -> 13 us  [shards(): lax.all_to_all(back_pairs, 'dp', split_axis=0, concat_axis=0, tiled=True)]
    unnamed x19 -> x15, local copies, waits for them, and re-layouts: 3.04 us -> 2.38 us
  transfers between devices with their start and end apart: 18 -> 18, of which waited for: 10 -> 9; matrix products, arithmetic and copies ran while one was open for 1% -> 1% of each run, Pallas kernels for 1% -> 1%
where the time goes in v3:
time: 140 us; the launch traced here: 139 us
  starting transfers between devices  92.3 us (66%)
  waiting for transfers between devices  24.8 us (18%)
  Pallas kernels  11.4 us (8%)
  local copies, waits for them, and re-layouts  6.67 us (5%)
  other arithmetic  2.07 us (1%)
    ppermute x7, starting transfers between devices, shards(): pieces[d] = lax.ppermute(pieces[d], 'ctx', exchange[d])  24.5 us
    ppermute x7, starting transfers between devices, shards(): results[d] = lax.ppermute(results[d], 'ctx', exchange[d])  22.9 us
    all_to_all x1, starting transfers between devices, shards(): lax.all_to_all(send_pairs, 'dp', split_axis=0, concat_axis=0, tiled=True)  16.7 us
    all_to_all x1, starting transfers between devices, shards(): lax.all_to_all(back_pairs, 'dp', split_axis=0, concat_axis=0, tiled=True)  13 us
    pallas_call x1, Pallas kernels, attend(): pl.pallas_call(attend_kernel, out_shape=[jax.ShapeDtypeStruct((mem_rows,...  9.99 us
    all_to_all x1, starting transfers between devices, shards(): lax.all_to_all(by_column, 'ctx', split_axis=0, concat_axis=0, tiled=True)  9.72 us
    ppermute x7, waiting for transfers between devices, shards(): results[d] = lax.ppermute(results[d], 'ctx', exchange[d])  9.59 us
    ppermute x7, waiting for transfers between devices, shards(): pieces[d] = lax.ppermute(pieces[d], 'ctx', exchange[d])  8.04 us
  transfers between devices with their start and end apart: 18, of which 9 were waited for; matrix products, arithmetic and copies ran while one was open for 1% of the time, Pallas kernels for 1%

profile of v3, /device:TPU:1, one launch (start us, length us, event | category | flops | bytes accessed | tf_op | source)
XLA Modules:
  0.0 139.4 jit_solution(17577469086710843187)
XLA Ops:
  3.7 16.7 %all-to-all-start = ((bf16[24,2,4224]{2,1,0:T(2,128)(2,1)}), bf16[24,2,4224]{2,1,0:T(2,128)(2,1)S(1)}, u32[]{:S(2)}, u32[]{:S(2)}) async-start(bf16[24,2,4224]{2,1,0:T(2,128)(2,1)} %all_to_all.22), calls=%async_computation | async-start | bytes 811008 | tf_op jit(solution)/shard_map/all_to_all | solution.py:288
  21.4 4.7 %collective-permute-start = (bf16[176,512]{1,0:T(8,128)(2,1)S(1)}, bf16[176,512]{1,0:T(8,128)(2,1)S(1)}, u32[]{:S(2)}, u32[]{:S(2)}) collective-permute-start(bf16[176,512]{1,0:T(8,128)(2,1)S(1)} %get-tuple-element.36), channel_id=1, source_target_pairs={{0,2},{1,3},{2,0},{3,1},{4,6},{5,7},{6,4},{7,5},{8,10},{9,11},{10,... | collective-permute-start | bytes 540680 | tf_op jit(solution)/shard_map/ppermute | solution.py:309
  26.1 3.1 %collective-permute-start.1 = (bf16[176,512]{1,0:T(8,128)(2,1)S(1)}, bf16[176,512]{1,0:T(8,128)(2,1)S(1)}, u32[]{:S(2)}, u32[]{:S(2)}) collective-permute-start(bf16[176,512]{1,0:T(8,128)(2,1)S(1)} %get-tuple-element.38), channel_id=1, source_target_pairs={{0,6},{1,7},{2,4},{3,5},{4,2},{5,3},{6,0},{7,1},{8,14},{9,15},{10,... | collective-permute-start | bytes 540680 | tf_op jit(solution)/shard_map/ppermute | solution.py:309
  29.2 3.0 %collective-permute-start.2 = (bf16[176,512]{1,0:T(8,128)(2,1)S(1)}, bf16[176,512]{1,0:T(8,128)(2,1)S(1)}, u32[]{:S(2)}, u32[]{:S(2)}) collective-permute-start(bf16[176,512]{1,0:T(8,128)(2,1)S(1)} %get-tuple-element.40), channel_id=1, source_target_pairs={{0,5},{1,4},{2,7},{3,6},{4,1},{5,0},{6,3},{7,2},{8,13},{9,12},{10,... | collective-permute-start | bytes 540680 | tf_op jit(solution)/shard_map/ppermute | solution.py:309
  32.3 3.2 %collective-permute-start.3 = (bf16[176,512]{1,0:T(8,128)(2,1)S(1)}, bf16[176,512]{1,0:T(8,128)(2,1)S(1)}, u32[]{:S(2)}, u32[]{:S(2)}) collective-permute-start(bf16[176,512]{1,0:T(8,128)(2,1)S(1)} %get-tuple-element.42), channel_id=1, source_target_pairs={{0,4},{1,5},{2,6},{3,7},{4,0},{5,1},{6,2},{7,3},{8,12},{9,13},{10,... | collective-permute-start | bytes 540680 | tf_op jit(solution)/shard_map/ppermute | solution.py:309
  35.5 3.5 %all-to-all-done = bf16[24,2,4224]{2,1,0:T(2,128)(2,1)S(1)} async-done(((bf16[24,2,4224]{2,1,0:T(2,128)(2,1)}), bf16[24,2,4224]{2,1,0:T(2,128)(2,1)S(1)}, u32[]{:S(2)}, u32[]{:S(2)}) %all-to-all-start) | async-done | bytes 405536 | tf_op jit(solution)/shard_map/all_to_all | solution.py:288
  41.3 9.7 %all-to-all-start.1 = ((bf16[32,16,512]{2,1,0:T(8,128)(2,1)}), bf16[32,16,512]{2,1,0:T(8,128)(2,1)S(1)}, u32[]{:S(2)}, u32[]{:S(2)}) async-start(bf16[32,16,512]{2,1,0:T(8,128)(2,1)} %bitcast.5), calls=%async_computation.1 | async-start | bytes 1048576 | tf_op jit(solution)/shard_map/all_to_all | solution.py:324
  51.0 3.1 %collective-permute-start.4 = (bf16[176,512]{1,0:T(8,128)(2,1)S(1)}, bf16[176,512]{1,0:T(8,128)(2,1)S(1)}, u32[]{:S(2)}, u32[]{:S(2)}) collective-permute-start(bf16[176,512]{1,0:T(8,128)(2,1)S(1)} %get-tuple-element.45), channel_id=1, source_target_pairs={{0,1},{1,0},{2,3},{3,2},{4,5},{5,4},{6,7},{7,6},{8,9},{9,8},{10,11... | collective-permute-start | bytes 540680 | tf_op jit(solution)/shard_map/ppermute | solution.py:309
  54.1 3.7 %collective-permute-start.5 = (bf16[176,512]{1,0:T(8,128)(2,1)S(1)}, bf16[176,512]{1,0:T(8,128)(2,1)S(1)}, u32[]{:S(2)}, u32[]{:S(2)}) collective-permute-start(bf16[176,512]{1,0:T(8,128)(2,1)S(1)} %get-tuple-element.47), channel_id=1, source_target_pairs={{0,3},{1,2},{2,1},{3,0},{4,7},{5,6},{6,5},{7,4},{8,11},{9,10},{10,... | collective-permute-start | bytes 540680 | tf_op jit(solution)/shard_map/ppermute | solution.py:309
  57.9 3.7 %collective-permute-start.6 = (bf16[176,512]{1,0:T(8,128)(2,1)S(1)}, bf16[176,512]{1,0:T(8,128)(2,1)S(1)}, u32[]{:S(2)}, u32[]{:S(2)}) collective-permute-start(bf16[176,512]{1,0:T(8,128)(2,1)S(1)} %get-tuple-element.51), channel_id=1, source_target_pairs={{0,7},{1,6},{2,5},{3,4},{4,3},{5,2},{6,1},{7,0},{8,15},{9,14},{10,... | collective-permute-start | bytes 540680 | tf_op jit(solution)/shard_map/ppermute | solution.py:309
  63.5 5.9 %collective-permute-done.6.rest_7_ = bf16[176,512]{1,0:T(8,128)(2,1)S(1)} collective-permute-done((bf16[176,512]{1,0:T(8,128)(2,1)S(1)}, bf16[176,512]{1,0:T(8,128)(2,1)S(1)}, u32[]{:S(2)}, u32[]{:S(2)}) %collective-permute-start.6) | collective-permute-done | bytes 180256 | tf_op jit(solution)/shard_map/ppermute | solution.py:309
  69.4 10.0 %attend.1 = (bf16[512,512]{1,0:T(8,128)(2,1)}, bf16[160,512]{1,0:T(8,128)(2,1)S(1)}, bf16[160,512]{1,0:T(8,128)(2,1)S(1)}, bf16[160,512]{1,0:T(8,128)(2,1)S(1)},...) custom-call(s32[1]{0:T(128)} %bitcast.member_ref, ...), custom_call_target="tpu_custom_call" | custom-call | flops 2013265920 | bytes 5242880 | tf_op jit(solution)/shard_map/attend/pallas_call | solution.py:236
  80.0 5.5 %all-to-all-start.2 = ((bf16[32,16,512]{2,1,0:T(8,128)(2,1)}), bf16[32,16,512]{2,1,0:T(8,128)(2,1)S(1)}, u32[]{:S(2)}, u32[]{:S(2)}) async-start(bf16[32,16,512]{2,1,0:T(8,128)(2,1)} %bitcast.10), calls=%async_computation.2 | async-start | bytes 1048576 | tf_op jit(solution)/shard_map/all_to_all | solution.py:332
  85.6 4.6 %collective-permute-start.7 = (bf16[160,512]{1,0:T(8,128)(2,1)S(1)}, bf16[160,512]{1,0:T(8,128)(2,1)S(1)}, u32[]{:S(2)}, u32[]{:S(2)}) collective-permute-start(bf16[160,512]{1,0:T(8,128)(2,1)S(1)} %copy-done.3), channel_id=1, source_target_pairs={{0,2},{1,3},{2,0},{3,1},{4,6},{5,7},{6,4},{7,5},{8,10},{9,11},{10,... | collective-permute-start | bytes 491528 | tf_op jit(solution)/shard_map/ppermute | solution.py:330
  92.4 2.5 %collective-permute-start.9 = (bf16[160,512]{1,0:T(8,128)(2,1)S(1)}, bf16[160,512]{1,0:T(8,128)(2,1)S(1)}, u32[]{:S(2)}, u32[]{:S(2)}) collective-permute-start(bf16[160,512]{1,0:T(8,128)(2,1)S(1)} %get-tuple-element.60), channel_id=1, source_target_pairs={{0,3},{1,2},{2,1},{3,0},{4,7},{5,6},{6,5},{7,4},{8,11},{9,10},{10,... | collective-permute-start | bytes 491528 | tf_op jit(solution)/shard_map/ppermute | solution.py:330
  95.0 3.6 %all-to-all-done.2 = bf16[32,16,512]{2,1,0:T(8,128)(2,1)S(1)} async-done(((bf16[32,16,512]{2,1,0:T(8,128)(2,1)}), bf16[32,16,512]{2,1,0:T(8,128)(2,1)S(1)}, u32[]{:S(2)}, u32[]{:S(2)}) %all-to-all-start.2) | async-done | bytes 524320 | tf_op jit(solution)/shard_map/all_to_all | solution.py:332
  100.3 2.6 %collective-permute-done.9.rest_3_ = bf16[160,512]{1,0:T(8,128)(2,1)S(1)} collective-permute-done((bf16[160,512]{1,0:T(8,128)(2,1)S(1)}, bf16[160,512]{1,0:T(8,128)(2,1)S(1)}, u32[]{:S(2)}, u32[]{:S(2)}) %collective-permute-start.9) | collective-permute-done | bytes 163872 | tf_op jit(solution)/shard_map/ppermute | solution.py:330
  105.1 13.0 %all-to-all-start.3 = ((bf16[24,2,4096]{2,1,0:T(2,128)(2,1)}), bf16[24,2,4096]{2,1,0:T(2,128)(2,1)S(1)}, u32[]{:S(2)}, u32[]{:S(2)}) async-start(bf16[24,2,4096]{2,1,0:T(2,128)(2,1)} %all_to_all.27), calls=%async_computation.3 | async-start | bytes 786432 | tf_op jit(solution)/shard_map/all_to_all | solution.py:339
  118.1 3.1 %collective-permute-start.10 = (bf16[160,512]{1,0:T(8,128)(2,1)S(1)}, bf16[160,512]{1,0:T(8,128)(2,1)S(1)}, u32[]{:S(2)}, u32[]{:S(2)}) collective-permute-start(bf16[160,512]{1,0:T(8,128)(2,1)S(1)} %get-tuple-element.62), channel_id=1, source_target_pairs={{0,4},{1,5},{2,6},{3,7},{4,0},{5,1},{6,2},{7,3},{8,12},{9,13},{10,... | collective-permute-start | bytes 491528 | tf_op jit(solution)/shard_map/ppermute | solution.py:330
  121.2 2.3 %collective-permute-start.11 = (bf16[160,512]{1,0:T(8,128)(2,1)S(1)}, bf16[160,512]{1,0:T(8,128)(2,1)S(1)}, u32[]{:S(2)}, u32[]{:S(2)}) collective-permute-start(bf16[160,512]{1,0:T(8,128)(2,1)S(1)} %get-tuple-element.63), channel_id=1, source_target_pairs={{0,5},{1,4},{2,7},{3,6},{4,1},{5,0},{6,3},{7,2},{8,13},{9,12},{10,... | collective-permute-start | bytes 491528 | tf_op jit(solution)/shard_map/ppermute | solution.py:330
  123.5 4.4 %collective-permute-start.12 = (bf16[160,512]{1,0:T(8,128)(2,1)S(1)}, bf16[160,512]{1,0:T(8,128)(2,1)S(1)}, u32[]{:S(2)}, u32[]{:S(2)}) collective-permute-start(bf16[160,512]{1,0:T(8,128)(2,1)S(1)} %get-tuple-element.64), channel_id=1, source_target_pairs={{0,6},{1,7},{2,4},{3,5},{4,2},{5,3},{6,0},{7,1},{8,14},{9,15},{10,... | collective-permute-start | bytes 491528 | tf_op jit(solution)/shard_map/ppermute | solution.py:330
  128.0 3.7 %collective-permute-start.13 = (bf16[160,512]{1,0:T(8,128)(2,1)S(1)}, bf16[160,512]{1,0:T(8,128)(2,1)S(1)}, u32[]{:S(2)}, u32[]{:S(2)}) collective-permute-start(bf16[160,512]{1,0:T(8,128)(2,1)S(1)} %get-tuple-element.65), channel_id=1, source_target_pairs={{0,7},{1,6},{2,5},{3,4},{4,3},{5,2},{6,1},{7,0},{8,15},{9,14},{10,... | collective-permute-start | bytes 491528 | tf_op jit(solution)/shard_map/ppermute | solution.py:330
  131.7 2.3 %collective-permute-done.12.rest_6_ = bf16[160,512]{1,0:T(8,128)(2,1)S(1)} collective-permute-done((bf16[160,512]{1,0:T(8,128)(2,1)S(1)}, bf16[160,512]{1,0:T(8,128)(2,1)S(1)}, u32[]{:S(2)}, u32[]{:S(2)}) %collective-permute-start.12) | collective-permute-done | bytes 163872 | tf_op jit(solution)/shard_map/ppermute | solution.py:330
  134.0 3.0 %collective-permute-done.13.rest_7_ = bf16[160,512]{1,0:T(8,128)(2,1)S(1)} collective-permute-done((bf16[160,512]{1,0:T(8,128)(2,1)S(1)}, bf16[160,512]{1,0:T(8,128)(2,1)S(1)}, u32[]{:S(2)}, u32[]{:S(2)}) %collective-permute-start.13) | collective-permute-done | bytes 163872 | tf_op jit(solution)/shard_map/ppermute | solution.py:330
  (57 shorter events, 17.3 us)
Async XLA Ops:
  2.8 18.5 %copy-start = (bf16[160,2048]{1,0:T(8,128)(2,1)S(1)}, bf16[160,2048]{1,0:T(8,128)(2,1)}, u32[]{:S(2)}) copy-start(bf16[160,2048]{1,0:T(8,128)(2,1)} %queries_ref.1) | copy-start | bytes 1966084
  2.8 18.4 %copy-start.1 = (bf16[160,2048]{1,0:T(8,128)(2,1)S(1)}, bf16[160,2048]{1,0:T(8,128)(2,1)}, u32[]{:S(2)}) copy-start(bf16[160,2048]{1,0:T(8,128)(2,1)} %grads_ref.1) | copy-start | bytes 1966084
  3.7 35.3 %all-to-all-start = ((bf16[24,2,4224]{2,1,0:T(2,128)(2,1)}), bf16[24,2,4224]{2,1,0:T(2,128)(2,1)S(1)}, u32[]{:S(2)}, u32[]{:S(2)}) async-start(bf16[24,2,4224]{2,1,0:T(2,128)(2,1)} %all_to_all.22), calls=%async_computation | async-start | bytes 811008 | tf_op jit(solution)/shard_map/all_to_all | solution.py:288
  20.4 0.7 copy-start.5
  21.4 18.4 %collective-permute-start = (bf16[176,512]{1,0:T(8,128)(2,1)S(1)}, bf16[176,512]{1,0:T(8,128)(2,1)S(1)}, u32[]{:S(2)}, u32[]{:S(2)}) collective-permute-start(bf16[176,512]{1,0:T(8,128)(2,1)S(1)} %get-tuple-element.36), channel_id=1, source_target_pairs={{0,2},{1,3},{2,0},{3,1},{4,6},{5,7},{6,4},{7,5},{8,10},{9,11},{10,... | collective-permute-start | bytes 540680 | tf_op jit(solution)/shard_map/ppermute | solution.py:309
  26.1 14.6 %collective-permute-start.1 = (bf16[176,512]{1,0:T(8,128)(2,1)S(1)}, bf16[176,512]{1,0:T(8,128)(2,1)S(1)}, u32[]{:S(2)}, u32[]{:S(2)}) collective-permute-start(bf16[176,512]{1,0:T(8,128)(2,1)S(1)} %get-tuple-element.38), channel_id=1, source_target_pairs={{0,6},{1,7},{2,4},{3,5},{4,2},{5,3},{6,0},{7,1},{8,14},{9,15},{10,... | collective-permute-start | bytes 540680 | tf_op jit(solution)/shard_map/ppermute | solution.py:309
  29.2 11.4 %collective-permute-start.2 = (bf16[176,512]{1,0:T(8,128)(2,1)S(1)}, bf16[176,512]{1,0:T(8,128)(2,1)S(1)}, u32[]{:S(2)}, u32[]{:S(2)}) collective-permute-start(bf16[176,512]{1,0:T(8,128)(2,1)S(1)} %get-tuple-element.40), channel_id=1, source_target_pairs={{0,5},{1,4},{2,7},{3,6},{4,1},{5,0},{6,3},{7,2},{8,13},{9,12},{10,... | collective-permute-start | bytes 540680 | tf_op jit(solution)/shard_map/ppermute | solution.py:309
  32.3 9.0 %collective-permute-start.3 = (bf16[176,512]{1,0:T(8,128)(2,1)S(1)}, bf16[176,512]{1,0:T(8,128)(2,1)S(1)}, u32[]{:S(2)}, u32[]{:S(2)}) collective-permute-start(bf16[176,512]{1,0:T(8,128)(2,1)S(1)} %get-tuple-element.42), channel_id=1, source_target_pairs={{0,4},{1,5},{2,6},{3,7},{4,0},{5,1},{6,2},{7,3},{8,12},{9,13},{10,... | collective-permute-start | bytes 540680 | tf_op jit(solution)/shard_map/ppermute | solution.py:309
  41.3 28.1 %all-to-all-start.1 = ((bf16[32,16,512]{2,1,0:T(8,128)(2,1)}), bf16[32,16,512]{2,1,0:T(8,128)(2,1)S(1)}, u32[]{:S(2)}, u32[]{:S(2)}) async-start(bf16[32,16,512]{2,1,0:T(8,128)(2,1)} %bitcast.5), calls=%async_computation.1 | async-start | bytes 1048576 | tf_op jit(solution)/shard_map/all_to_all | solution.py:324
  51.0 10.9 %collective-permute-start.4 = (bf16[176,512]{1,0:T(8,128)(2,1)S(1)}, bf16[176,512]{1,0:T(8,128)(2,1)S(1)}, u32[]{:S(2)}, u32[]{:S(2)}) collective-permute-start(bf16[176,512]{1,0:T(8,128)(2,1)S(1)} %get-tuple-element.45), channel_id=1, source_target_pairs={{0,1},{1,0},{2,3},{3,2},{4,5},{5,4},{6,7},{7,6},{8,9},{9,8},{10,11... | collective-permute-start | bytes 540680 | tf_op jit(solution)/shard_map/ppermute | solution.py:309
  54.1 7.4 %copy-start.4 = (s32[1,512]{1,0:T(1,128)S(1)}, s32[1,512]{1,0:T(1,128)}, u32[]{:S(2)}) copy-start(s32[1,512]{1,0:T(1,128)} %param.10) | copy-start | bytes 6148
  54.1 9.3 %collective-permute-start.5 = (bf16[176,512]{1,0:T(8,128)(2,1)S(1)}, bf16[176,512]{1,0:T(8,128)(2,1)S(1)}, u32[]{:S(2)}, u32[]{:S(2)}) collective-permute-start(bf16[176,512]{1,0:T(8,128)(2,1)S(1)} %get-tuple-element.47), channel_id=1, source_target_pairs={{0,3},{1,2},{2,1},{3,0},{4,7},{5,6},{6,5},{7,4},{8,11},{9,10},{10,... | collective-permute-start | bytes 540680 | tf_op jit(solution)/shard_map/ppermute | solution.py:309
  57.9 11.5 %collective-permute-start.6 = (bf16[176,512]{1,0:T(8,128)(2,1)S(1)}, bf16[176,512]{1,0:T(8,128)(2,1)S(1)}, u32[]{:S(2)}, u32[]{:S(2)}) collective-permute-start(bf16[176,512]{1,0:T(8,128)(2,1)S(1)} %get-tuple-element.51), channel_id=1, source_target_pairs={{0,7},{1,6},{2,5},{3,4},{4,3},{5,2},{6,1},{7,0},{8,15},{9,14},{10,... | collective-permute-start | bytes 540680 | tf_op jit(solution)/shard_map/ppermute | solution.py:309
  79.4 0.7 copy-start.2
  80.0 5.5 %copy-start.3 = (bf16[160,512]{1,0:T(8,128)(2,1)S(1)}, bf16[160,512]{1,0:T(8,128)(2,1)}, u32[]{:S(2)}) copy-start(bf16[160,512]{1,0:T(8,128)(2,1)} %copy-done.2) | copy-start | bytes 491524
  80.0 18.6 %all-to-all-start.2 = ((bf16[32,16,512]{2,1,0:T(8,128)(2,1)}), bf16[32,16,512]{2,1,0:T(8,128)(2,1)S(1)}, u32[]{:S(2)}, u32[]{:S(2)}) async-start(bf16[32,16,512]{2,1,0:T(8,128)(2,1)} %bitcast.10), calls=%async_computation.2 | async-start | bytes 1048576 | tf_op jit(solution)/shard_map/all_to_all | solution.py:332
  85.6 9.4 %collective-permute-start.7 = (bf16[160,512]{1,0:T(8,128)(2,1)S(1)}, bf16[160,512]{1,0:T(8,128)(2,1)S(1)}, u32[]{:S(2)}, u32[]{:S(2)}) collective-permute-start(bf16[160,512]{1,0:T(8,128)(2,1)S(1)} %copy-done.3), channel_id=1, source_target_pairs={{0,2},{1,3},{2,0},{3,1},{4,6},{5,7},{6,4},{7,5},{8,10},{9,11},{10,... | collective-permute-start | bytes 491528 | tf_op jit(solution)/shard_map/ppermute | solution.py:330
  90.2 10.1 %collective-permute-start.8 = (bf16[160,512]{1,0:T(8,128)(2,1)S(1)}, bf16[160,512]{1,0:T(8,128)(2,1)S(1)}, u32[]{:S(2)}, u32[]{:S(2)}) collective-permute-start(bf16[160,512]{1,0:T(8,128)(2,1)S(1)} %get-tuple-element.56), channel_id=1, source_target_pairs={{0,1},{1,0},{2,3},{3,2},{4,5},{5,4},{6,7},{7,6},{8,9},{9,8},{10,11... | collective-permute-start | bytes 491528 | tf_op jit(solution)/shard_map/ppermute | solution.py:330
  92.4 10.4 %collective-permute-start.9 = (bf16[160,512]{1,0:T(8,128)(2,1)S(1)}, bf16[160,512]{1,0:T(8,128)(2,1)S(1)}, u32[]{:S(2)}, u32[]{:S(2)}) collective-permute-start(bf16[160,512]{1,0:T(8,128)(2,1)S(1)} %get-tuple-element.60), channel_id=1, source_target_pairs={{0,3},{1,2},{2,1},{3,0},{4,7},{5,6},{6,5},{7,4},{8,11},{9,10},{10,... | collective-permute-start | bytes 491528 | tf_op jit(solution)/shard_map/ppermute | solution.py:330
  105.1 33.1 %all-to-all-start.3 = ((bf16[24,2,4096]{2,1,0:T(2,128)(2,1)}), bf16[24,2,4096]{2,1,0:T(2,128)(2,1)S(1)}, u32[]{:S(2)}, u32[]{:S(2)}) async-start(bf16[24,2,4096]{2,1,0:T(2,128)(2,1)} %all_to_all.27), calls=%async_computation.3 | async-start | bytes 786432 | tf_op jit(solution)/shard_map/all_to_all | solution.py:339
  118.1 13.6 %collective-permute-start.10 = (bf16[160,512]{1,0:T(8,128)(2,1)S(1)}, bf16[160,512]{1,0:T(8,128)(2,1)S(1)}, u32[]{:S(2)}, u32[]{:S(2)}) collective-permute-start(bf16[160,512]{1,0:T(8,128)(2,1)S(1)} %get-tuple-element.62), channel_id=1, source_target_pairs={{0,4},{1,5},{2,6},{3,7},{4,0},{5,1},{6,2},{7,3},{8,12},{9,13},{10,... | collective-permute-start | bytes 491528 | tf_op jit(solution)/shard_map/ppermute | solution.py:330
  121.2 10.5 %collective-permute-start.11 = (bf16[160,512]{1,0:T(8,128)(2,1)S(1)}, bf16[160,512]{1,0:T(8,128)(2,1)S(1)}, u32[]{:S(2)}, u32[]{:S(2)}) collective-permute-start(bf16[160,512]{1,0:T(8,128)(2,1)S(1)} %get-tuple-element.63), channel_id=1, source_target_pairs={{0,5},{1,4},{2,7},{3,6},{4,1},{5,0},{6,3},{7,2},{8,13},{9,12},{10,... | collective-permute-start | bytes 491528 | tf_op jit(solution)/shard_map/ppermute | solution.py:330
  123.5 10.5 %collective-permute-start.12 = (bf16[160,512]{1,0:T(8,128)(2,1)S(1)}, bf16[160,512]{1,0:T(8,128)(2,1)S(1)}, u32[]{:S(2)}, u32[]{:S(2)}) collective-permute-start(bf16[160,512]{1,0:T(8,128)(2,1)S(1)} %get-tuple-element.64), channel_id=1, source_target_pairs={{0,6},{1,7},{2,4},{3,5},{4,2},{5,3},{6,0},{7,1},{8,14},{9,15},{10,... | collective-permute-start | bytes 491528 | tf_op jit(solution)/shard_map/ppermute | solution.py:330
  128.0 9.1 %collective-permute-start.13 = (bf16[160,512]{1,0:T(8,128)(2,1)S(1)}, bf16[160,512]{1,0:T(8,128)(2,1)S(1)}, u32[]{:S(2)}, u32[]{:S(2)}) collective-permute-start(bf16[160,512]{1,0:T(8,128)(2,1)S(1)} %get-tuple-element.65), channel_id=1, source_target_pairs={{0,7},{1,6},{2,5},{3,4},{4,3},{5,2},{6,1},{7,0},{8,15},{9,14},{10,... | collective-permute-start | bytes 491528 | tf_op jit(solution)/shard_map/ppermute | solution.py:330

commit v4 on v3

--- a/solution.py
+++ b/solution.py
@@ -13,7 +13,8 @@
 FAR = -1e30
 BLOCK = 8
 CHUNK = 256
-SPANS = (64, 128, 256, 384, 512)
+SPANS = (64, 128, 192, 256, 384, 512)
+TOGETHER = (192,)
 VMEM_BYTES = 48 * 1024 * 1024
 COPY_BYTES = 16 * 1024 * 1024
 EARLY, LATE = (2, 6, 5, 4), (7, 3, 1)
@@ -155,67 +156,96 @@
         )
         window[chunk, 1] = jnp.max(jnp.where(present, spans_ref[1:2], 0.0)).astype(jnp.int32)
 
-    def on_window(here, start, span):
-        mine = pl.ds(start, span)
-        chunk_docs = docs[here, :]
+    key_columns = [pl.ds(pair * LANES, LANES) for pair in range(pairs)]
+    value_columns = [pl.ds(half + pair * LANES, LANES) for pair in range(pairs)]
+
+    def on_windows(heres, starts, span):
         half_lanes = lax.broadcasted_iota(jnp.int32, (span, LANES), 1) < DH
-        key_columns = [pl.ds(pair * LANES, LANES) for pair in range(pairs)]
-        value_columns = [pl.ds(half + pair * LANES, LANES) for pair in range(pairs)]
-        query = [held[here, columns] for columns in key_columns]
-        grad = [held[here, columns] for columns in value_columns]
+        items = [
+            (pair, here, pl.ds(start, span))
+            for here, start in zip(heres, starts)
+            for pair in range(pairs)
+        ]
+        query = [held[here, key_columns[pair]] for pair, here, _ in items]
+        grad = [held[here, value_columns[pair]] for pair, here, _ in items]
         scores = [
             nt_dot(
                 key_aug[pair, :, mine, :].reshape(2 * span, 2 * LANES),
-                jnp.concatenate([query[pair], chunk_docs], axis=1),
+                jnp.concatenate([query[i], docs[here, :]], axis=1),
             ).reshape(2, span, CHUNK)
-            for pair in range(pairs)
+            for i, (pair, here, mine) in enumerate(items)
         ]
         grad_normed = [
-            nt_dot(values[pair, :, mine, :].reshape(2 * span, LANES), grad[pair]).reshape(
+            nt_dot(values[pair, :, mine, :].reshape(2 * span, LANES), grad[i]).reshape(
                 2, span, CHUNK
             )
-            for pair in range(pairs)
+            for i, (pair, here, mine) in enumerate(items)
         ]
         rounded, grad_scores = [], []
-        for pair in range(pairs):
-            top = jnp.max(scores[pair], axis=1, keepdims=True)
-            weights = jnp.exp(scores[pair] - top)
+        for i in range(len(items)):
+            top = jnp.max(scores[i], axis=1, keepdims=True)
+            weights = jnp.exp(scores[i] - top)
             normed = weights * (1.0 / jnp.sum(weights, axis=1, keepdims=True))
-            delta = jnp.sum(normed * grad_normed[pair], axis=1, keepdims=True)
+            delta = jnp.sum(normed * grad_normed[i], axis=1, keepdims=True)
             rounded.append(normed.astype(jnp.bfloat16))
-            grad_scores.append((normed * (grad_normed[pair] - delta)).astype(jnp.bfloat16))
-        for pair in range(pairs):
-            key_grad = nn_dot(grad_scores[pair].reshape(2 * span, CHUNK), query[pair])
-            value_grad = nn_dot(rounded[pair].reshape(2 * span, CHUNK), grad[pair])
+            grad_scores.append((normed * (grad_normed[i] - delta)).astype(jnp.bfloat16))
+        for i, (pair, here, mine) in enumerate(items):
+            key_grad = nn_dot(grad_scores[i].reshape(2 * span, CHUNK), query[i])
+            value_grad = nn_dot(rounded[i].reshape(2 * span, CHUNK), grad[i])
             key_acc[pair, mine, :] += jnp.where(half_lanes, key_grad[:span], key_grad[span:])
             value_acc[pair, mine, :] += jnp.where(half_lanes, value_grad[:span], value_grad[span:])
+        for i, (pair, here, mine) in enumerate(items):
             key_turned = keys[pair, mine, :].T
             value_turned = kv_ref[mine, value_columns[pair]].T
             for columns, turned, terms in (
-                (key_columns[pair], value_turned, rounded[pair]),
-                (value_columns[pair], key_turned, grad_scores[pair]),
+                (key_columns[pair], value_turned, rounded[i]),
+                (value_columns[pair], key_turned, grad_scores[i]),
             ):
                 both = [
                     nn_dot(turned[head * DH : (head + 1) * DH], terms[head]) for head in range(2)
                 ]
                 result[here, columns] = jnp.concatenate(both, axis=0).astype(jnp.bfloat16).T
 
+    def start_of(chunk, span):
+        first = jnp.minimum((window[chunk, 0] // 16) * 16, mem_rows - span)
+        return pl.multiple_of(first, 16)
+
+    def fits(chunk, span):
+        return window[chunk, 1] <= start_of(chunk, span) + span
+
     def step(chunk, carry):
         here = pl.ds(pl.multiple_of(chunk * CHUNK, CHUNK), CHUNK)
-        first, last = window[chunk, 0], window[chunk, 1]
         taken = jnp.bool_(False)
         for span in SPANS:
-            start = jnp.minimum((first // 16) * 16, mem_rows - span)
-            fits = last <= start + span
-
-            @pl.when(fits & ~taken)
-            def _(start=start, span=span):
-                on_window(here, pl.multiple_of(start, 16), span)
-
-            taken = taken | fits
+            fit = fits(chunk, span)
+
+            @pl.when(fit & ~taken)
+            def _(span=span):
+                on_windows([here], [start_of(chunk, span)], span)
+
+            taken = taken | fit
         return carry
 
-    lax.fori_loop(0, chunks, step, 0)
+    taken = jnp.bool_(False)
+    for span in TOGETHER:
+        fit = jnp.bool_(True)
+        for chunk in range(chunks):
+            fit = fit & fits(chunk, span)
+
+        @pl.when(fit & ~taken)
+        def _(span=span):
+            on_windows(
+                [pl.ds(chunk * CHUNK, CHUNK) for chunk in range(chunks)],
+                [start_of(chunk, span) for chunk in range(chunks)],
+                span,
+            )
+
+        taken = taken | fit
+
+    @pl.when(~taken)
+    def _():
+        lax.fori_loop(0, chunks, step, 0)
+
     for pair in range(pairs):
         grad_ref[:, pl.ds(pair * LANES, LANES)] = (key_acc[pair] * scale).astype(jnp.bfloat16)
         grad_ref[:, pl.ds(half + pair * LANES, LANES)] = value_acc[pair].astype(jnp.bfloat16)

time: 140 us -> 140 us (level)
    all_to_all x1, starting transfers between devices: 5.5 us -> 7.81 us  [shards(): lax.all_to_all(part_grad, 'ctx', split_axis=0, concat_axis=0, tiled=True)]
    all_to_all x1, starting transfers between devices: 13 us -> 11.5 us  [shards(): lax.all_to_all(back_pairs, 'dp', split_axis=0, concat_axis=0, tiled=True)]
  transfers between devices with their start and end apart: 18 -> 18, of which waited for: 9 -> 10; matrix products, arithmetic and copies ran while one was open for 1% -> 1% of each run, Pallas kernels for 1% -> 1%
where the time goes in v4:
time: 140 us; the launch traced here: 139 us
  starting transfers between devices  93.2 us (67%)
  waiting for transfers between devices  24.6 us (18%)
  Pallas kernels  10.7 us (8%)
  local copies, waits for them, and re-layouts  6.67 us (5%)
  other arithmetic  2.07 us (1%)
    ppermute x7, starting transfers between devices, shards(): pieces[d] = lax.ppermute(pieces[d], 'ctx', exchange[d])  24.5 us
    ppermute x7, starting transfers between devices, shards(): results[d] = lax.ppermute(results[d], 'ctx', exchange[d])  22.9 us
    all_to_all x1, starting transfers between devices, shards(): lax.all_to_all(send_pairs, 'dp', split_axis=0, concat_axis=0, tiled=True)  16.7 us
    all_to_all x1, starting transfers between devices, shards(): lax.all_to_all(back_pairs, 'dp', split_axis=0, concat_axis=0, tiled=True)  11.5 us
    all_to_all x1, starting transfers between devices, shards(): lax.all_to_all(by_column, 'ctx', split_axis=0, concat_axis=0, tiled=True)  9.72 us
    pallas_call x1, Pallas kernels, attend(): pl.pallas_call(attend_kernel, out_shape=[jax.ShapeDtypeStruct((mem_rows,...  9.31 us
    ppermute x7, waiting for transfers between devices, shards(): results[d] = lax.ppermute(results[d], 'ctx', exchange[d])  9.31 us
    ppermute x7, waiting for transfers between devices, shards(): pieces[d] = lax.ppermute(pieces[d], 'ctx', exchange[d])  8.04 us
  transfers between devices with their start and end apart: 18, of which 10 were waited for; matrix products, arithmetic and copies ran while one was open for 1% of the time, Pallas kernels for 1%

profile of v4, /device:TPU:1, one launch (start us, length us, event | category | flops | bytes accessed | tf_op | source)
XLA Modules:
  0.0 139.3 jit_solution(9638967653803918353)
XLA Ops:
  3.7 16.7 %all-to-all-start = ((bf16[24,2,4224]{2,1,0:T(2,128)(2,1)}), bf16[24,2,4224]{2,1,0:T(2,128)(2,1)S(1)}, u32[]{:S(2)}, u32[]{:S(2)}) async-start(bf16[24,2,4224]{2,1,0:T(2,128)(2,1)} %all_to_all.22), calls=%async_computation | async-start | bytes 811008 | tf_op jit(solution)/shard_map/all_to_all | solution.py:318
  21.4 4.6 %collective-permute-start = (bf16[176,512]{1,0:T(8,128)(2,1)S(1)}, bf16[176,512]{1,0:T(8,128)(2,1)S(1)}, u32[]{:S(2)}, u32[]{:S(2)}) collective-permute-start(bf16[176,512]{1,0:T(8,128)(2,1)S(1)} %get-tuple-element.36), channel_id=1, source_target_pairs={{0,2},{1,3},{2,0},{3,1},{4,6},{5,7},{6,4},{7,5},{8,10},{9,11},{10,... | collective-permute-start | bytes 540680 | tf_op jit(solution)/shard_map/ppermute | solution.py:339
  26.1 3.1 %collective-permute-start.1 = (bf16[176,512]{1,0:T(8,128)(2,1)S(1)}, bf16[176,512]{1,0:T(8,128)(2,1)S(1)}, u32[]{:S(2)}, u32[]{:S(2)}) collective-permute-start(bf16[176,512]{1,0:T(8,128)(2,1)S(1)} %get-tuple-element.38), channel_id=1, source_target_pairs={{0,6},{1,7},{2,4},{3,5},{4,2},{5,3},{6,0},{7,1},{8,14},{9,15},{10,... | collective-permute-start | bytes 540680 | tf_op jit(solution)/shard_map/ppermute | solution.py:339
  29.2 3.0 %collective-permute-start.2 = (bf16[176,512]{1,0:T(8,128)(2,1)S(1)}, bf16[176,512]{1,0:T(8,128)(2,1)S(1)}, u32[]{:S(2)}, u32[]{:S(2)}) collective-permute-start(bf16[176,512]{1,0:T(8,128)(2,1)S(1)} %get-tuple-element.40), channel_id=1, source_target_pairs={{0,5},{1,4},{2,7},{3,6},{4,1},{5,0},{6,3},{7,2},{8,13},{9,12},{10,... | collective-permute-start | bytes 540680 | tf_op jit(solution)/shard_map/ppermute | solution.py:339
  32.3 3.2 %collective-permute-start.3 = (bf16[176,512]{1,0:T(8,128)(2,1)S(1)}, bf16[176,512]{1,0:T(8,128)(2,1)S(1)}, u32[]{:S(2)}, u32[]{:S(2)}) collective-permute-start(bf16[176,512]{1,0:T(8,128)(2,1)S(1)} %get-tuple-element.42), channel_id=1, source_target_pairs={{0,4},{1,5},{2,6},{3,7},{4,0},{5,1},{6,2},{7,3},{8,12},{9,13},{10,... | collective-permute-start | bytes 540680 | tf_op jit(solution)/shard_map/ppermute | solution.py:339
  35.5 3.5 %all-to-all-done = bf16[24,2,4224]{2,1,0:T(2,128)(2,1)S(1)} async-done(((bf16[24,2,4224]{2,1,0:T(2,128)(2,1)}), bf16[24,2,4224]{2,1,0:T(2,128)(2,1)S(1)}, u32[]{:S(2)}, u32[]{:S(2)}) %all-to-all-start) | async-done | bytes 405536 | tf_op jit(solution)/shard_map/all_to_all | solution.py:318
  41.3 9.7 %all-to-all-start.1 = ((bf16[32,16,512]{2,1,0:T(8,128)(2,1)}), bf16[32,16,512]{2,1,0:T(8,128)(2,1)S(1)}, u32[]{:S(2)}, u32[]{:S(2)}) async-start(bf16[32,16,512]{2,1,0:T(8,128)(2,1)} %bitcast.5), calls=%async_computation.1 | async-start | bytes 1048576 | tf_op jit(solution)/shard_map/all_to_all | solution.py:354
  51.0 3.1 %collective-permute-start.4 = (bf16[176,512]{1,0:T(8,128)(2,1)S(1)}, bf16[176,512]{1,0:T(8,128)(2,1)S(1)}, u32[]{:S(2)}, u32[]{:S(2)}) collective-permute-start(bf16[176,512]{1,0:T(8,128)(2,1)S(1)} %get-tuple-element.45), channel_id=1, source_target_pairs={{0,1},{1,0},{2,3},{3,2},{4,5},{5,4},{6,7},{7,6},{8,9},{9,8},{10,11... | collective-permute-start | bytes 540680 | tf_op jit(solution)/shard_map/ppermute | solution.py:339
  54.1 3.7 %collective-permute-start.5 = (bf16[176,512]{1,0:T(8,128)(2,1)S(1)}, bf16[176,512]{1,0:T(8,128)(2,1)S(1)}, u32[]{:S(2)}, u32[]{:S(2)}) collective-permute-start(bf16[176,512]{1,0:T(8,128)(2,1)S(1)} %get-tuple-element.47), channel_id=1, source_target_pairs={{0,3},{1,2},{2,1},{3,0},{4,7},{5,6},{6,5},{7,4},{8,11},{9,10},{10,... | collective-permute-start | bytes 540680 | tf_op jit(solution)/shard_map/ppermute | solution.py:339
  57.9 3.7 %collective-permute-start.6 = (bf16[176,512]{1,0:T(8,128)(2,1)S(1)}, bf16[176,512]{1,0:T(8,128)(2,1)S(1)}, u32[]{:S(2)}, u32[]{:S(2)}) collective-permute-start(bf16[176,512]{1,0:T(8,128)(2,1)S(1)} %get-tuple-element.51), channel_id=1, source_target_pairs={{0,7},{1,6},{2,5},{3,4},{4,3},{5,2},{6,1},{7,0},{8,15},{9,14},{10,... | collective-permute-start | bytes 540680 | tf_op jit(solution)/shard_map/ppermute | solution.py:339
  63.5 5.9 %collective-permute-done.6.rest_7_ = bf16[176,512]{1,0:T(8,128)(2,1)S(1)} collective-permute-done((bf16[176,512]{1,0:T(8,128)(2,1)S(1)}, bf16[176,512]{1,0:T(8,128)(2,1)S(1)}, u32[]{:S(2)}, u32[]{:S(2)}) %collective-permute-start.6) | collective-permute-done | bytes 180256 | tf_op jit(solution)/shard_map/ppermute | solution.py:339
  69.4 9.3 %attend.1 = (bf16[512,512]{1,0:T(8,128)(2,1)}, bf16[160,512]{1,0:T(8,128)(2,1)S(1)}, bf16[160,512]{1,0:T(8,128)(2,1)S(1)}, bf16[160,512]{1,0:T(8,128)(2,1)S(1)},...) custom-call(s32[1]{0:T(128)} %bitcast.member_ref, ...), custom_call_target="tpu_custom_call" | custom-call | flops 2013265920 | bytes 5242880 | tf_op jit(solution)/shard_map/attend/pallas_call | solution.py:266
  79.4 7.8 %all-to-all-start.2 = ((bf16[32,16,512]{2,1,0:T(8,128)(2,1)}), bf16[32,16,512]{2,1,0:T(8,128)(2,1)S(1)}, u32[]{:S(2)}, u32[]{:S(2)}) async-start(bf16[32,16,512]{2,1,0:T(8,128)(2,1)} %bitcast.10), calls=%async_computation.2 | async-start | bytes 1048576 | tf_op jit(solution)/shard_map/all_to_all | solution.py:362
  87.2 4.6 %collective-permute-start.7 = (bf16[160,512]{1,0:T(8,128)(2,1)S(1)}, bf16[160,512]{1,0:T(8,128)(2,1)S(1)}, u32[]{:S(2)}, u32[]{:S(2)}) collective-permute-start(bf16[160,512]{1,0:T(8,128)(2,1)S(1)} %copy-done.3), channel_id=1, source_target_pairs={{0,2},{1,3},{2,0},{3,1},{4,6},{5,7},{6,4},{7,5},{8,10},{9,11},{10,... | collective-permute-start | bytes 491528 | tf_op jit(solution)/shard_map/ppermute | solution.py:360
  91.8 2.2 %collective-permute-start.8 = (bf16[160,512]{1,0:T(8,128)(2,1)S(1)}, bf16[160,512]{1,0:T(8,128)(2,1)S(1)}, u32[]{:S(2)}, u32[]{:S(2)}) collective-permute-start(bf16[160,512]{1,0:T(8,128)(2,1)S(1)} %get-tuple-element.56), channel_id=1, source_target_pairs={{0,1},{1,0},{2,3},{3,2},{4,5},{5,4},{6,7},{7,6},{8,9},{9,8},{10,11... | collective-permute-start | bytes 491528 | tf_op jit(solution)/shard_map/ppermute | solution.py:360
  94.0 2.5 %collective-permute-start.9 = (bf16[160,512]{1,0:T(8,128)(2,1)S(1)}, bf16[160,512]{1,0:T(8,128)(2,1)S(1)}, u32[]{:S(2)}, u32[]{:S(2)}) collective-permute-start(bf16[160,512]{1,0:T(8,128)(2,1)S(1)} %get-tuple-element.60), channel_id=1, source_target_pairs={{0,3},{1,2},{2,1},{3,0},{4,7},{5,6},{6,5},{7,4},{8,11},{9,10},{10,... | collective-permute-start | bytes 491528 | tf_op jit(solution)/shard_map/ppermute | solution.py:360
  96.6 1.9 %collective-permute-done.7.rest_2_ = bf16[160,512]{1,0:T(8,128)(2,1)S(1)} collective-permute-done((bf16[160,512]{1,0:T(8,128)(2,1)S(1)}, bf16[160,512]{1,0:T(8,128)(2,1)S(1)}, u32[]{:S(2)}, u32[]{:S(2)}) %collective-permute-start.7) | collective-permute-done | bytes 163872 | tf_op jit(solution)/shard_map/ppermute | solution.py:360
  98.5 3.7 %all-to-all-done.2 = bf16[32,16,512]{2,1,0:T(8,128)(2,1)S(1)} async-done(((bf16[32,16,512]{2,1,0:T(8,128)(2,1)}), bf16[32,16,512]{2,1,0:T(8,128)(2,1)S(1)}, u32[]{:S(2)}, u32[]{:S(2)}) %all-to-all-start.2) | async-done | bytes 524320 | tf_op jit(solution)/shard_map/all_to_all | solution.py:362
  102.5 2.0 %collective-permute-done.9.rest_3_ = bf16[160,512]{1,0:T(8,128)(2,1)S(1)} collective-permute-done((bf16[160,512]{1,0:T(8,128)(2,1)S(1)}, bf16[160,512]{1,0:T(8,128)(2,1)S(1)}, u32[]{:S(2)}, u32[]{:S(2)}) %collective-permute-start.9) | collective-permute-done | bytes 163872 | tf_op jit(solution)/shard_map/ppermute | solution.py:360
  106.8 11.5 %all-to-all-start.3 = ((bf16[24,2,4096]{2,1,0:T(2,128)(2,1)}), bf16[24,2,4096]{2,1,0:T(2,128)(2,1)S(1)}, u32[]{:S(2)}, u32[]{:S(2)}) async-start(bf16[24,2,4096]{2,1,0:T(2,128)(2,1)} %all_to_all.27), calls=%async_computation.3 | async-start | bytes 786432 | tf_op jit(solution)/shard_map/all_to_all | solution.py:369
  118.3 3.1 %collective-permute-start.10 = (bf16[160,512]{1,0:T(8,128)(2,1)S(1)}, bf16[160,512]{1,0:T(8,128)(2,1)S(1)}, u32[]{:S(2)}, u32[]{:S(2)}) collective-permute-start(bf16[160,512]{1,0:T(8,128)(2,1)S(1)} %get-tuple-element.62), channel_id=1, source_target_pairs={{0,4},{1,5},{2,6},{3,7},{4,0},{5,1},{6,2},{7,3},{8,12},{9,13},{10,... | collective-permute-start | bytes 491528 | tf_op jit(solution)/shard_map/ppermute | solution.py:360
  123.3 4.3 %collective-permute-start.12 = (bf16[160,512]{1,0:T(8,128)(2,1)S(1)}, bf16[160,512]{1,0:T(8,128)(2,1)S(1)}, u32[]{:S(2)}, u32[]{:S(2)}) collective-permute-start(bf16[160,512]{1,0:T(8,128)(2,1)S(1)} %get-tuple-element.64), channel_id=1, source_target_pairs={{0,6},{1,7},{2,4},{3,5},{4,2},{5,3},{6,0},{7,1},{8,14},{9,15},{10,... | collective-permute-start | bytes 491528 | tf_op jit(solution)/shard_map/ppermute | solution.py:360
  127.6 4.2 %collective-permute-start.13 = (bf16[160,512]{1,0:T(8,128)(2,1)S(1)}, bf16[160,512]{1,0:T(8,128)(2,1)S(1)}, u32[]{:S(2)}, u32[]{:S(2)}) collective-permute-start(bf16[160,512]{1,0:T(8,128)(2,1)S(1)} %get-tuple-element.65), channel_id=1, source_target_pairs={{0,7},{1,6},{2,5},{3,4},{4,3},{5,2},{6,1},{7,0},{8,15},{9,14},{10,... | collective-permute-start | bytes 491528 | tf_op jit(solution)/shard_map/ppermute | solution.py:360
  132.9 4.1 %collective-permute-done.13.rest_7_ = bf16[160,512]{1,0:T(8,128)(2,1)S(1)} collective-permute-done((bf16[160,512]{1,0:T(8,128)(2,1)S(1)}, bf16[160,512]{1,0:T(8,128)(2,1)S(1)}, u32[]{:S(2)}, u32[]{:S(2)}) %collective-permute-start.13) | collective-permute-done | bytes 163872 | tf_op jit(solution)/shard_map/ppermute | solution.py:360
  (57 shorter events, 16.6 us)
Async XLA Ops:
  2.8 18.5 %copy-start = (bf16[160,2048]{1,0:T(8,128)(2,1)S(1)}, bf16[160,2048]{1,0:T(8,128)(2,1)}, u32[]{:S(2)}) copy-start(bf16[160,2048]{1,0:T(8,128)(2,1)} %queries_ref.1) | copy-start | bytes 1966084
  2.8 18.5 %copy-start.1 = (bf16[160,2048]{1,0:T(8,128)(2,1)S(1)}, bf16[160,2048]{1,0:T(8,128)(2,1)}, u32[]{:S(2)}) copy-start(bf16[160,2048]{1,0:T(8,128)(2,1)} %grads_ref.1) | copy-start | bytes 1966084
  3.7 35.3 %all-to-all-start = ((bf16[24,2,4224]{2,1,0:T(2,128)(2,1)}), bf16[24,2,4224]{2,1,0:T(2,128)(2,1)S(1)}, u32[]{:S(2)}, u32[]{:S(2)}) async-start(bf16[24,2,4224]{2,1,0:T(2,128)(2,1)} %all_to_all.22), calls=%async_computation | async-start | bytes 811008 | tf_op jit(solution)/shard_map/all_to_all | solution.py:318
  20.4 0.7 copy-start.5
  21.4 18.4 %collective-permute-start = (bf16[176,512]{1,0:T(8,128)(2,1)S(1)}, bf16[176,512]{1,0:T(8,128)(2,1)S(1)}, u32[]{:S(2)}, u32[]{:S(2)}) collective-permute-start(bf16[176,512]{1,0:T(8,128)(2,1)S(1)} %get-tuple-element.36), channel_id=1, source_target_pairs={{0,2},{1,3},{2,0},{3,1},{4,6},{5,7},{6,4},{7,5},{8,10},{9,11},{10,... | collective-permute-start | bytes 540680 | tf_op jit(solution)/shard_map/ppermute | solution.py:339
  26.1 14.6 %collective-permute-start.1 = (bf16[176,512]{1,0:T(8,128)(2,1)S(1)}, bf16[176,512]{1,0:T(8,128)(2,1)S(1)}, u32[]{:S(2)}, u32[]{:S(2)}) collective-permute-start(bf16[176,512]{1,0:T(8,128)(2,1)S(1)} %get-tuple-element.38), channel_id=1, source_target_pairs={{0,6},{1,7},{2,4},{3,5},{4,2},{5,3},{6,0},{7,1},{8,14},{9,15},{10,... | collective-permute-start | bytes 540680 | tf_op jit(solution)/shard_map/ppermute | solution.py:339
  29.2 11.5 %collective-permute-start.2 = (bf16[176,512]{1,0:T(8,128)(2,1)S(1)}, bf16[176,512]{1,0:T(8,128)(2,1)S(1)}, u32[]{:S(2)}, u32[]{:S(2)}) collective-permute-start(bf16[176,512]{1,0:T(8,128)(2,1)S(1)} %get-tuple-element.40), channel_id=1, source_target_pairs={{0,5},{1,4},{2,7},{3,6},{4,1},{5,0},{6,3},{7,2},{8,13},{9,12},{10,... | collective-permute-start | bytes 540680 | tf_op jit(solution)/shard_map/ppermute | solution.py:339
  32.3 9.0 %collective-permute-start.3 = (bf16[176,512]{1,0:T(8,128)(2,1)S(1)}, bf16[176,512]{1,0:T(8,128)(2,1)S(1)}, u32[]{:S(2)}, u32[]{:S(2)}) collective-permute-start(bf16[176,512]{1,0:T(8,128)(2,1)S(1)} %get-tuple-element.42), channel_id=1, source_target_pairs={{0,4},{1,5},{2,6},{3,7},{4,0},{5,1},{6,2},{7,3},{8,12},{9,13},{10,... | collective-permute-start | bytes 540680 | tf_op jit(solution)/shard_map/ppermute | solution.py:339
  41.3 28.1 %all-to-all-start.1 = ((bf16[32,16,512]{2,1,0:T(8,128)(2,1)}), bf16[32,16,512]{2,1,0:T(8,128)(2,1)S(1)}, u32[]{:S(2)}, u32[]{:S(2)}) async-start(bf16[32,16,512]{2,1,0:T(8,128)(2,1)} %bitcast.5), calls=%async_computation.1 | async-start | bytes 1048576 | tf_op jit(solution)/shard_map/all_to_all | solution.py:354
  51.0 10.9 %collective-permute-start.4 = (bf16[176,512]{1,0:T(8,128)(2,1)S(1)}, bf16[176,512]{1,0:T(8,128)(2,1)S(1)}, u32[]{:S(2)}, u32[]{:S(2)}) collective-permute-start(bf16[176,512]{1,0:T(8,128)(2,1)S(1)} %get-tuple-element.45), channel_id=1, source_target_pairs={{0,1},{1,0},{2,3},{3,2},{4,5},{5,4},{6,7},{7,6},{8,9},{9,8},{10,11... | collective-permute-start | bytes 540680 | tf_op jit(solution)/shard_map/ppermute | solution.py:339
  54.1 7.4 %copy-start.4 = (s32[1,512]{1,0:T(1,128)S(1)}, s32[1,512]{1,0:T(1,128)}, u32[]{:S(2)}) copy-start(s32[1,512]{1,0:T(1,128)} %param.10) | copy-start | bytes 6148
  54.1 9.3 %collective-permute-start.5 = (bf16[176,512]{1,0:T(8,128)(2,1)S(1)}, bf16[176,512]{1,0:T(8,128)(2,1)S(1)}, u32[]{:S(2)}, u32[]{:S(2)}) collective-permute-start(bf16[176,512]{1,0:T(8,128)(2,1)S(1)} %get-tuple-element.47), channel_id=1, source_target_pairs={{0,3},{1,2},{2,1},{3,0},{4,7},{5,6},{6,5},{7,4},{8,11},{9,10},{10,... | collective-permute-start | bytes 540680 | tf_op jit(solution)/shard_map/ppermute | solution.py:339
  57.9 11.5 %collective-permute-start.6 = (bf16[176,512]{1,0:T(8,128)(2,1)S(1)}, bf16[176,512]{1,0:T(8,128)(2,1)S(1)}, u32[]{:S(2)}, u32[]{:S(2)}) collective-permute-start(bf16[176,512]{1,0:T(8,128)(2,1)S(1)} %get-tuple-element.51), channel_id=1, source_target_pairs={{0,7},{1,6},{2,5},{3,4},{4,3},{5,2},{6,1},{7,0},{8,15},{9,14},{10,... | collective-permute-start | bytes 540680 | tf_op jit(solution)/shard_map/ppermute | solution.py:339
  78.7 0.7 copy-start.2
  79.4 7.8 %copy-start.3 = (bf16[160,512]{1,0:T(8,128)(2,1)S(1)}, bf16[160,512]{1,0:T(8,128)(2,1)}, u32[]{:S(2)}) copy-start(bf16[160,512]{1,0:T(8,128)(2,1)} %copy-done.2) | copy-start | bytes 491524
  79.4 22.9 %all-to-all-start.2 = ((bf16[32,16,512]{2,1,0:T(8,128)(2,1)}), bf16[32,16,512]{2,1,0:T(8,128)(2,1)S(1)}, u32[]{:S(2)}, u32[]{:S(2)}) async-start(bf16[32,16,512]{2,1,0:T(8,128)(2,1)} %bitcast.10), calls=%async_computation.2 | async-start | bytes 1048576 | tf_op jit(solution)/shard_map/all_to_all | solution.py:362
  87.2 11.3 %collective-permute-start.7 = (bf16[160,512]{1,0:T(8,128)(2,1)S(1)}, bf16[160,512]{1,0:T(8,128)(2,1)S(1)}, u32[]{:S(2)}, u32[]{:S(2)}) collective-permute-start(bf16[160,512]{1,0:T(8,128)(2,1)S(1)} %copy-done.3), channel_id=1, source_target_pairs={{0,2},{1,3},{2,0},{3,1},{4,6},{5,7},{6,4},{7,5},{8,10},{9,11},{10,... | collective-permute-start | bytes 491528 | tf_op jit(solution)/shard_map/ppermute | solution.py:360
  91.8 10.7 %collective-permute-start.8 = (bf16[160,512]{1,0:T(8,128)(2,1)S(1)}, bf16[160,512]{1,0:T(8,128)(2,1)S(1)}, u32[]{:S(2)}, u32[]{:S(2)}) collective-permute-start(bf16[160,512]{1,0:T(8,128)(2,1)S(1)} %get-tuple-element.56), channel_id=1, source_target_pairs={{0,1},{1,0},{2,3},{3,2},{4,5},{5,4},{6,7},{7,6},{8,9},{9,8},{10,11... | collective-permute-start | bytes 491528 | tf_op jit(solution)/shard_map/ppermute | solution.py:360
  94.0 10.5 %collective-permute-start.9 = (bf16[160,512]{1,0:T(8,128)(2,1)S(1)}, bf16[160,512]{1,0:T(8,128)(2,1)S(1)}, u32[]{:S(2)}, u32[]{:S(2)}) collective-permute-start(bf16[160,512]{1,0:T(8,128)(2,1)S(1)} %get-tuple-element.60), channel_id=1, source_target_pairs={{0,3},{1,2},{2,1},{3,0},{4,7},{5,6},{6,5},{7,4},{8,11},{9,10},{10,... | collective-permute-start | bytes 491528 | tf_op jit(solution)/shard_map/ppermute | solution.py:360
  106.8 31.4 %all-to-all-start.3 = ((bf16[24,2,4096]{2,1,0:T(2,128)(2,1)}), bf16[24,2,4096]{2,1,0:T(2,128)(2,1)S(1)}, u32[]{:S(2)}, u32[]{:S(2)}) async-start(bf16[24,2,4096]{2,1,0:T(2,128)(2,1)} %all_to_all.27), calls=%async_computation.3 | async-start | bytes 786432 | tf_op jit(solution)/shard_map/all_to_all | solution.py:369
  118.3 13.6 %collective-permute-start.10 = (bf16[160,512]{1,0:T(8,128)(2,1)S(1)}, bf16[160,512]{1,0:T(8,128)(2,1)S(1)}, u32[]{:S(2)}, u32[]{:S(2)}) collective-permute-start(bf16[160,512]{1,0:T(8,128)(2,1)S(1)} %get-tuple-element.62), channel_id=1, source_target_pairs={{0,4},{1,5},{2,6},{3,7},{4,0},{5,1},{6,2},{7,3},{8,12},{9,13},{10,... | collective-permute-start | bytes 491528 | tf_op jit(solution)/shard_map/ppermute | solution.py:360
  121.3 10.5 %collective-permute-start.11 = (bf16[160,512]{1,0:T(8,128)(2,1)S(1)}, bf16[160,512]{1,0:T(8,128)(2,1)S(1)}, u32[]{:S(2)}, u32[]{:S(2)}) collective-permute-start(bf16[160,512]{1,0:T(8,128)(2,1)S(1)} %get-tuple-element.63), channel_id=1, source_target_pairs={{0,5},{1,4},{2,7},{3,6},{4,1},{5,0},{6,3},{7,2},{8,13},{9,12},{10,... | collective-permute-start | bytes 491528 | tf_op jit(solution)/shard_map/ppermute | solution.py:360
  123.3 9.7 %collective-permute-start.12 = (bf16[160,512]{1,0:T(8,128)(2,1)S(1)}, bf16[160,512]{1,0:T(8,128)(2,1)S(1)}, u32[]{:S(2)}, u32[]{:S(2)}) collective-permute-start(bf16[160,512]{1,0:T(8,128)(2,1)S(1)} %get-tuple-element.64), channel_id=1, source_target_pairs={{0,6},{1,7},{2,4},{3,5},{4,2},{5,3},{6,0},{7,1},{8,14},{9,15},{10,... | collective-permute-start | bytes 491528 | tf_op jit(solution)/shard_map/ppermute | solution.py:360
  127.6 9.4 %collective-permute-start.13 = (bf16[160,512]{1,0:T(8,128)(2,1)S(1)}, bf16[160,512]{1,0:T(8,128)(2,1)S(1)}, u32[]{:S(2)}, u32[]{:S(2)}) collective-permute-start(bf16[160,512]{1,0:T(8,128)(2,1)S(1)} %get-tuple-element.65), channel_id=1, source_target_pairs={{0,7},{1,6},{2,5},{3,4},{4,3},{5,2},{6,1},{7,0},{8,15},{9,14},{10,... | collective-permute-start | bytes 491528 | tf_op jit(solution)/shard_map/ppermute | solution.py:360

commit v5 on v4

--- a/solution.py
+++ b/solution.py
@@ -17,8 +17,8 @@
 TOGETHER = (192,)
 VMEM_BYTES = 48 * 1024 * 1024
 COPY_BYTES = 16 * 1024 * 1024
-EARLY, LATE = (2, 6, 5, 4), (7, 3, 1)
-RETURNED, LAST = (2, 1, 3), (6, 7, 5, 4)
+EARLY, LATE = (2, 6, 5, 7), (4, 3, 1)
+RETURNED, LAST = (2, 1, 3, 4), (6, 7, 5)
 VMEM = pl.BlockSpec(memory_space=pltpu.VMEM)
 ANY = pl.BlockSpec(memory_space=pl.ANY)
 SMEM = pl.BlockSpec(memory_space=pltpu.SMEM)

time: 140 us -> 140 us (level); the launches traced: 139 us -> 137 us
  waiting for transfers between devices: 24.6 us -> 21.8 us
    all_to_all x1, starting transfers between devices: 9.72 us -> 7.81 us  [shards(): lax.all_to_all(by_column, 'ctx', split_axis=0, concat_axis=0, tiled=True)]
    all_to_all x1, waiting for transfers between devices: 3.52 us -> 1.99 us  [shards(): lax.all_to_all(send_pairs, 'dp', split_axis=0, concat_axis=0, tiled=True)]
    ppermute x7, waiting for transfers between devices: 9.31 us -> 7.82 us  [shards(): results[d] = lax.ppermute(results[d], 'ctx', exchange[d])]
  transfers between devices with their start and end apart: 18 -> 18, of which waited for: 10 -> 11; matrix products, arithmetic and copies ran while one was open for 1% -> 1% of each run, Pallas kernels for 1% -> 1%
where the time goes in v5:
time: 140 us; the launch traced here: 137 us
  starting transfers between devices  93.7 us (67%)
  waiting for transfers between devices  21.8 us (16%)
  Pallas kernels  10.7 us (8%)
  local copies, waits for them, and re-layouts  6.67 us (5%)
  other arithmetic  2.07 us (1%)
    ppermute x7, starting transfers between devices, shards(): pieces[d] = lax.ppermute(pieces[d], 'ctx', exchange[d])  25.5 us
    ppermute x7, starting transfers between devices, shards(): results[d] = lax.ppermute(results[d], 'ctx', exchange[d])  23.6 us
    all_to_all x1, starting transfers between devices, shards(): lax.all_to_all(send_pairs, 'dp', split_axis=0, concat_axis=0, tiled=True)  16.7 us
    all_to_all x1, starting transfers between devices, shards(): lax.all_to_all(back_pairs, 'dp', split_axis=0, concat_axis=0, tiled=True)  11.9 us
    pallas_call x1, Pallas kernels, attend(): pl.pallas_call(attend_kernel, out_shape=[jax.ShapeDtypeStruct((mem_rows,...  9.33 us
    ppermute x7, waiting for transfers between devices, shards(): pieces[d] = lax.ppermute(pieces[d], 'ctx', exchange[d])  9.19 us
    all_to_all x1, starting transfers between devices, shards(): lax.all_to_all(part_grad, 'ctx', split_axis=0, concat_axis=0, tiled=True)  8.18 us
    ppermute x7, waiting for transfers between devices, shards(): results[d] = lax.ppermute(results[d], 'ctx', exchange[d])  7.82 us
  transfers between devices with their start and end apart: 18, of which 11 were waited for; matrix products, arithmetic and copies ran while one was open for 1% of the time, Pallas kernels for 1%

profile of v5, /device:TPU:1, one launch (start us, length us, event | category | flops | bytes accessed | tf_op | source)
XLA Modules:
  0.0 137.1 jit_solution(16892788261925179802)
XLA Ops:
  3.7 16.7 %all-to-all-start = ((bf16[24,2,4224]{2,1,0:T(2,128)(2,1)}), bf16[24,2,4224]{2,1,0:T(2,128)(2,1)S(1)}, u32[]{:S(2)}, u32[]{:S(2)}) async-start(bf16[24,2,4224]{2,1,0:T(2,128)(2,1)} %all_to_all.22), calls=%async_computation | async-start | bytes 811008 | tf_op jit(solution)/shard_map/all_to_all | solution.py:318
  21.4 4.6 %collective-permute-start = (bf16[176,512]{1,0:T(8,128)(2,1)S(1)}, bf16[176,512]{1,0:T(8,128)(2,1)S(1)}, u32[]{:S(2)}, u32[]{:S(2)}) collective-permute-start(bf16[176,512]{1,0:T(8,128)(2,1)S(1)} %get-tuple-element.38), channel_id=1, source_target_pairs={{0,2},{1,3},{2,0},{3,1},{4,6},{5,7},{6,4},{7,5},{8,10},{9,11},{10,... | collective-permute-start | bytes 540680 | tf_op jit(solution)/shard_map/ppermute | solution.py:339
  26.1 3.1 %collective-permute-start.1 = (bf16[176,512]{1,0:T(8,128)(2,1)S(1)}, bf16[176,512]{1,0:T(8,128)(2,1)S(1)}, u32[]{:S(2)}, u32[]{:S(2)}) collective-permute-start(bf16[176,512]{1,0:T(8,128)(2,1)S(1)} %get-tuple-element.40), channel_id=1, source_target_pairs={{0,6},{1,7},{2,4},{3,5},{4,2},{5,3},{6,0},{7,1},{8,14},{9,15},{10,... | collective-permute-start | bytes 540680 | tf_op jit(solution)/shard_map/ppermute | solution.py:339
  29.2 3.0 %collective-permute-start.2 = (bf16[176,512]{1,0:T(8,128)(2,1)S(1)}, bf16[176,512]{1,0:T(8,128)(2,1)S(1)}, u32[]{:S(2)}, u32[]{:S(2)}) collective-permute-start(bf16[176,512]{1,0:T(8,128)(2,1)S(1)} %get-tuple-element.42), channel_id=1, source_target_pairs={{0,5},{1,4},{2,7},{3,6},{4,1},{5,0},{6,3},{7,2},{8,13},{9,12},{10,... | collective-permute-start | bytes 540680 | tf_op jit(solution)/shard_map/ppermute | solution.py:339
  32.3 4.7 %collective-permute-start.3 = (bf16[176,512]{1,0:T(8,128)(2,1)S(1)}, bf16[176,512]{1,0:T(8,128)(2,1)S(1)}, u32[]{:S(2)}, u32[]{:S(2)}) collective-permute-start(bf16[176,512]{1,0:T(8,128)(2,1)S(1)} %get-tuple-element.44), channel_id=1, source_target_pairs={{0,7},{1,6},{2,5},{3,4},{4,3},{5,2},{6,1},{7,0},{8,15},{9,14},{10,... | collective-permute-start | bytes 540680 | tf_op jit(solution)/shard_map/ppermute | solution.py:339
  40.7 2.9 %collective-permute-done.3.rest_7_ = bf16[176,512]{1,0:T(8,128)(2,1)S(1)} collective-permute-done((bf16[176,512]{1,0:T(8,128)(2,1)S(1)}, bf16[176,512]{1,0:T(8,128)(2,1)S(1)}, u32[]{:S(2)}, u32[]{:S(2)}) %collective-permute-start.3) | collective-permute-done | bytes 180256 | tf_op jit(solution)/shard_map/ppermute | solution.py:339
  43.6 7.8 %all-to-all-start.1 = ((bf16[32,16,512]{2,1,0:T(8,128)(2,1)}), bf16[32,16,512]{2,1,0:T(8,128)(2,1)S(1)}, u32[]{:S(2)}, u32[]{:S(2)}) async-start(bf16[32,16,512]{2,1,0:T(8,128)(2,1)} %bitcast.5), calls=%async_computation.1 | async-start | bytes 1048576 | tf_op jit(solution)/shard_map/all_to_all | solution.py:354
  51.4 3.1 %collective-permute-start.4 = (bf16[176,512]{1,0:T(8,128)(2,1)S(1)}, bf16[176,512]{1,0:T(8,128)(2,1)S(1)}, u32[]{:S(2)}, u32[]{:S(2)}) collective-permute-start(bf16[176,512]{1,0:T(8,128)(2,1)S(1)} %get-tuple-element.47), channel_id=1, source_target_pairs={{0,1},{1,0},{2,3},{3,2},{4,5},{5,4},{6,7},{7,6},{8,9},{9,8},{10,11... | collective-permute-start | bytes 540680 | tf_op jit(solution)/shard_map/ppermute | solution.py:339
  54.5 3.7 %collective-permute-start.5 = (bf16[176,512]{1,0:T(8,128)(2,1)S(1)}, bf16[176,512]{1,0:T(8,128)(2,1)S(1)}, u32[]{:S(2)}, u32[]{:S(2)}) collective-permute-start(bf16[176,512]{1,0:T(8,128)(2,1)S(1)} %get-tuple-element.49), channel_id=1, source_target_pairs={{0,3},{1,2},{2,1},{3,0},{4,7},{5,6},{6,5},{7,4},{8,11},{9,10},{10,... | collective-permute-start | bytes 540680 | tf_op jit(solution)/shard_map/ppermute | solution.py:339
  58.2 3.1 %collective-permute-start.6 = (bf16[176,512]{1,0:T(8,128)(2,1)S(1)}, bf16[176,512]{1,0:T(8,128)(2,1)S(1)}, u32[]{:S(2)}, u32[]{:S(2)}) collective-permute-start(bf16[176,512]{1,0:T(8,128)(2,1)S(1)} %get-tuple-element.50), channel_id=1, source_target_pairs={{0,4},{1,5},{2,6},{3,7},{4,0},{5,1},{6,2},{7,3},{8,12},{9,13},{10,... | collective-permute-start | bytes 540680 | tf_op jit(solution)/shard_map/ppermute | solution.py:339
  61.8 2.8 %collective-permute-done.5.rest_3_ = bf16[176,512]{1,0:T(8,128)(2,1)S(1)} collective-permute-done((bf16[176,512]{1,0:T(8,128)(2,1)S(1)}, bf16[176,512]{1,0:T(8,128)(2,1)S(1)}, u32[]{:S(2)}, u32[]{:S(2)}) %collective-permute-start.5) | collective-permute-done | bytes 180256 | tf_op jit(solution)/shard_map/ppermute | solution.py:339
  64.6 3.4 %collective-permute-done.6.rest_4_ = bf16[176,512]{1,0:T(8,128)(2,1)S(1)} collective-permute-done((bf16[176,512]{1,0:T(8,128)(2,1)S(1)}, bf16[176,512]{1,0:T(8,128)(2,1)S(1)}, u32[]{:S(2)}, u32[]{:S(2)}) %collective-permute-start.6) | collective-permute-done | bytes 180256 | tf_op jit(solution)/shard_map/ppermute | solution.py:339
  68.0 9.3 %attend.1 = (bf16[512,512]{1,0:T(8,128)(2,1)}, bf16[160,512]{1,0:T(8,128)(2,1)S(1)}, bf16[160,512]{1,0:T(8,128)(2,1)S(1)}, bf16[160,512]{1,0:T(8,128)(2,1)S(1)},...) custom-call(s32[1]{0:T(128)} %bitcast.member_ref, ...), custom_call_target="tpu_custom_call" | custom-call | flops 2013265920 | bytes 5242880 | tf_op jit(solution)/shard_map/attend/pallas_call | solution.py:266
  78.0 8.2 %all-to-all-start.2 = ((bf16[32,16,512]{2,1,0:T(8,128)(2,1)}), bf16[32,16,512]{2,1,0:T(8,128)(2,1)S(1)}, u32[]{:S(2)}, u32[]{:S(2)}) async-start(bf16[32,16,512]{2,1,0:T(8,128)(2,1)} %bitcast.10), calls=%async_computation.2 | async-start | bytes 1048576 | tf_op jit(solution)/shard_map/all_to_all | solution.py:362
  86.2 4.6 %collective-permute-start.7 = (bf16[160,512]{1,0:T(8,128)(2,1)S(1)}, bf16[160,512]{1,0:T(8,128)(2,1)S(1)}, u32[]{:S(2)}, u32[]{:S(2)}) collective-permute-start(bf16[160,512]{1,0:T(8,128)(2,1)S(1)} %copy-done.3), channel_id=1, source_target_pairs={{0,2},{1,3},{2,0},{3,1},{4,6},{5,7},{6,4},{7,5},{8,10},{9,11},{10,... | collective-permute-start | bytes 491528 | tf_op jit(solution)/shard_map/ppermute | solution.py:360
  90.9 2.2 %collective-permute-start.8 = (bf16[160,512]{1,0:T(8,128)(2,1)S(1)}, bf16[160,512]{1,0:T(8,128)(2,1)S(1)}, u32[]{:S(2)}, u32[]{:S(2)}) collective-permute-start(bf16[160,512]{1,0:T(8,128)(2,1)S(1)} %get-tuple-element.58), channel_id=1, source_target_pairs={{0,1},{1,0},{2,3},{3,2},{4,5},{5,4},{6,7},{7,6},{8,9},{9,8},{10,11... | collective-permute-start | bytes 491528 | tf_op jit(solution)/shard_map/ppermute | solution.py:360
  93.1 2.5 %collective-permute-start.9 = (bf16[160,512]{1,0:T(8,128)(2,1)S(1)}, bf16[160,512]{1,0:T(8,128)(2,1)S(1)}, u32[]{:S(2)}, u32[]{:S(2)}) collective-permute-start(bf16[160,512]{1,0:T(8,128)(2,1)S(1)} %get-tuple-element.62), channel_id=1, source_target_pairs={{0,3},{1,2},{2,1},{3,0},{4,7},{5,6},{6,5},{7,4},{8,11},{9,10},{10,... | collective-permute-start | bytes 491528 | tf_op jit(solution)/shard_map/ppermute | solution.py:360
  95.6 3.1 %collective-permute-start.10 = (bf16[160,512]{1,0:T(8,128)(2,1)S(1)}, bf16[160,512]{1,0:T(8,128)(2,1)S(1)}, u32[]{:S(2)}, u32[]{:S(2)}) collective-permute-start(bf16[160,512]{1,0:T(8,128)(2,1)S(1)} %get-tuple-element.65), channel_id=1, source_target_pairs={{0,4},{1,5},{2,6},{3,7},{4,0},{5,1},{6,2},{7,3},{8,12},{9,13},{10,... | collective-permute-start | bytes 491528 | tf_op jit(solution)/shard_map/ppermute | solution.py:360
  98.7 2.5 %all-to-all-done.2 = bf16[32,16,512]{2,1,0:T(8,128)(2,1)S(1)} async-done(((bf16[32,16,512]{2,1,0:T(8,128)(2,1)}), bf16[32,16,512]{2,1,0:T(8,128)(2,1)S(1)}, u32[]{:S(2)}, u32[]{:S(2)}) %all-to-all-start.2) | async-done | bytes 524320 | tf_op jit(solution)/shard_map/all_to_all | solution.py:362
  105.8 11.9 %all-to-all-start.3 = ((bf16[24,2,4096]{2,1,0:T(2,128)(2,1)}), bf16[24,2,4096]{2,1,0:T(2,128)(2,1)S(1)}, u32[]{:S(2)}, u32[]{:S(2)}) async-start(bf16[24,2,4096]{2,1,0:T(2,128)(2,1)} %all_to_all.27), calls=%async_computation.3 | async-start | bytes 786432 | tf_op jit(solution)/shard_map/all_to_all | solution.py:369
  117.7 3.4 %collective-permute-start.11 = (bf16[160,512]{1,0:T(8,128)(2,1)S(1)}, bf16[160,512]{1,0:T(8,128)(2,1)S(1)}, u32[]{:S(2)}, u32[]{:S(2)}) collective-permute-start(bf16[160,512]{1,0:T(8,128)(2,1)S(1)} %get-tuple-element.67), channel_id=1, source_target_pairs={{0,5},{1,4},{2,7},{3,6},{4,1},{5,0},{6,3},{7,2},{8,13},{9,12},{10,... | collective-permute-start | bytes 491528 | tf_op jit(solution)/shard_map/ppermute | solution.py:360
  121.1 4.3 %collective-permute-start.12 = (bf16[160,512]{1,0:T(8,128)(2,1)S(1)}, bf16[160,512]{1,0:T(8,128)(2,1)S(1)}, u32[]{:S(2)}, u32[]{:S(2)}) collective-permute-start(bf16[160,512]{1,0:T(8,128)(2,1)S(1)} %get-tuple-element.68), channel_id=1, source_target_pairs={{0,6},{1,7},{2,4},{3,5},{4,2},{5,3},{6,0},{7,1},{8,14},{9,15},{10,... | collective-permute-start | bytes 491528 | tf_op jit(solution)/shard_map/ppermute | solution.py:360
  125.4 3.4 %collective-permute-start.13 = (bf16[160,512]{1,0:T(8,128)(2,1)S(1)}, bf16[160,512]{1,0:T(8,128)(2,1)S(1)}, u32[]{:S(2)}, u32[]{:S(2)}) collective-permute-start(bf16[160,512]{1,0:T(8,128)(2,1)S(1)} %get-tuple-element.69), channel_id=1, source_target_pairs={{0,7},{1,6},{2,5},{3,4},{4,3},{5,2},{6,1},{7,0},{8,15},{9,14},{10,... | collective-permute-start | bytes 491528 | tf_op jit(solution)/shard_map/ppermute | solution.py:360
  131.0 3.5 %collective-permute-done.13.rest_7_ = bf16[160,512]{1,0:T(8,128)(2,1)S(1)} collective-permute-done((bf16[160,512]{1,0:T(8,128)(2,1)S(1)}, bf16[160,512]{1,0:T(8,128)(2,1)S(1)}, u32[]{:S(2)}, u32[]{:S(2)}) %collective-permute-start.13) | collective-permute-done | bytes 163872 | tf_op jit(solution)/shard_map/ppermute | solution.py:360
  (57 shorter events, 18.1 us)
Async XLA Ops:
  2.8 18.5 %copy-start = (bf16[160,2048]{1,0:T(8,128)(2,1)S(1)}, bf16[160,2048]{1,0:T(8,128)(2,1)}, u32[]{:S(2)}) copy-start(bf16[160,2048]{1,0:T(8,128)(2,1)} %queries_ref.1) | copy-start | bytes 1966084
  2.8 18.5 %copy-start.1 = (bf16[160,2048]{1,0:T(8,128)(2,1)S(1)}, bf16[160,2048]{1,0:T(8,128)(2,1)}, u32[]{:S(2)}) copy-start(bf16[160,2048]{1,0:T(8,128)(2,1)} %grads_ref.1) | copy-start | bytes 1966084
  3.7 35.3 %all-to-all-start = ((bf16[24,2,4224]{2,1,0:T(2,128)(2,1)}), bf16[24,2,4224]{2,1,0:T(2,128)(2,1)S(1)}, u32[]{:S(2)}, u32[]{:S(2)}) async-start(bf16[24,2,4224]{2,1,0:T(2,128)(2,1)} %all_to_all.22), calls=%async_computation | async-start | bytes 811008 | tf_op jit(solution)/shard_map/all_to_all | solution.py:318
  20.4 0.7 copy-start.5
  21.4 18.4 %collective-permute-start = (bf16[176,512]{1,0:T(8,128)(2,1)S(1)}, bf16[176,512]{1,0:T(8,128)(2,1)S(1)}, u32[]{:S(2)}, u32[]{:S(2)}) collective-permute-start(bf16[176,512]{1,0:T(8,128)(2,1)S(1)} %get-tuple-element.38), channel_id=1, source_target_pairs={{0,2},{1,3},{2,0},{3,1},{4,6},{5,7},{6,4},{7,5},{8,10},{9,11},{10,... | collective-permute-start | bytes 540680 | tf_op jit(solution)/shard_map/ppermute | solution.py:339
  26.1 14.6 %collective-permute-start.1 = (bf16[176,512]{1,0:T(8,128)(2,1)S(1)}, bf16[176,512]{1,0:T(8,128)(2,1)S(1)}, u32[]{:S(2)}, u32[]{:S(2)}) collective-permute-start(bf16[176,512]{1,0:T(8,128)(2,1)S(1)} %get-tuple-element.40), channel_id=1, source_target_pairs={{0,6},{1,7},{2,4},{3,5},{4,2},{5,3},{6,0},{7,1},{8,14},{9,15},{10,... | collective-permute-start | bytes 540680 | tf_op jit(solution)/shard_map/ppermute | solution.py:339
  29.2 11.5 %collective-permute-start.2 = (bf16[176,512]{1,0:T(8,128)(2,1)S(1)}, bf16[176,512]{1,0:T(8,128)(2,1)S(1)}, u32[]{:S(2)}, u32[]{:S(2)}) collective-permute-start(bf16[176,512]{1,0:T(8,128)(2,1)S(1)} %get-tuple-element.42), channel_id=1, source_target_pairs={{0,5},{1,4},{2,7},{3,6},{4,1},{5,0},{6,3},{7,2},{8,13},{9,12},{10,... | collective-permute-start | bytes 540680 | tf_op jit(solution)/shard_map/ppermute | solution.py:339
  32.3 11.3 %collective-permute-start.3 = (bf16[176,512]{1,0:T(8,128)(2,1)S(1)}, bf16[176,512]{1,0:T(8,128)(2,1)S(1)}, u32[]{:S(2)}, u32[]{:S(2)}) collective-permute-start(bf16[176,512]{1,0:T(8,128)(2,1)S(1)} %get-tuple-element.44), channel_id=1, source_target_pairs={{0,7},{1,6},{2,5},{3,4},{4,3},{5,2},{6,1},{7,0},{8,15},{9,14},{10,... | collective-permute-start | bytes 540680 | tf_op jit(solution)/shard_map/ppermute | solution.py:339
  43.6 24.4 %all-to-all-start.1 = ((bf16[32,16,512]{2,1,0:T(8,128)(2,1)}), bf16[32,16,512]{2,1,0:T(8,128)(2,1)S(1)}, u32[]{:S(2)}, u32[]{:S(2)}) async-start(bf16[32,16,512]{2,1,0:T(8,128)(2,1)} %bitcast.5), calls=%async_computation.1 | async-start | bytes 1048576 | tf_op jit(solution)/shard_map/all_to_all | solution.py:354
  51.4 10.4 %collective-permute-start.4 = (bf16[176,512]{1,0:T(8,128)(2,1)S(1)}, bf16[176,512]{1,0:T(8,128)(2,1)S(1)}, u32[]{:S(2)}, u32[]{:S(2)}) collective-permute-start(bf16[176,512]{1,0:T(8,128)(2,1)S(1)} %get-tuple-element.47), channel_id=1, source_target_pairs={{0,1},{1,0},{2,3},{3,2},{4,5},{5,4},{6,7},{7,6},{8,9},{9,8},{10,11... | collective-permute-start | bytes 540680 | tf_op jit(solution)/shard_map/ppermute | solution.py:339
  54.5 6.8 %copy-start.4 = (s32[1,512]{1,0:T(1,128)S(1)}, s32[1,512]{1,0:T(1,128)}, u32[]{:S(2)}) copy-start(s32[1,512]{1,0:T(1,128)} %param.10) | copy-start | bytes 6148
  54.5 10.1 %collective-permute-start.5 = (bf16[176,512]{1,0:T(8,128)(2,1)S(1)}, bf16[176,512]{1,0:T(8,128)(2,1)S(1)}, u32[]{:S(2)}, u32[]{:S(2)}) collective-permute-start(bf16[176,512]{1,0:T(8,128)(2,1)S(1)} %get-tuple-element.49), channel_id=1, source_target_pairs={{0,3},{1,2},{2,1},{3,0},{4,7},{5,6},{6,5},{7,4},{8,11},{9,10},{10,... | collective-permute-start | bytes 540680 | tf_op jit(solution)/shard_map/ppermute | solution.py:339
  58.2 9.8 %collective-permute-start.6 = (bf16[176,512]{1,0:T(8,128)(2,1)S(1)}, bf16[176,512]{1,0:T(8,128)(2,1)S(1)}, u32[]{:S(2)}, u32[]{:S(2)}) collective-permute-start(bf16[176,512]{1,0:T(8,128)(2,1)S(1)} %get-tuple-element.50), channel_id=1, source_target_pairs={{0,4},{1,5},{2,6},{3,7},{4,0},{5,1},{6,2},{7,3},{8,12},{9,13},{10,... | collective-permute-start | bytes 540680 | tf_op jit(solution)/shard_map/ppermute | solution.py:339
  77.3 0.7 copy-start.2
  78.0 8.2 %copy-start.3 = (bf16[160,512]{1,0:T(8,128)(2,1)S(1)}, bf16[160,512]{1,0:T(8,128)(2,1)}, u32[]{:S(2)}) copy-start(bf16[160,512]{1,0:T(8,128)(2,1)} %copy-done.2) | copy-start | bytes 491524
  78.0 23.2 %all-to-all-start.2 = ((bf16[32,16,512]{2,1,0:T(8,128)(2,1)}), bf16[32,16,512]{2,1,0:T(8,128)(2,1)S(1)}, u32[]{:S(2)}, u32[]{:S(2)}) async-start(bf16[32,16,512]{2,1,0:T(8,128)(2,1)} %bitcast.10), calls=%async_computation.2 | async-start | bytes 1048576 | tf_op jit(solution)/shard_map/all_to_all | solution.py:362
  86.2 12.5 %collective-permute-start.7 = (bf16[160,512]{1,0:T(8,128)(2,1)S(1)}, bf16[160,512]{1,0:T(8,128)(2,1)S(1)}, u32[]{:S(2)}, u32[]{:S(2)}) collective-permute-start(bf16[160,512]{1,0:T(8,128)(2,1)S(1)} %copy-done.3), channel_id=1, source_target_pairs={{0,2},{1,3},{2,0},{3,1},{4,6},{5,7},{6,4},{7,5},{8,10},{9,11},{10,... | collective-permute-start | bytes 491528 | tf_op jit(solution)/shard_map/ppermute | solution.py:360
  90.9 10.7 %collective-permute-start.8 = (bf16[160,512]{1,0:T(8,128)(2,1)S(1)}, bf16[160,512]{1,0:T(8,128)(2,1)S(1)}, u32[]{:S(2)}, u32[]{:S(2)}) collective-permute-start(bf16[160,512]{1,0:T(8,128)(2,1)S(1)} %get-tuple-element.58), channel_id=1, source_target_pairs={{0,1},{1,0},{2,3},{3,2},{4,5},{5,4},{6,7},{7,6},{8,9},{9,8},{10,11... | collective-permute-start | bytes 491528 | tf_op jit(solution)/shard_map/ppermute | solution.py:360
  93.1 10.5 %collective-permute-start.9 = (bf16[160,512]{1,0:T(8,128)(2,1)S(1)}, bf16[160,512]{1,0:T(8,128)(2,1)S(1)}, u32[]{:S(2)}, u32[]{:S(2)}) collective-permute-start(bf16[160,512]{1,0:T(8,128)(2,1)S(1)} %get-tuple-element.62), channel_id=1, source_target_pairs={{0,3},{1,2},{2,1},{3,0},{4,7},{5,6},{6,5},{7,4},{8,11},{9,10},{10,... | collective-permute-start | bytes 491528 | tf_op jit(solution)/shard_map/ppermute | solution.py:360
  95.6 7.9 %collective-permute-start.10 = (bf16[160,512]{1,0:T(8,128)(2,1)S(1)}, bf16[160,512]{1,0:T(8,128)(2,1)S(1)}, u32[]{:S(2)}, u32[]{:S(2)}) collective-permute-start(bf16[160,512]{1,0:T(8,128)(2,1)S(1)} %get-tuple-element.65), channel_id=1, source_target_pairs={{0,4},{1,5},{2,6},{3,7},{4,0},{5,1},{6,2},{7,3},{8,12},{9,13},{10,... | collective-permute-start | bytes 491528 | tf_op jit(solution)/shard_map/ppermute | solution.py:360
  105.8 30.1 %all-to-all-start.3 = ((bf16[24,2,4096]{2,1,0:T(2,128)(2,1)}), bf16[24,2,4096]{2,1,0:T(2,128)(2,1)S(1)}, u32[]{:S(2)}, u32[]{:S(2)}) async-start(bf16[24,2,4096]{2,1,0:T(2,128)(2,1)} %all_to_all.27), calls=%async_computation.3 | async-start | bytes 786432 | tf_op jit(solution)/shard_map/all_to_all | solution.py:369
  117.7 11.2 %collective-permute-start.11 = (bf16[160,512]{1,0:T(8,128)(2,1)S(1)}, bf16[160,512]{1,0:T(8,128)(2,1)S(1)}, u32[]{:S(2)}, u32[]{:S(2)}) collective-permute-start(bf16[160,512]{1,0:T(8,128)(2,1)S(1)} %get-tuple-element.67), channel_id=1, source_target_pairs={{0,5},{1,4},{2,7},{3,6},{4,1},{5,0},{6,3},{7,2},{8,13},{9,12},{10,... | collective-permute-start | bytes 491528 | tf_op jit(solution)/shard_map/ppermute | solution.py:360
  121.1 9.8 %collective-permute-start.12 = (bf16[160,512]{1,0:T(8,128)(2,1)S(1)}, bf16[160,512]{1,0:T(8,128)(2,1)S(1)}, u32[]{:S(2)}, u32[]{:S(2)}) collective-permute-start(bf16[160,512]{1,0:T(8,128)(2,1)S(1)} %get-tuple-element.68), channel_id=1, source_target_pairs={{0,6},{1,7},{2,4},{3,5},{4,2},{5,3},{6,0},{7,1},{8,14},{9,15},{10,... | collective-permute-start | bytes 491528 | tf_op jit(solution)/shard_map/ppermute | solution.py:360
  125.4 9.0 %collective-permute-start.13 = (bf16[160,512]{1,0:T(8,128)(2,1)S(1)}, bf16[160,512]{1,0:T(8,128)(2,1)S(1)}, u32[]{:S(2)}, u32[]{:S(2)}) collective-permute-start(bf16[160,512]{1,0:T(8,128)(2,1)S(1)} %get-tuple-element.69), channel_id=1, source_target_pairs={{0,7},{1,6},{2,5},{3,4},{4,3},{5,2},{6,1},{7,0},{8,15},{9,14},{10,... | collective-permute-start | bytes 491528 | tf_op jit(solution)/shard_map/ppermute | solution.py:360
